TPU v7x, 32 devices: a whole 2x2x4 slice. The times are simulated.
32 devices in a mesh: grp: 2 (over y), view: 4 (over z), slab: 2 (over x), chan: 2 (over core).
Axes of the slice: x: 2, y: 2, z: 4, core: 2. Of those that a mesh axis runs over, the one named last changes fastest.
Arguments:
- volume: bfloat16 [32, 8, 1024], P('grp', ('view', 'slab')), parts along dimension 0, may hold values from -6 to 6
- dual_state: bfloat16 [8, 16, 512], P(('grp', 'view'), 'chan', 'slab'), parts along dimension 0, may hold values from -6 to 6
- measured: bfloat16 [8, 16, 512], P(('grp', 'view'), 'chan', 'slab'), parts along dimension 0, may hold values from -6 to 6
- cotangent: bfloat16 [32, 8, 1024], P('grp', ('view', 'slab')), parts along dimension 0, may hold values from -0.125 to 0.125
- conv_first: bfloat16 [16, 2, 3, 3, 3], P('chan'), may hold values from -0.875 to 0.875
- conv_middle: bfloat16 [16, 16, 3, 3, 3], P('chan'), may hold values from -0.3125 to 0.3125
- conv_last: bfloat16 [1, 16, 3, 3, 3], P(None, 'chan'), may hold values from -0.3125 to 0.3125
- dual_mixing: float32 [16, 3], replicated, may hold values from -3.5 to 3.5
- dual_readout: float32 [16], replicated, may hold values from -1.5 to 1.5
- footprints: bfloat16 [64, 128, 128], replicated, may hold values from -0.1875 to 0.1875
- tile_rows: int32 [4, 4, 8, 1], replicated, may hold values from 0 to 7
- tile_blocks: int32 [4, 4, 8, 1], replicated, may hold values from 0 to 63
Outputs:
- new_volume: float32 [32, 8, 1024], P('grp', ('view', 'slab')), parts along dimension 0
- new_dual: float32 [8, 16, 512], P(('grp', 'view'), 'chan', 'slab'), parts along dimension 0
- grad_first: float32 [32, 2, 3, 3, 3], P(('grp', 'chan')), parts along dimension 0
- grad_middle: float32 [32, 16, 3, 3, 3], P(('grp', 'chan')), parts along dimension 0
- grad_last: float32 [2, 16, 3, 3, 3], P('grp', 'chan'), parts along dimension 0
- grad_mixing: float32 [32, 3], P('grp'), parts along dimension 0
- grad_readout: float32 [32], P('grp'), parts along dimension 0
There are 2 independent parts, one for each index of `grp`. A program takes and returns all parts, laid end to end along the dimension named above; an argument that names none is the same for every part. Nothing has to cross between parts.
All inputs are finite; a program needn't handle non-finite values.
Results may differ from a plain program's by a relative error of at most 0.0098.
Values may be sent and summed in bfloat16 or wider, within the bound.
No kernel may reach another device: no remote copies, remote signals or barrier semaphores. Data moves between devices by JAX's collectives and lax.ppermute only.
A program may use at most 64 MiB of HBM per device.

v0:
```python
import functools

import jax
import jax.numpy as jnp
from jax import lax
from jax.experimental import pallas as pl
from jax.experimental.pallas import tpu as pltpu
from jax.sharding import PartitionSpec as P

F32 = jnp.float32
BF16 = jnp.bfloat16
ALL_AXES = ("view", "slab", "chan")
ROW_AXES = ("view", "slab")
HID = 16
TILE = 128
REACH = 4
TAPS = 9
NN = (((1,), (0,)), ((), ()))
NT = (((1,), (1,)), ((), ()))
TN = (((0,), (0,)), ((), ()))
VMEM_LIMIT = 56 * 1024 * 1024


def dot(left, right, dims=NN, precision=None):
    return lax.dot_general(left, right, dims, precision=precision, preferred_element_type=F32)


def iota(shape, dim):
    return lax.broadcasted_iota(jnp.int32, shape, dim)


def repeat(count, step, limit=16):
    if count <= limit:
        for index in range(count):
            step(index)
    else:

        @pl.loop(0, count)
        def unused(index):
            step(index)


def weights_kernel(base, middle, first, last):
    wide = HID * HID
    spread = ((iota((HID, wide), 1) & (HID - 1)) == iota((HID, wide), 0)).astype(BF16)
    values = dot(base[...], spread)
    lane_z = iota((HID, wide), 1) >> 4
    row_z = iota((HID, wide), 0)

    def part(depth, tap, start, count):
        begin = (depth * TAPS + tap) * 2 * HID + start
        return values[begin : begin + count]

    for z in range(HID):
        below, level, above = (lane_z == z + 1, lane_z == z, lane_z == z - 1)
        for tap in range(TAPS):
            block = jnp.where(
                below,
                part(0, tap, 0, HID),
                jnp.where(
                    level,
                    part(1, tap, 0, HID),
                    jnp.where(above, part(2, tap, 0, HID), 0.0),
                ),
            )
            begin = (tap % 3) * wide + z * HID
            middle[tap // 3, begin : begin + HID, :] = block.astype(BF16)

    def banded(tap, row, step):
        out = jnp.zeros((HID, wide), F32)
        for depth in range(3):
            line = jnp.broadcast_to(part(depth, tap, row, 1), (HID, wide))
            out = jnp.where(row_z - lane_z == step * (depth - 1), line, out)
        return out.astype(BF16)

    for tap in range(TAPS):
        for channel in range(2):
            begin = (channel * TAPS + tap) * HID
            first[begin : begin + HID, :] = banded(tap, HID + channel, 1)
        last[tap * HID : (tap + 1) * HID, :] = banded(tap, HID + 2, -1)


def build_weights(conv_first, conv_middle, conv_last):
    own = jnp.concatenate(
        [
            conv_middle.reshape(conv_middle.shape[0], HID, 27),
            conv_first.reshape(conv_first.shape[0], 2, 27),
            jnp.swapaxes(conv_last.reshape(1, -1, 27), 0, 1),
        ],
        axis=1,
    )
    other = lax.ppermute(own, "chan", [(0, 1), (1, 0)])
    is_low = lax.axis_index("chan") == 0
    full = jnp.concatenate([jnp.where(is_low, own, other), jnp.where(is_low, other, own)], axis=0)
    base = jnp.pad(full.transpose(2, 1, 0), ((0, 0), (0, 2 * HID - 19), (0, 0)))
    wide = HID * HID
    return pl.pallas_call(
        weights_kernel,
        out_shape=(
            jax.ShapeDtypeStruct((3, 3 * wide, wide), BF16),
            jax.ShapeDtypeStruct((2 * TAPS * HID, wide), BF16),
            jax.ShapeDtypeStruct((TAPS * HID, wide), BF16),
        ),
        cost_estimate=pl.CostEstimate(flops=10**8, bytes_accessed=2 * 10**6, transcendentals=0),
        name="band_weights",
    )(base.reshape(27 * 2 * HID, HID))


def sigmoid(value):
    return jax.nn.sigmoid(value)


def projector(sizes, table, footprints):
    rows_count, detectors = (sizes[0], sizes[2])
    entries = rows_count
    groups = rows_count // 8

    def tile_of(tile, owner):
        return table[tile * entries + owner]

    def block_of(tile, owner):
        return footprints[table[(detectors + tile) * entries + owner]]

    def project(tile, pick):
        def one(group):
            owners = [group * 8 + o for o in range(8)]
            left = jnp.concatenate([pick(tile, o) for o in owners], axis=1)
            right = jnp.concatenate([block_of(tile, o) for o in owners], axis=0)
            return dot(left, right)

        if groups == 1:
            return one(0)
        return lax.fori_loop(0, groups, lambda g, a: a + one(g), jnp.zeros((16, TILE), F32))

    return tile_of, block_of, project


def dual_reader(scalars, proj, dual, meas):
    batch = 4

    def mixed_of(m, parts):
        return scalars[3 * m] * parts[0] + scalars[3 * m + 1] * parts[1] + scalars[3 * m + 2] * parts[2]

    def stack_of(chunk):
        span = pl.ds(chunk * batch, batch)
        return span, (dual[span], proj[span], meas[span])

    return batch, mixed_of, stack_of


def dual_gradients(sizes, table, scalars, footprints, proj, dual, meas, grad_tiles, grad, sums):
    rows_count, chans, detectors, tiles, width = sizes[:5]
    low = (table[2 * detectors * rows_count] * chans + table[2 * detectors * rows_count + 1]) * width
    tile_of, _, project = projector(sizes, table, footprints)
    batch, mixed_of, stack_of = dual_reader(scalars, proj, dual, meas)

    def project_grad(tile):
        def pick(t, o):
            return grad_tiles[o, (tile_of(t, o) == lax.div(low, TILE)).astype(jnp.int32)]

        grad[tile] = project(tile, pick)

    repeat(detectors, project_grad)
    sums[...] = jnp.zeros_like(sums)

    def dual_sums(chunk):
        span, parts = stack_of(chunk)
        pulled_in = grad[span]
        for m in range(HID):
            mixed = mixed_of(m, parts)
            gate = sigmoid(mixed)
            slope = gate * (1.0 + mixed * (1.0 - gate))
            pulled = pulled_in * slope * scalars[3 * HID + m]
            terms = [pulled_in * (mixed * gate)] + [pulled * part for part in parts]
            for k, term in enumerate(terms):
                sums[k, m] += jnp.sum(term.reshape(batch * 2, 8, TILE), axis=0)

    repeat(detectors // batch, dual_sums)
    lane_out = iota((HID, TILE), 1)
    small = jnp.zeros((HID, TILE), F32)
    for k in range(4):
        column = jnp.sum(jnp.sum(sums[k], axis=1), axis=1, keepdims=True)
        small = jnp.where(lane_out == k, column, small)
    return small


def dual_gradients_kernel(sizes, table, scalars, footprints, proj, dual, meas, grad_tiles, out,
                          grad, sums):
    out[...] = dual_gradients(
        sizes, table, scalars, footprints, proj, dual, meas, grad_tiles, grad, sums
    )


def main_kernel(sizes, whole, table, scalars, payload, footprints, middle, first, last,
                keep, send, dual_out, proj, dual, meas, grad_tiles,
                vol, cot, dual_half, dual_new, back, field, col_in, col_cot,
                act_wide, grad_wide, slope_first, slope_middle, row_tiles, sums):
    rows_count, chans, detectors, tiles, width, stride, cells, piece_slot, update_row = sizes
    near = tiles // chans
    entries = rows_count
    row = table[2 * detectors * entries]
    chan = table[2 * detectors * entries + 1]
    low = (row * chans + chan) * width
    count = rows_count * stride
    lanes = count + TILE

    def place(device):
        owner, part = (device // chans, device % chans)
        slot = piece_slot(owner, part, row, chan)
        for k in range(near):
            vol[owner * tiles + part * near + k] = payload[slot, k]
            cot[owner * tiles + part * near + k] = payload[slot, near + k]
        for k, target in ((2 * near, dual), (2 * near + 1, meas)):
            piece = payload[slot, k].astype(F32)
            for t in range(2):
                target[owner * 2 + t, pl.ds(pl.multiple_of(part * 8, 8), 8), :] = piece[
                    t * 8 : (t + 1) * 8
                ]

    repeat(rows_count * chans, place)

    tile_of, block_of, project = projector(sizes, table, footprints)

    def project_volume(tile):
        proj[tile] = project(tile, lambda t, o: vol[o * tiles + tile_of(t, o)])

    repeat(detectors, project_volume)

    batch, mixed_of, stack_of = dual_reader(scalars, proj, dual, meas)

    def dual_block(chunk):
        span, parts = stack_of(chunk)
        total = parts[0]
        for m in range(HID):
            mixed = mixed_of(m, parts)
            total = total + scalars[3 * HID + m] * (mixed * sigmoid(mixed))
        dual_new[span] = total
        dual_half[span] = total.astype(BF16)

    repeat(detectors // batch, dual_block)
    for t in range(2):
        dual_out[:, t * TILE : (t + 1) * TILE] = dual_new[
            row * 2 + t, pl.ds(pl.multiple_of(chan * 8, 8), 8), :
        ]

    window = width + 2 * REACH
    tile_low = lax.div(low - REACH + TILE, TILE) - 1
    offset = low - REACH - tile_low * TILE

    def backproject(group):
        owners = [group * 8 + o for o in range(8)]

        def add(tile, totals):
            right = jnp.concatenate([block_of(tile, o) for o in owners], axis=0)
            products = dot(dual_half[tile], right, NT)
            out = []
            for o in range(8):
                place_of = tile_of(tile, owners[o]) - tile_low
                product = products[:, o * TILE : (o + 1) * TILE]
                for side in range(2):
                    out.append(totals[2 * o + side] + jnp.where(place_of == side, product, 0.0))
            return tuple(out)

        totals = tuple(jnp.zeros((16, TILE), F32) for _ in range(16))
        if detectors <= 16:
            for tile in range(detectors):
                totals = add(tile, totals)
        else:
            totals = lax.fori_loop(0, detectors, add, totals)
        for o in range(8):
            for side in range(2):
                back[owners[o], side] = totals[2 * o + side]

    repeat(rows_count // 8, backproject)

    lane = iota((3 * 16, TILE), 1)
    clip_low = jnp.clip(tile_low, 0, tiles - 1)
    clip_high = jnp.clip(tile_low + 1, 0, tiles - 1)
    pieces = [None] * (lanes // TILE)
    for y in range(rows_count):
        sides = []
        for side, clipped in ((0, clip_low), (1, clip_high)):
            sides.append(
                jnp.concatenate(
                    [
                        vol[y * tiles + clipped].astype(F32),
                        back[y, side].astype(BF16).astype(F32),
                        cot[y * tiles + clipped].astype(F32),
                    ],
                    axis=0,
                )
            )
        merged = jnp.where(lane >= offset, sides[0], sides[1])
        shift = lax.rem(y * stride - offset + TILE * (count // TILE + 1), TILE)
        merged = pltpu.roll(merged, shift, 1)
        for t in range(y * stride // TILE, (y * stride + window - 1) // TILE + 1):
            column = lane + (t * TILE - y * stride)
            cell = column + (low - REACH)
            inside = (column >= 0) & (column < window) & (cell >= 0) & (cell < cells)
            taken = jnp.where(inside, merged, 0.0)
            pieces[t] = taken if pieces[t] is None else pieces[t] + taken
    for t in range(lanes // TILE):
        field[:, t * TILE : (t + 1) * TILE] = (
            jnp.zeros((3 * 16, TILE), F32) if pieces[t] is None else pieces[t]
        )

    def shift_of(tap):
        return stride * (tap // 3 - 1) + (tap % 3 - 1)

    def rolled(value, amount):
        amount = amount % lanes
        return value if amount == 0 else pltpu.roll(value, amount, 1)

    for tap in range(TAPS):
        for channel in range(2):
            begin = (channel * TAPS + tap) * HID
            part = rolled(field[channel * 16 : (channel + 1) * 16, :], -shift_of(tap))
            col_in[begin : begin + HID, :] = part[:, :count].astype(BF16)
        part = rolled(field[32:48, :], shift_of(tap))
        col_cot[tap * HID : (tap + 1) * HID, :] = part[:, :count].astype(BF16)

    wide = HID * HID
    place_x = iota((stride, wide), 0)
    cell_x = place_x + (low - REACH)
    valid = (cell_x >= 0) & (cell_x < cells)
    own = (place_x >= REACH) & (place_x < REACH + width)

    def masked(mask, value):
        shaped = value.reshape(rows_count, stride, wide)
        return jnp.where(mask[None], shaped, 0.0).reshape(count, wide)

    def widen(target, value, step):
        zero = jnp.zeros((stride, 3 * wide), BF16)
        target[0:stride, :] = zero
        target[stride + count :, :] = zero
        for k, amount in ((0, step), (1, 0), (2, -step)):
            moved = value if amount == 0 else pltpu.roll(value, amount % count, 0)
            target[stride : stride + count, k * wide : (k + 1) * wide] = moved.astype(BF16)

    first_pre = dot(col_in[...], first[...], TN)
    gate = sigmoid(first_pre)
    slope_first[...] = gate * (1.0 + first_pre * (1.0 - gate))
    widen(act_wide, masked(valid, first_pre * gate), 1)
    middle_pre = None
    for dy in range(3):
        part = dot(act_wide[stride * dy : stride * dy + count, :], middle[dy])
        middle_pre = part if middle_pre is None else middle_pre + part
    gate = sigmoid(middle_pre)
    slope_middle[...] = gate * (1.0 + middle_pre * (1.0 - gate))
    middle_act = masked(valid, middle_pre * gate)
    middle_half = middle_act.astype(BF16)

    def gather_taps(products, sign):
        padded = jnp.concatenate([products, jnp.zeros((TAPS * HID, TILE), F32)], axis=1)
        total = None
        for tap in range(TAPS):
            part = rolled(padded[tap * HID : (tap + 1) * HID], sign * shift_of(tap))
            total = part if total is None else total + part
        return total

    def rows_to_tiles(value, target):
        lane_one = iota((16, TILE), 1)
        for y in range(rows_count):
            begin = y * stride + REACH
            merged = None
            for t in range(begin // TILE, (begin + width - 1) // TILE + 1):
                column = lane_one + t * TILE
                inside = (column >= begin) & (column < begin + width)
                part = jnp.where(inside, value[:, t * TILE : (t + 1) * TILE], 0.0)
                merged = part if merged is None else merged + part
            shift = lax.rem(low - begin + TILE * (count // TILE + 1), TILE)
            target(y, pltpu.roll(merged, shift, 1))

    update = gather_taps(dot(last[...], middle_half, NT), -1) + field[0:16, :]

    def put_row(y, tile):
        row_tiles[y] = tile

    rows_to_tiles(update, put_row)

    middle_grad = masked(valid, dot(col_cot[...], last[...], TN) * slope_middle[...])
    grad_last = dot(col_cot[...], masked(own, middle_act).astype(BF16))
    widen(grad_wide, middle_grad, -1)
    turned = jnp.transpose(masked(own, middle_grad)).astype(BF16)
    grads_middle = [
        dot(turned, act_wide[stride * dy : stride * dy + count, :]) for dy in range(3)
    ]
    first_sum = None
    for dy in range(3):
        for dx in range(3):
            part = dot(
                grad_wide[stride * (2 - dy) : stride * (2 - dy) + count, dx * wide : (dx + 1) * wide],
                middle[dy, dx * wide : (dx + 1) * wide, :],
                NT,
            )
            first_sum = part if first_sum is None else first_sum + part
    first_grad = masked(valid, first_sum * slope_first[...])
    first_half = first_grad.astype(BF16)
    turned = jnp.transpose(masked(own, first_grad)).astype(BF16)
    grad_first = dot(turned, col_in[...], NT)
    back_grad = gather_taps(dot(first[TAPS * HID :, :], first_half, NT), 1)

    def put_grad(y, tile):
        grad_tiles[y, 0] = jnp.zeros((16, TILE), BF16)
        grad_tiles[y, 1] = tile.astype(BF16)

    rows_to_tiles(back_grad, put_grad)

    lane_z = iota((HID, wide), 1) >> 4
    lane_group = iota((HID, TILE), 1) >> 4
    out_tiles = [jnp.zeros((HID, TILE), F32) for _ in range(5)]

    def fold_lanes(value):
        value = value[:, :TILE] + value[:, TILE:]
        for amount in (64, 32, 16):
            value = value + pltpu.roll(value, amount, 1)
        return value

    def put(index, value):
        group = index // 8
        out_tiles[group] = jnp.where(lane_group == index % 8, value, out_tiles[group])

    for tap in range(TAPS):
        plane = grads_middle[tap // 3][:, (tap % 3) * wide : (tap % 3 + 1) * wide]
        for depth in range(3):
            total = jnp.zeros((HID, wide), F32)
            for z in range(HID):
                total = total + jnp.where(lane_z == z + depth - 1, plane[z * HID : (z + 1) * HID], 0.0)
            put(depth * TAPS + tap, fold_lanes(total))

    lane_in = iota((HID, 2 * TAPS * HID), 1) & (HID - 1)
    folds = []
    for depth in range(3):
        total = jnp.zeros((HID, 2 * TAPS * HID), F32)
        for z in range(HID):
            total = total + jnp.where(lane_in == z + depth - 1, grad_first[z * HID : (z + 1) * HID], 0.0)
        folds.append(total)
    source = iota((2 * TAPS * HID, TILE), 0) >> 4
    target = iota((2 * TAPS * HID, TILE), 1)
    for depth in range(3):
        fold = (target == 48 + depth * 2 * TAPS + source).astype(F32)
        out_tiles[3] = out_tiles[3] + dot(folds[depth], fold, precision=lax.Precision.HIGHEST)

    row_z = iota((HID, wide), 0)
    lines = []
    for depth in range(3):
        keep_last = lane_z == row_z + depth - 1
        for tap in range(TAPS):
            part = jnp.where(keep_last, grad_last[tap * HID : (tap + 1) * HID], 0.0)
            lines.append(jnp.sum(part, axis=0, keepdims=True))
    lines.append(jnp.zeros((TILE - 27, wide), F32))
    out_tiles[4] = jnp.transpose(fold_lanes(jnp.concatenate(lines, axis=0)))[:HID]

    if whole:
        small = dual_gradients(
            sizes, table, scalars, footprints, proj, dual, meas, grad_tiles, dual_new, sums
        )
    else:
        small = jnp.zeros((HID, TILE), F32)

    for t in range(5):
        slope_first[0:HID, 0:TILE] = out_tiles[t]
        keep[t * 8 : (t + 1) * 8, :] = slope_first[pl.ds(pl.multiple_of(chan * 8, 8), 8), 0:TILE]
        send[t * 8 : (t + 1) * 8, :] = slope_first[
            pl.ds(pl.multiple_of((chans - 1 - chan) * 8, 8), 8), 0:TILE
        ]
    keep[40:56, :] = small
    send[40:56, :] = small

    def put_update(y):
        begin = pl.multiple_of(56 + y * 16, 8)
        tile = row_tiles[update_row(y, row)]
        keep[pl.ds(begin, 16), :] = tile
        send[pl.ds(begin, 16), :] = tile

    repeat(rows_count, put_update)


def finish_kernel(table, own, one, two, three, far, total, *rest):
    volume, grads, slots = rest
    row = table[0]
    grads[...] = total[...] + far[0:56, :]
    for k, (source, begin) in enumerate(
        ((own, 56), (one, 56), (two, 56), (three, 56), (far, 56), (far, 72), (far, 88), (far, 104))
    ):
        slots[k] = source[begin : begin + 16, :]
    for tile in range(8):
        volume[:, tile * TILE : (tile + 1) * TILE] = slots[tile ^ row]


def row_mask_pairs(devices, mask):
    return [(index, index ^ mask) for index in range(devices)]


def body(
    volume,
    dual_state,
    measured,
    cotangent,
    conv_first,
    conv_middle,
    conv_last,
    dual_mixing,
    dual_readout,
    footprints,
    tile_rows,
    tile_blocks,
):
    views, slabs, chans = (lax.axis_size(a) for a in ALL_AXES)
    rows_count = views * slabs
    devices = rows_count * chans
    cells = volume.shape[2]
    tiles = cells // TILE
    width = cells // devices
    stride = -(-(width + 2 * REACH) // 16) * 16
    detectors = tile_rows.shape[0] * tile_rows.shape[1]
    entries = tile_rows.shape[2]
    near = tiles // chans
    chan = lax.axis_index("chan")
    row = lax.axis_index("view") * slabs + lax.axis_index("slab")
    quick = rows_count == 8 and chans == 2

    def chan_half(value):
        shaped = jnp.swapaxes(value.reshape(16, tiles, TILE), 0, 1)
        return lax.dynamic_slice_in_dim(shaped, chan * near, near, 0)

    def dual_piece(value):
        return jnp.swapaxes(value.reshape(8, 2, TILE), 0, 1).reshape(1, 16, TILE)

    payload = jnp.concatenate(
        [chan_half(volume), chan_half(cotangent), dual_piece(dual_state), dual_piece(measured)],
        axis=0,
    )[None]

    def swap(value, mask):
        return lax.ppermute(value, ALL_AXES, row_mask_pairs(devices, mask))

    if quick:
        payload = jnp.concatenate([payload, swap(payload, 8)], axis=0)
        payload = jnp.concatenate([payload] + [swap(payload, k) for k in (2, 4, 6)], axis=0)
        payload = jnp.concatenate([payload, swap(payload, 1)], axis=0)
    else:
        payload = lax.all_gather(payload, ALL_AXES, axis=0, tiled=True)

    def piece_slot(owner, part, row, chan):
        if not quick:
            return owner * chans + part
        mask = owner ^ row
        return (mask & 3) * 2 + (mask >> 2) + rows_count * (part ^ chan)

    def update_row(owner, row):
        return owner ^ row if quick else owner

    middle, first, last = build_weights(conv_first, conv_middle, conv_last)
    table = jnp.concatenate(
        [
            tile_rows.reshape(-1),
            tile_blocks.reshape(-1),
            jnp.stack([row, chan]).astype(jnp.int32),
        ]
    )
    scalars = jnp.concatenate([dual_mixing.reshape(-1), dual_readout])
    count = rows_count * stride
    wide = HID * HID
    moved = 56 + 16 * rows_count
    vmem = pl.BlockSpec(memory_space=pltpu.VMEM)
    smem = pl.BlockSpec(memory_space=pltpu.SMEM)
    sizes = (rows_count, chans, detectors, tiles, width, stride, cells, piece_slot, update_row)
    outs = [
        ((moved, TILE), F32),
        ((moved, TILE), F32),
        ((8, 2 * TILE), F32),
    ]
    shared = [
        ((detectors, 16, TILE), F32),
        ((detectors, 16, TILE), F32),
        ((detectors, 16, TILE), F32),
        ((rows_count, 2, 16, TILE), BF16),
    ]
    scratch = [
        ((rows_count * tiles, 16, TILE), BF16),
        ((rows_count * tiles, 16, TILE), BF16),
        ((detectors, 16, TILE), BF16),
        ((detectors, 16, TILE), F32),
        ((rows_count, 2, 16, TILE), F32),
        ((48, count + TILE), F32),
        ((2 * TAPS * HID, count), BF16),
        ((TAPS * HID, count), BF16),
        ((count + 2 * stride, 3 * wide), BF16),
        ((count + 2 * stride, 3 * wide), BF16),
        ((count, wide), F32),
        ((count, wide), F32),
        ((rows_count, 16, TILE), F32),
        ((4, HID, 8, TILE), F32),
    ]
    if quick:
        scratch = shared + scratch
    else:
        outs = outs + shared
    keep, send, new_dual, *rest = pl.pallas_call(
        functools.partial(main_kernel, sizes, quick),
        out_shape=[jax.ShapeDtypeStruct(*spec) for spec in outs],
        in_specs=[smem, smem] + [vmem] * 5,
        out_specs=[vmem] * len(outs),
        scratch_shapes=[pltpu.VMEM(*spec) for spec in scratch],
        compiler_params=pltpu.CompilerParams(vmem_limit_bytes=VMEM_LIMIT),
        cost_estimate=pl.CostEstimate(
            flops=5 * 10**9, bytes_accessed=5 * 10**6, transcendentals=2 * 10**6
        ),
        name="primal_dual",
    )(table, scalars, payload, footprints, middle, first, last)

    mine = keep + swap(send, 1)
    if quick:

        def piece(value, index):
            return value[56 + 16 * index : 72 + 16 * index]

        parts = [
            swap(jnp.concatenate([mine[:56], piece(mine, k), piece(mine, k ^ 4)], axis=0), 2 * k)
            for k in (1, 2, 3)
        ]
        total = mine[:56] + parts[0][:56] + parts[1][:56] + parts[2][:56]
        far = swap(
            jnp.concatenate([total, piece(mine, 4)] + [piece(part, 1) for part in parts], axis=0), 8
        )
        new_volume, grads = pl.pallas_call(
            finish_kernel,
            out_shape=(
                jax.ShapeDtypeStruct((16, cells), F32),
                jax.ShapeDtypeStruct((56, TILE), F32),
            ),
            in_specs=[smem] + [vmem] * 6,
            out_specs=(vmem, vmem),
            scratch_shapes=[pltpu.VMEM((8, 16, TILE), F32)],
            name="finish",
        )(row.reshape(1).astype(jnp.int32), mine, *parts, far, total)
    else:
        small = pl.pallas_call(
            functools.partial(dual_gradients_kernel, sizes),
            out_shape=jax.ShapeDtypeStruct((HID, TILE), F32),
            in_specs=[smem, smem] + [vmem] * 5,
            out_specs=vmem,
            scratch_shapes=[
                pltpu.VMEM((detectors, 16, TILE), F32),
                pltpu.VMEM((4, HID, 8, TILE), F32),
            ],
            compiler_params=pltpu.CompilerParams(vmem_limit_bytes=VMEM_LIMIT),
            name="dual_gradients",
        )(table, scalars, footprints, *rest)
        grads = lax.psum(mine[:40], ROW_AXES)
        grads = jnp.concatenate([grads, lax.psum(small, ALL_AXES)], axis=0)
        pieces = lax.all_to_all(
            mine[56:].reshape(rows_count, 16, TILE), ROW_AXES, 0, 0, tiled=True
        )
        pieces = pieces.reshape(tiles, rows_count // tiles, 16, TILE).sum(axis=1)
        new_volume = jnp.swapaxes(pieces, 0, 1)

    kernels = jnp.swapaxes(grads[:40].reshape(5, 8, TILE), 0, 1).reshape(8, 5 * TILE)
    grad_middle = jnp.swapaxes(kernels[:, :432].reshape(8, 27, HID), 1, 2)
    grad_first = jnp.swapaxes(kernels[:, 432:486].reshape(8, 3, 2, TAPS), 1, 2)
    grad_last = kernels[:, 512:539]
    small = grads[40:56]
    return (
        new_volume.reshape(volume.shape),
        new_dual.reshape(dual_state.shape),
        grad_first.reshape(8, 2, 3, 3, 3),
        grad_middle.reshape(8, HID, 3, 3, 3),
        grad_last.reshape(1, 8, 3, 3, 3),
        small[:, 1:4],
        small[:, 0],
    )


def solution(mesh):
    placed = (
        P("grp", ("view", "slab"), None),
        P(("grp", "view"), "chan", "slab"),
        P(("grp", "view"), "chan", "slab"),
        P("grp", ("view", "slab"), None),
        P("chan", None, None, None, None),
        P("chan", None, None, None, None),
        P(None, "chan", None, None, None),
        P(),
        P(),
        P(),
        P(),
        P(),
    )
    return jax.shard_map(
        body,
        mesh=mesh,
        in_specs=placed,
        out_specs=(
            P("grp", ("view", "slab"), None),
            P(("grp", "view"), "chan", "slab"),
            P(("grp", "chan"), None, None, None, None),
            P(("grp", "chan"), None, None, None, None),
            P("grp", "chan", None, None, None),
            P("grp", None),
            P("grp"),
        ),
        check_vma=False,
    )
```

profile of v0, /device:TPU:0, one launch (start us, length us, event | category | flops | bytes accessed | tf_op | source)
XLA Modules:
  0.0 69.8 jit_solution(13556123113944437502)
XLA Ops:
  2.9 4.1 %collective-permute-start = (bf16[1,10,16,128]{3,2,1,0:T(8,128)(2,1)S(1)}, bf16[1,10,16,128]{3,2,1,0:T(8,128)(2,1)S(1)}, u32[]{:S(2)}, u32[]{:S(2)}) collective-permute-start(bf16[1,10,16,128]{3,2,1,0:T(8,128)(2,1)S(1)} %maximum_bitcast_fusion.1), channel_id=1, source_target_pairs={{0,8},{1,9},{2,10},{3,11},{4,12},{5,13},{6,14},{7,15},{8,0},{9,1},... | collective-permute-start | bytes 122888 | tf_op jit(solution)/shard_map/ppermute | solution.py:536
  7.0 1.0 %copy.75 = bf16[8,16,27]{2,0,1:T(8,128)(2,1)S(1)} copy(bf16[8,16,27]{1,0,2:T(8,128)(2,1)} %bitcast.66) | data formatting | bytes 13824 | tf_op jit(solution)/shard_map/reshape | solution.py:86
  10.9 1.4 %reduce.9 = s32[4,4,8]{2,1,0:T(4,128)S(1)} reduce(s32[4,4,8,1]{2,3,1,0:T(1,128)} %param.22, s32[]{:T(128)} %broadcast.9), dimensions={3}, to_apply=%param.22.reduce_sub_computation.3 | reduce | bytes 1028 | tf_op args[10]
  12.4 1.4 %reduce.8 = s32[4,4,8]{2,1,0:T(4,128)S(1)} reduce(s32[4,4,8,1]{2,3,1,0:T(1,128)} %param.23, s32[]{:T(128)} %broadcast.9), dimensions={3}, to_apply=%param.23.reduce_sub_computation.3 | reduce | bytes 1028 | tf_op args[11]
  15.4 1.2 %pad_maximum_fusion.5.scalars = f32[64]{0:T(128)} fusion(f32[16]{0:T(128)} %param.20, f32[48]{0:T(128)S(1)} %reshape.83), kind=kLoop, calls=%fused_computation.36 | loop fusion | flops 64 | bytes 512 | tf_op jit(solution)/shard_map/concatenate | solution.py:562
  16.7 1.6 %collective-permute-start.1 = (bf16[2,10,16,128]{3,2,1,0:T(8,128)(2,1)S(1)}, bf16[2,10,16,128]{3,2,1,0:T(8,128)(2,1)S(1)}, u32[]{:S(2)}, u32[]{:S(2)}) collective-permute-start(bf16[2,10,16,128]{3,2,1,0:T(8,128)(2,1)S(1)} %pad_maximum_fusion), channel_id=1, source_target_pairs={{0,2},{1,3},{2,0},{3,1},{4,6},{5,7},{6,4},{7,5},{8,10},{9,11},{10,... | collective-permute-start | bytes 245768 | tf_op jit(solution)/shard_map/ppermute | solution.py:536
  18.2 1.6 %collective-permute-start.2 = (bf16[2,10,16,128]{3,2,1,0:T(8,128)(2,1)S(1)}, bf16[2,10,16,128]{3,2,1,0:T(8,128)(2,1)S(1)}, u32[]{:S(2)}, u32[]{:S(2)}) collective-permute-start(bf16[2,10,16,128]{3,2,1,0:T(8,128)(2,1)S(1)} %pad_maximum_fusion), channel_id=1, source_target_pairs={{0,4},{1,5},{2,6},{3,7},{4,0},{5,1},{6,2},{7,3},{8,12},{9,13},{10,... | collective-permute-start | bytes 245768 | tf_op jit(solution)/shard_map/ppermute | solution.py:536
  20.2 1.3 %collective-permute-done.1 = bf16[2,10,16,128]{3,2,1,0:T(8,128)(2,1)S(1)} collective-permute-done((bf16[2,10,16,128]{3,2,1,0:T(8,128)(2,1)S(1)}, bf16[2,10,16,128]{3,2,1,0:T(8,128)(2,1)S(1)}, u32[]{:S(2)}, u32[]{:S(2)}) %collective-permute-start.1) | collective-permute-done | bytes 81952 | tf_op jit(solution)/shard_map/ppermute | solution.py:536
  21.6 1.7 %collective-permute-done.2 = bf16[2,10,16,128]{3,2,1,0:T(8,128)(2,1)S(1)} collective-permute-done((bf16[2,10,16,128]{3,2,1,0:T(8,128)(2,1)S(1)}, bf16[2,10,16,128]{3,2,1,0:T(8,128)(2,1)S(1)}, u32[]{:S(2)}, u32[]{:S(2)}) %collective-permute-start.2) | collective-permute-done | bytes 81952 | tf_op jit(solution)/shard_map/ppermute | solution.py:536
  23.4 1.8 %collective-permute-done.3 = bf16[2,10,16,128]{3,2,1,0:T(8,128)(2,1)S(1)} collective-permute-done((bf16[2,10,16,128]{3,2,1,0:T(8,128)(2,1)S(1)}, bf16[2,10,16,128]{3,2,1,0:T(8,128)(2,1)S(1)}, u32[]{:S(2)}, u32[]{:S(2)}) %collective-permute-start.3) | collective-permute-done | bytes 81952 | tf_op jit(solution)/shard_map/ppermute | solution.py:536
  26.3 2.7 %band_weights.1 = (bf16[3,768,256]{2,1,0:T(8,128)(2,1)}, bf16[288,256]{1,0:T(8,128)(2,1)}, bf16[144,256]{1,0:T(8,128)(2,1)}) custom-call(bf16[864,16]{1,0:T(8,128)(2,1)} %bitcast.56), custom_call_target="tpu_custom_call" | custom-call | flops 100000000 | bytes 2000000 | tf_op jit(solution)/shard_map/band_weights/pallas_call | solution.py:97
  29.1 0.8 %copy-done.5 = bf16[16,10,16,128]{3,2,1,0:T(8,128)(2,1)} copy-done((bf16[16,10,16,128]{3,2,1,0:T(8,128)(2,1)}, bf16[16,10,16,128]{3,2,1,0:T(8,128)(2,1)S(1)}, u32[]{:S(2)}) %copy-start.5) | copy-done | bytes 655384
  29.9 13.8 %primal_dual.1 = (f32[184,128]{1,0:T(8,128)}, f32[184,128]{1,0:T(8,128)}, f32[8,256]{1,0:T(8,128)}) custom-call(s32[258]{0:T(512)} %pad_add_fusion.table, f32[64]{0:T(128)} %pad_maximum_fusion.5.scalars, bf16[16,10,16,128]{3,2,1,0:T(8,128)(2,1)} %copy-done.5, bf16[64,128,128]{2,1,0:T(8,128)(2,1)} %footprints.1, ...), custom_call_target="tpu_custom_call" | custom-call | flops 5000000000 | bytes 5000000 | tf_op jit(solution)/shard_map/primal_dual/pallas_call | solution.py:600
  44.2 1.1 %collective-permute-done.6 = f32[184,128]{1,0:T(8,128)S(1)} collective-permute-done((f32[184,128]{1,0:T(8,128)}, f32[184,128]{1,0:T(8,128)S(1)}, u32[]{:S(2)}, u32[]{:S(2)}) %collective-permute-start.6) | collective-permute-done | bytes 94240 | tf_op jit(solution)/shard_map/ppermute | solution.py:536
  45.3 0.9 %add.23.own = f32[184,128]{1,0:T(8,128)S(1)} add(f32[184,128]{1,0:T(8,128)} %get-tuple-element.18, f32[184,128]{1,0:T(8,128)S(1)} %collective-permute-done.6) | non-fusion elementwise | flops 23552 | bytes 282624 | tf_op jit(solution)/shard_map/add | solution.py:613
  46.3 0.9 %collective-permute-start.7 = (f32[88,128]{1,0:T(8,128)S(1)}, f32[88,128]{1,0:T(8,128)S(1)}, u32[]{:S(2)}, u32[]{:S(2)}) collective-permute-start(f32[88,128]{1,0:T(8,128)S(1)} %get-tuple-element.87), channel_id=1, source_target_pairs={{0,2},{1,3},{2,0},{3,1},{4,6},{5,7},{6,4},{7,5},{8,10},{9,11},{10,... | collective-permute-start | bytes 135176 | tf_op jit(solution)/shard_map/ppermute | solution.py:536
  47.2 1.6 %collective-permute-start.8 = (f32[88,128]{1,0:T(8,128)S(1)}, f32[88,128]{1,0:T(8,128)S(1)}, u32[]{:S(2)}, u32[]{:S(2)}) collective-permute-start(f32[88,128]{1,0:T(8,128)S(1)} %get-tuple-element.86), channel_id=1, source_target_pairs={{0,4},{1,5},{2,6},{3,7},{4,0},{5,1},{6,2},{7,3},{8,12},{9,13},{10,... | collective-permute-start | bytes 135176 | tf_op jit(solution)/shard_map/ppermute | solution.py:536
  48.8 1.0 %collective-permute-start.9 = (f32[88,128]{1,0:T(8,128)S(1)}, f32[88,128]{1,0:T(8,128)S(1)}, u32[]{:S(2)}, u32[]{:S(2)}) collective-permute-start(f32[88,128]{1,0:T(8,128)S(1)} %get-tuple-element.85), channel_id=1, source_target_pairs={{0,6},{1,7},{2,4},{3,5},{4,2},{5,3},{6,0},{7,1},{8,14},{9,15},{10,... | collective-permute-start | bytes 135176 | tf_op jit(solution)/shard_map/ppermute | solution.py:536
  50.4 1.1 %collective-permute-done.8.two = f32[88,128]{1,0:T(8,128)S(1)} collective-permute-done((f32[88,128]{1,0:T(8,128)S(1)}, f32[88,128]{1,0:T(8,128)S(1)}, u32[]{:S(2)}, u32[]{:S(2)}) %collective-permute-start.8) | collective-permute-done | bytes 45088 | tf_op jit(solution)/shard_map/ppermute | solution.py:536
  51.5 2.3 %collective-permute-done.9.three = f32[88,128]{1,0:T(8,128)S(1)} collective-permute-done((f32[88,128]{1,0:T(8,128)S(1)}, f32[88,128]{1,0:T(8,128)S(1)}, u32[]{:S(2)}, u32[]{:S(2)}) %collective-permute-start.9) | collective-permute-done | bytes 45088 | tf_op jit(solution)/shard_map/ppermute | solution.py:536
  54.8 5.3 %collective-permute-done.10.far = f32[120,128]{1,0:T(8,128)S(1)} collective-permute-done((f32[120,128]{1,0:T(8,128)S(1)}, f32[120,128]{1,0:T(8,128)S(1)}, u32[]{:S(2)}, u32[]{:S(2)}) %collective-permute-start.10) | collective-permute-done | bytes 61472 | tf_op jit(solution)/shard_map/ppermute | solution.py:536
  60.8 1.6 %finish.1 = (f32[16,1024]{1,0:T(8,128)}, f32[56,128]{1,0:T(8,128)}) custom-call(s32[1]{0:T(128)} %bitcast.table, f32[184,128]{1,0:T(8,128)} %copy-done, f32[88,128]{1,0:T(8,128)} %copy-done.1, f32[88,128]{1,0:T(8,128)} %copy-done.2, f32[88,128]{1,0:T(8,128)} %copy-done.3, f32[120,128]{1,0:T(8,128)} %copy-done.4, f32[56,128]{1,0:T(8,128)} %get-tuple-element.66.total), custom_call_target="tpu_custom_call" | custom-call | tf_op jit(solution)/shard_map/finish/pallas_call | solution.py:627
  63.9 1.3 %slice_reduce_fusion = f32[16]{0:T(128)} fusion(f32[56,128]{1,0:T(8,128)} %get-tuple-element.22), kind=kLoop, calls=%fused_computation.34 | loop fusion | bytes 128 | tf_op jit(solution)/shard_map/slice | solution.py:671
  66.9 1.5 %copy.82 = f32[16,1,1024]{2,1,0:T(1,128)} copy(f32[16,1,1024]{2,0,1:T(8,128)} %bitcast.65) | data formatting | bytes 131072
  (67 shorter events, 15.9 us)
Async XLA Ops:
  2.9 13.7 %collective-permute-start = (bf16[1,10,16,128]{3,2,1,0:T(8,128)(2,1)S(1)}, bf16[1,10,16,128]{3,2,1,0:T(8,128)(2,1)S(1)}, u32[]{:S(2)}, u32[]{:S(2)}) collective-permute-start(bf16[1,10,16,128]{3,2,1,0:T(8,128)(2,1)S(1)} %maximum_bitcast_fusion.1), channel_id=1, source_target_pairs={{0,8},{1,9},{2,10},{3,11},{4,12},{5,13},{6,14},{7,15},{8,0},{9,1},... | collective-permute-start | bytes 122888 | tf_op jit(solution)/shard_map/ppermute | solution.py:536
  9.6 15.6 %collective-permute-start.5 = (bf16[8,19,27]{2,0,1:T(8,128)(2,1)S(1)}, bf16[8,19,27]{2,0,1:T(8,128)(2,1)S(1)}, u32[]{:S(2)}, u32[]{:S(2)}) collective-permute-start(bf16[8,19,27]{2,0,1:T(8,128)(2,1)S(1)} %pad_maximum_fusion.4), channel_id=1, source_target_pairs={{0,1},{1,0},{2,3},{3,2},{4,5},{5,4},{6,7},{7,6},{8,9},{9,8},{10,11... | collective-permute-start | bytes 24632 | tf_op jit(solution)/shard_map/ppermute | solution.py:92
  16.7 4.9 %collective-permute-start.1 = (bf16[2,10,16,128]{3,2,1,0:T(8,128)(2,1)S(1)}, bf16[2,10,16,128]{3,2,1,0:T(8,128)(2,1)S(1)}, u32[]{:S(2)}, u32[]{:S(2)}) collective-permute-start(bf16[2,10,16,128]{3,2,1,0:T(8,128)(2,1)S(1)} %pad_maximum_fusion), channel_id=1, source_target_pairs={{0,2},{1,3},{2,0},{3,1},{4,6},{5,7},{6,4},{7,5},{8,10},{9,11},{10,... | collective-permute-start | bytes 245768 | tf_op jit(solution)/shard_map/ppermute | solution.py:536
  18.2 5.1 %collective-permute-start.2 = (bf16[2,10,16,128]{3,2,1,0:T(8,128)(2,1)S(1)}, bf16[2,10,16,128]{3,2,1,0:T(8,128)(2,1)S(1)}, u32[]{:S(2)}, u32[]{:S(2)}) collective-permute-start(bf16[2,10,16,128]{3,2,1,0:T(8,128)(2,1)S(1)} %pad_maximum_fusion), channel_id=1, source_target_pairs={{0,4},{1,5},{2,6},{3,7},{4,0},{5,1},{6,2},{7,3},{8,12},{9,13},{10,... | collective-permute-start | bytes 245768 | tf_op jit(solution)/shard_map/ppermute | solution.py:536
  19.8 5.3 %collective-permute-start.3 = (bf16[2,10,16,128]{3,2,1,0:T(8,128)(2,1)S(1)}, bf16[2,10,16,128]{3,2,1,0:T(8,128)(2,1)S(1)}, u32[]{:S(2)}, u32[]{:S(2)}) collective-permute-start(bf16[2,10,16,128]{3,2,1,0:T(8,128)(2,1)S(1)} %pad_maximum_fusion), channel_id=1, source_target_pairs={{0,6},{1,7},{2,4},{3,5},{4,2},{5,3},{6,0},{7,1},{8,14},{9,15},{10,... | collective-permute-start | bytes 245768 | tf_op jit(solution)/shard_map/ppermute | solution.py:536
  25.2 3.8 %collective-permute-start.4 = (bf16[8,10,16,128]{3,2,1,0:T(8,128)(2,1)S(1)}, bf16[8,10,16,128]{3,2,1,0:T(8,128)(2,1)S(1)}, u32[]{:S(2)}, u32[]{:S(2)}) collective-permute-start(bf16[8,10,16,128]{3,2,1,0:T(8,128)(2,1)S(1)} %get-tuple-element.73), channel_id=1, source_target_pairs={{0,1},{1,0},{2,3},{3,2},{4,5},{5,4},{6,7},{7,6},{8,9},{9,8},{10,11... | collective-permute-start | bytes 983048 | tf_op jit(solution)/shard_map/ppermute | solution.py:536
  29.1 0.8 %copy-start.5 = (bf16[16,10,16,128]{3,2,1,0:T(8,128)(2,1)}, bf16[16,10,16,128]{3,2,1,0:T(8,128)(2,1)S(1)}, u32[]{:S(2)}) copy-start(bf16[16,10,16,128]{3,2,1,0:T(8,128)(2,1)S(1)} %constant_dynamic-update-slice_fusion.5.payload) | copy-start | bytes 1966084
  43.7 1.6 %collective-permute-start.6 = (f32[184,128]{1,0:T(8,128)}, f32[184,128]{1,0:T(8,128)S(1)}, u32[]{:S(2)}, u32[]{:S(2)}) collective-permute-start(f32[184,128]{1,0:T(8,128)} %get-tuple-element.19), channel_id=1, source_target_pairs={{0,1},{1,0},{2,3},{3,2},{4,5},{5,4},{6,7},{7,6},{8,9},{9,8},{10,11... | collective-permute-start | bytes 282632 | tf_op jit(solution)/shard_map/ppermute | solution.py:536
  46.2 13.9 %copy-start = (f32[184,128]{1,0:T(8,128)}, f32[184,128]{1,0:T(8,128)S(1)}, u32[]{:S(2)}) copy-start(f32[184,128]{1,0:T(8,128)S(1)} %add.23.own) | copy-start | bytes 282628
  46.3 4.1 %collective-permute-start.7 = (f32[88,128]{1,0:T(8,128)S(1)}, f32[88,128]{1,0:T(8,128)S(1)}, u32[]{:S(2)}, u32[]{:S(2)}) collective-permute-start(f32[88,128]{1,0:T(8,128)S(1)} %get-tuple-element.87), channel_id=1, source_target_pairs={{0,2},{1,3},{2,0},{3,1},{4,6},{5,7},{6,4},{7,5},{8,10},{9,11},{10,... | collective-permute-start | bytes 135176 | tf_op jit(solution)/shard_map/ppermute | solution.py:536
  47.2 4.3 %collective-permute-start.8 = (f32[88,128]{1,0:T(8,128)S(1)}, f32[88,128]{1,0:T(8,128)S(1)}, u32[]{:S(2)}, u32[]{:S(2)}) collective-permute-start(f32[88,128]{1,0:T(8,128)S(1)} %get-tuple-element.86), channel_id=1, source_target_pairs={{0,4},{1,5},{2,6},{3,7},{4,0},{5,1},{6,2},{7,3},{8,12},{9,13},{10,... | collective-permute-start | bytes 135176 | tf_op jit(solution)/shard_map/ppermute | solution.py:536
  48.8 4.9 %collective-permute-start.9 = (f32[88,128]{1,0:T(8,128)S(1)}, f32[88,128]{1,0:T(8,128)S(1)}, u32[]{:S(2)}, u32[]{:S(2)}) collective-permute-start(f32[88,128]{1,0:T(8,128)S(1)} %get-tuple-element.85), channel_id=1, source_target_pairs={{0,6},{1,7},{2,4},{3,5},{4,2},{5,3},{6,0},{7,1},{8,14},{9,15},{10,... | collective-permute-start | bytes 135176 | tf_op jit(solution)/shard_map/ppermute | solution.py:536
  50.4 9.7 %copy-start.1 = (f32[88,128]{1,0:T(8,128)}, f32[88,128]{1,0:T(8,128)S(1)}, u32[]{:S(2)}) copy-start(f32[88,128]{1,0:T(8,128)S(1)} %collective-permute-done.7.one) | copy-start | bytes 135172
  51.5 8.7 %copy-start.2 = (f32[88,128]{1,0:T(8,128)}, f32[88,128]{1,0:T(8,128)S(1)}, u32[]{:S(2)}) copy-start(f32[88,128]{1,0:T(8,128)S(1)} %collective-permute-done.8.two) | copy-start | bytes 135172
  53.7 6.4 %copy-start.3 = (f32[88,128]{1,0:T(8,128)}, f32[88,128]{1,0:T(8,128)S(1)}, u32[]{:S(2)}) copy-start(f32[88,128]{1,0:T(8,128)S(1)} %collective-permute-done.9.three) | copy-start | bytes 135172
  54.4 5.7 %collective-permute-start.10 = (f32[120,128]{1,0:T(8,128)S(1)}, f32[120,128]{1,0:T(8,128)S(1)}, u32[]{:S(2)}, u32[]{:S(2)}) collective-permute-start(f32[120,128]{1,0:T(8,128)S(1)} %constant_dynamic-update-slice_fusion.11), channel_id=1, source_target_pairs={{0,8},{1,9},{2,10},{3,11},{4,12},{5,13},{6,14},{7,15},{8,0},{9,1},... | collective-permute-start | bytes 184328 | tf_op jit(solution)/shard_map/ppermute | solution.py:536
  60.1 0.6 copy-start.4
where the time goes:
time: 70.7 us; the launch traced here: 69.8 us
  Pallas kernels  18.1 us (26%)
  local copies, waits for them, and re-layouts  15.7 us (22%)
  waiting for transfers between devices  15.2 us (21%)
  starting transfers between devices  12.3 us (17%)
  other arithmetic  7.7 us (11%)
  between operations  0.84 us (1%)
    ppermute x10, waiting for transfers between devices, swap(): return lax.ppermute(value, ALL_AXES, row_mask_pairs(devices, mask))  15.2 us
    pallas_call x1, Pallas kernels, body(): pl.pallas_call(functools.partial(main_kernel, sizes, quick), out_shape=[j...  13.8 us
    ppermute x10, starting transfers between devices, swap(): return lax.ppermute(value, ALL_AXES, row_mask_pairs(devices, mask))  12.2 us
    unnamed x27, local copies, waits for them, and re-layouts  6.81 us
    unnamed x4, other arithmetic  4.1 us
    pallas_call x1, Pallas kernels, build_weights(): pl.pallas_call(weights_kernel, out_shape=(jax.ShapeDtypeStruct((3, 3 * wi...  2.7 us
    pallas_call x1, Pallas kernels, body(): pl.pallas_call(finish_kernel, out_shape=(jax.ShapeDtypeStruct((16, cells)...  1.6 us
  transfers between devices with their start and end apart: 11, of which 8 were waited for; matrix products, arithmetic and copies ran while one was open for 15% of the time, Pallas kernels for 4%

commit v1 on v0

--- a/solution.py
+++ b/solution.py
@@ -18,7 +18,7 @@
 NN = (((1,), (0,)), ((), ()))
 NT = (((1,), (1,)), ((), ()))
 TN = (((0,), (0,)), ((), ()))
-VMEM_LIMIT = 56 * 1024 * 1024
+MIB = 1024 * 1024
 
 
 def dot(left, right, dims=NN, precision=None):
@@ -40,60 +40,74 @@
             step(index)
 
 
-def weights_kernel(base, middle, first, last):
+def weights_kernel(chan_ref, middle_own, first_own, last_own, middle_other, first_other, last_other,
+                   middle, first, last):
     wide = HID * HID
-    spread = ((iota((HID, wide), 1) & (HID - 1)) == iota((HID, wide), 0)).astype(BF16)
-    values = dot(base[...], spread)
+    chan = chan_ref[0]
     lane_z = iota((HID, wide), 1) >> 4
     row_z = iota((HID, wide), 0)
 
-    def part(depth, tap, start, count):
-        begin = (depth * TAPS + tap) * 2 * HID + start
-        return values[begin : begin + count]
-
-    for z in range(HID):
-        below, level, above = (lane_z == z + 1, lane_z == z, lane_z == z - 1)
-        for tap in range(TAPS):
+    spread = ((iota((HID, wide), 1) & (HID - 1)) == iota((HID, wide), 0)).astype(BF16)
+
+    def spread_middle(source):
+        rows = jnp.concatenate([source[k].astype(F32) for k in range(27)], axis=0)
+        return dot(rows.astype(BF16), spread)
+
+    mine, theirs = (spread_middle(middle_own), spread_middle(middle_other))
+    lower = jnp.where(chan == 0, mine, theirs)
+    upper = jnp.where(chan == 0, theirs, mine)
+    for tap in range(TAPS):
+        parts = []
+        for depth in range(3):
+            begin = (depth * TAPS + tap) * 8
+            parts.append(
+                jnp.concatenate([lower[begin : begin + 8], upper[begin : begin + 8]], axis=0)
+            )
+        for z in range(HID):
             block = jnp.where(
-                below,
-                part(0, tap, 0, HID),
-                jnp.where(
-                    level,
-                    part(1, tap, 0, HID),
-                    jnp.where(above, part(2, tap, 0, HID), 0.0),
-                ),
+                lane_z == z - 1,
+                parts[0],
+                jnp.where(lane_z == z, parts[1], jnp.where(lane_z == z + 1, parts[2], 0.0)),
             )
             begin = (tap % 3) * wide + z * HID
             middle[tap // 3, begin : begin + HID, :] = block.astype(BF16)
 
-    def banded(tap, row, step):
+    channel = iota((8, wide), 1) & (HID - 1)
+    spread_own = (channel == iota((8, wide), 0) + 8 * chan).astype(BF16)
+    spread_other = (channel == iota((8, wide), 0) + 8 * (1 - chan)).astype(BF16)
+
+    def lines(own, other):
+        return dot(own, spread_own) + dot(other, spread_other)
+
+    def banded(rows, step):
         out = jnp.zeros((HID, wide), F32)
-        for depth in range(3):
-            line = jnp.broadcast_to(part(depth, tap, row, 1), (HID, wide))
+        for depth, line in enumerate(rows):
+            line = jnp.broadcast_to(line, (HID, wide))
             out = jnp.where(row_z - lane_z == step * (depth - 1), line, out)
         return out.astype(BF16)
 
+    first_lines = [lines(first_own[k], first_other[k]) for k in range(27)]
+    last_lines = [lines(last_own[k // 3, k % 3], last_other[k // 3, k % 3]) for k in range(9)]
     for tap in range(TAPS):
-        for channel in range(2):
-            begin = (channel * TAPS + tap) * HID
-            first[begin : begin + HID, :] = banded(tap, HID + channel, 1)
-        last[tap * HID : (tap + 1) * HID, :] = banded(tap, HID + 2, -1)
-
-
-def build_weights(conv_first, conv_middle, conv_last):
-    own = jnp.concatenate(
-        [
-            conv_middle.reshape(conv_middle.shape[0], HID, 27),
-            conv_first.reshape(conv_first.shape[0], 2, 27),
-            jnp.swapaxes(conv_last.reshape(1, -1, 27), 0, 1),
-        ],
-        axis=1,
+        for c in range(2):
+            begin = (c * TAPS + tap) * HID
+            rows = [first_lines[depth * TAPS + tap][c : c + 1] for depth in range(3)]
+            first[begin : begin + HID, :] = banded(rows, 1)
+        dy, dx = (tap // 3, tap % 3)
+        rows = [last_lines[depth * 3 + dy][dx : dx + 1] for depth in range(3)]
+        last[tap * HID : (tap + 1) * HID, :] = banded(rows, -1)
+
+
+def build_weights(chan, conv_first, conv_middle, conv_last):
+    own = (
+        conv_middle.transpose(2, 3, 4, 0, 1).reshape(27, 8, HID),
+        conv_first.transpose(2, 3, 4, 1, 0).reshape(27, 2, 8),
+        conv_last.transpose(0, 2, 3, 4, 1).reshape(3, 3, 3, 8),
     )
-    other = lax.ppermute(own, "chan", [(0, 1), (1, 0)])
-    is_low = lax.axis_index("chan") == 0
-    full = jnp.concatenate([jnp.where(is_low, own, other), jnp.where(is_low, other, own)], axis=0)
-    base = jnp.pad(full.transpose(2, 1, 0), ((0, 0), (0, 2 * HID - 19), (0, 0)))
+    other = tuple(lax.ppermute(value, "chan", [(0, 1), (1, 0)]) for value in own)
     wide = HID * HID
+    smem = pl.BlockSpec(memory_space=pltpu.SMEM)
+    vmem = pl.BlockSpec(memory_space=pltpu.VMEM)
     return pl.pallas_call(
         weights_kernel,
         out_shape=(
@@ -101,9 +115,12 @@
             jax.ShapeDtypeStruct((2 * TAPS * HID, wide), BF16),
             jax.ShapeDtypeStruct((TAPS * HID, wide), BF16),
         ),
+        in_specs=[smem] + [vmem] * 6,
+        out_specs=(vmem, vmem, vmem),
+        compiler_params=pltpu.CompilerParams(vmem_limit_bytes=16 * MIB),
         cost_estimate=pl.CostEstimate(flops=10**8, bytes_accessed=2 * 10**6, transcendentals=0),
         name="band_weights",
-    )(base.reshape(27 * 2 * HID, HID))
+    )(chan, *own, *other)
 
 
 def sigmoid(value):
@@ -111,15 +128,14 @@
 
 
 def projector(sizes, table, footprints):
-    rows_count, detectors = (sizes[0], sizes[2])
-    entries = rows_count
+    rows_count, per_view = (sizes[0], sizes[9])
     groups = rows_count // 8
 
     def tile_of(tile, owner):
-        return table[tile * entries + owner]
+        return table[0][tile // per_view, tile % per_view, 0, owner]
 
     def block_of(tile, owner):
-        return footprints[table[(detectors + tile) * entries + owner]]
+        return footprints[table[1][tile // per_view, tile % per_view, 0, owner]]
 
     def project(tile, pick):
         def one(group):
@@ -139,7 +155,7 @@
     batch = 4
 
     def mixed_of(m, parts):
-        return scalars[3 * m] * parts[0] + scalars[3 * m + 1] * parts[1] + scalars[3 * m + 2] * parts[2]
+        return scalars[0][0, m] * parts[0] + scalars[0][1, m] * parts[1] + scalars[0][2, m] * parts[2]
 
     def stack_of(chunk):
         span = pl.ds(chunk * batch, batch)
@@ -150,7 +166,7 @@
 
 def dual_gradients(sizes, table, scalars, footprints, proj, dual, meas, grad_tiles, grad, sums):
     rows_count, chans, detectors, tiles, width = sizes[:5]
-    low = (table[2 * detectors * rows_count] * chans + table[2 * detectors * rows_count + 1]) * width
+    low = (table[2][0] * chans + table[3][0]) * width
     tile_of, _, project = projector(sizes, table, footprints)
     batch, mixed_of, stack_of = dual_reader(scalars, proj, dual, meas)
 
@@ -170,7 +186,7 @@
             mixed = mixed_of(m, parts)
             gate = sigmoid(mixed)
             slope = gate * (1.0 + mixed * (1.0 - gate))
-            pulled = pulled_in * slope * scalars[3 * HID + m]
+            pulled = pulled_in * slope * scalars[1][m]
             terms = [pulled_in * (mixed * gate)] + [pulled * part for part in parts]
             for k, term in enumerate(terms):
                 sums[k, m] += jnp.sum(term.reshape(batch * 2, 8, TILE), axis=0)
@@ -181,43 +197,46 @@
     for k in range(4):
         column = jnp.sum(jnp.sum(sums[k], axis=1), axis=1, keepdims=True)
         small = jnp.where(lane_out == k, column, small)
-    return small
-
-
-def dual_gradients_kernel(sizes, table, scalars, footprints, proj, dual, meas, grad_tiles, out,
-                          grad, sums):
+    filled = jnp.concatenate([small, jnp.zeros((TILE - HID, TILE), F32)], axis=0)
+    return jnp.transpose(filled)[0:8]
+
+
+def dual_gradients_kernel(sizes, rows_ref, blocks_ref, row_ref, chan_ref, mixing, readout,
+                          footprints, proj, dual, meas, grad_tiles, out, grad, sums):
+    table = (rows_ref, blocks_ref, row_ref, chan_ref)
     out[...] = dual_gradients(
-        sizes, table, scalars, footprints, proj, dual, meas, grad_tiles, grad, sums
+        sizes, table, (mixing, readout), footprints, proj, dual, meas, grad_tiles, grad, sums
     )
 
 
-def main_kernel(sizes, whole, table, scalars, payload, footprints, middle, first, last,
+def main_kernel(sizes, whole, rows_ref, blocks_ref, row_ref, chan_ref, mixing, readout, payload, footprints, middle, first, last,
                 keep, send, dual_out, proj, dual, meas, grad_tiles,
                 vol, cot, dual_half, dual_new, back, field, col_in, col_cot,
                 act_wide, grad_wide, slope_first, slope_middle, row_tiles, sums):
-    rows_count, chans, detectors, tiles, width, stride, cells, piece_slot, update_row = sizes
-    near = tiles // chans
-    entries = rows_count
-    row = table[2 * detectors * entries]
-    chan = table[2 * detectors * entries + 1]
+    rows_count, chans, detectors, tiles, width, stride, cells, piece_slot, update_row, _ = sizes
+    table = (rows_ref, blocks_ref, row_ref, chan_ref)
+    scalars = (mixing, readout)
+    row = row_ref[0]
+    chan = chan_ref[0]
     low = (row * chans + chan) * width
     count = rows_count * stride
     lanes = count + TILE
 
-    def place(device):
-        owner, part = (device // chans, device % chans)
-        slot = piece_slot(owner, part, row, chan)
-        for k in range(near):
-            vol[owner * tiles + part * near + k] = payload[slot, k]
-            cot[owner * tiles + part * near + k] = payload[slot, near + k]
-        for k, target in ((2 * near, dual), (2 * near + 1, meas)):
-            piece = payload[slot, k].astype(F32)
-            for t in range(2):
-                target[owner * 2 + t, pl.ds(pl.multiple_of(part * 8, 8), 8), :] = piece[
-                    t * 8 : (t + 1) * 8
-                ]
-
-    repeat(rows_count * chans, place)
+    def place(owner):
+        slots = [piece_slot(owner, part, row, chan) for part in range(2)]
+        for field_index, target in ((0, vol), (1, cot)):
+            for k in range(tiles // 2):
+                halves = [payload[slot, field_index * (tiles // 2) + k].astype(F32) for slot in slots]
+                for t in range(2):
+                    whole_tile = jnp.concatenate([h[t * 8 : (t + 1) * 8] for h in halves], axis=0)
+                    target[owner * tiles + 2 * k + t] = whole_tile.astype(BF16)
+        for k, target in ((tiles, dual), (tiles + 1, meas)):
+            for part in range(2):
+                piece = payload[slots[part], k].astype(F32)
+                for t in range(2):
+                    target[owner * 2 + t, part * 8 : (part + 1) * 8, :] = piece[t * 8 : (t + 1) * 8]
+
+    repeat(rows_count, place)
 
     tile_of, block_of, project = projector(sizes, table, footprints)
 
@@ -233,7 +252,7 @@
         total = parts[0]
         for m in range(HID):
             mixed = mixed_of(m, parts)
-            total = total + scalars[3 * HID + m] * (mixed * sigmoid(mixed))
+            total = total + scalars[1][m] * (mixed * sigmoid(mixed))
         dual_new[span] = total
         dual_half[span] = total.astype(BF16)
 
@@ -343,8 +362,13 @@
     widen(act_wide, masked(valid, first_pre * gate), 1)
     middle_pre = None
     for dy in range(3):
-        part = dot(act_wide[stride * dy : stride * dy + count, :], middle[dy])
-        middle_pre = part if middle_pre is None else middle_pre + part
+        for dx in range(3):
+            part = dot(
+                act_wide[stride * dy : stride * dy + count, dx * wide : (dx + 1) * wide],
+                middle[dy, dx * wide : (dx + 1) * wide, :],
+                NT,
+            )
+            middle_pre = part if middle_pre is None else middle_pre + part
     gate = sigmoid(middle_pre)
     slope_middle[...] = gate * (1.0 + middle_pre * (1.0 - gate))
     middle_act = masked(valid, middle_pre * gate)
@@ -387,13 +411,8 @@
     ]
     first_sum = None
     for dy in range(3):
-        for dx in range(3):
-            part = dot(
-                grad_wide[stride * (2 - dy) : stride * (2 - dy) + count, dx * wide : (dx + 1) * wide],
-                middle[dy, dx * wide : (dx + 1) * wide, :],
-                NT,
-            )
-            first_sum = part if first_sum is None else first_sum + part
+        part = dot(grad_wide[stride * (2 - dy) : stride * (2 - dy) + count, :], middle[dy])
+        first_sum = part if first_sum is None else first_sum + part
     first_grad = masked(valid, first_sum * slope_first[...])
     first_half = first_grad.astype(BF16)
     turned = jnp.transpose(masked(own, first_grad)).astype(BF16)
@@ -408,7 +427,7 @@
 
     lane_z = iota((HID, wide), 1) >> 4
     lane_group = iota((HID, TILE), 1) >> 4
-    out_tiles = [jnp.zeros((HID, TILE), F32) for _ in range(5)]
+    out_tiles = [jnp.zeros((HID, TILE), F32) for _ in range(4)]
 
     def fold_lanes(value):
         value = value[:, :TILE] + value[:, TILE:]
@@ -438,7 +457,8 @@
     source = iota((2 * TAPS * HID, TILE), 0) >> 4
     target = iota((2 * TAPS * HID, TILE), 1)
     for depth in range(3):
-        fold = (target == 48 + depth * 2 * TAPS + source).astype(F32)
+        channel = (source >= TAPS).astype(jnp.int32)
+        fold = (target == 48 + (depth * TAPS + source - TAPS * channel) * 2 + channel).astype(F32)
         out_tiles[3] = out_tiles[3] + dot(folds[depth], fold, precision=lax.Precision.HIGHEST)
 
     row_z = iota((HID, wide), 0)
@@ -448,27 +468,35 @@
         for tap in range(TAPS):
             part = jnp.where(keep_last, grad_last[tap * HID : (tap + 1) * HID], 0.0)
             lines.append(jnp.sum(part, axis=0, keepdims=True))
-    lines.append(jnp.zeros((TILE - 27, wide), F32))
-    out_tiles[4] = jnp.transpose(fold_lanes(jnp.concatenate(lines, axis=0)))[:HID]
+    lines.append(jnp.zeros((32 - 27, wide), F32))
+    lines = fold_lanes(jnp.concatenate(lines, axis=0))
+    row_eight = iota((8, TILE), 0)
+    packed_last = jnp.zeros((8, TILE), F32)
+    for r in range(4):
+        picked = jnp.where(row_eight == iota((8, TILE), 1) >> 4, lines[r * 8 : (r + 1) * 8], 0.0)
+        packed_last = jnp.where(
+            row_eight == r, jnp.sum(picked, axis=0, keepdims=True), packed_last
+        )
 
     if whole:
         small = dual_gradients(
             sizes, table, scalars, footprints, proj, dual, meas, grad_tiles, dual_new, sums
         )
     else:
-        small = jnp.zeros((HID, TILE), F32)
-
-    for t in range(5):
+        small = jnp.zeros((8, TILE), F32)
+
+    for t in range(4):
         slope_first[0:HID, 0:TILE] = out_tiles[t]
         keep[t * 8 : (t + 1) * 8, :] = slope_first[pl.ds(pl.multiple_of(chan * 8, 8), 8), 0:TILE]
         send[t * 8 : (t + 1) * 8, :] = slope_first[
             pl.ds(pl.multiple_of((chans - 1 - chan) * 8, 8), 8), 0:TILE
         ]
-    keep[40:56, :] = small
-    send[40:56, :] = small
+    for target in (keep, send):
+        target[32:40, :] = packed_last
+        target[40:48, :] = small
 
     def put_update(y):
-        begin = pl.multiple_of(56 + y * 16, 8)
+        begin = pl.multiple_of(48 + y * 16, 8)
         tile = row_tiles[update_row(y, row)]
         keep[pl.ds(begin, 16), :] = tile
         send[pl.ds(begin, 16), :] = tile
@@ -476,16 +504,39 @@
     repeat(rows_count, put_update)
 
 
-def finish_kernel(table, own, one, two, three, far, total, *rest):
-    volume, grads, slots = rest
-    row = table[0]
-    grads[...] = total[...] + far[0:56, :]
+def write_grads(chan, grads, middle, first, last, mixing, readout):
+    for k in range(27):
+        block = grads[(k // 8) * 8 : (k // 8 + 1) * 8]
+        block = block if k % 8 == 0 else pltpu.roll(block, TILE - 16 * (k % 8), 1)
+        middle[k] = block[:, :HID]
+    filled = jnp.concatenate([grads[24:32], jnp.zeros((TILE - 8, TILE), F32)], axis=0)
+    turned = jnp.transpose(filled)
+    for k in range(27):
+        first[k] = turned[48 + 2 * k : 50 + 2 * k, :8]
+    block = pltpu.roll(grads[32:40], lax.rem(TILE - 8 * chan, TILE), 1)
+    for group in range(8):
+        moved = block if group == 0 else pltpu.roll(block, TILE - 16 * group, 1)
+        for r in range(4):
+            if r * 8 + group < 27:
+                last[r * 8 + group] = moved[r : r + 1, :8]
+    mixing[...] = grads[41:44, :HID]
+    readout[...] = grads[40:41, :HID]
+
+
+def finish_kernel(row_ref, chan_ref, own, one, two, three, far, total, volume, *rest):
+    grads, slots = (rest[:-1], rest[-1])
+    row = row_ref[0]
+    write_grads(chan_ref[0], total[...] + far[0:48, :], *grads)
     for k, (source, begin) in enumerate(
-        ((own, 56), (one, 56), (two, 56), (three, 56), (far, 56), (far, 72), (far, 88), (far, 104))
+        ((own, 48), (one, 48), (two, 48), (three, 48), (far, 48), (far, 64), (far, 80), (far, 96))
     ):
         slots[k] = source[begin : begin + 16, :]
     for tile in range(8):
-        volume[:, tile * TILE : (tile + 1) * TILE] = slots[tile ^ row]
+        volume[:, tile, :] = slots[tile ^ row]
+
+
+def finish_grads_kernel(chan_ref, total, *grads):
+    write_grads(chan_ref[0], total[...], *grads)
 
 
 def row_mask_pairs(devices, mask):
@@ -514,15 +565,14 @@
     width = cells // devices
     stride = -(-(width + 2 * REACH) // 16) * 16
     detectors = tile_rows.shape[0] * tile_rows.shape[1]
-    entries = tile_rows.shape[2]
-    near = tiles // chans
     chan = lax.axis_index("chan")
     row = lax.axis_index("view") * slabs + lax.axis_index("slab")
     quick = rows_count == 8 and chans == 2
 
     def chan_half(value):
-        shaped = jnp.swapaxes(value.reshape(16, tiles, TILE), 0, 1)
-        return lax.dynamic_slice_in_dim(shaped, chan * near, near, 0)
+        shaped = jnp.swapaxes(value.reshape(2, 8, tiles, TILE), 1, 2)
+        half = lax.dynamic_index_in_dim(shaped, chan, 0, keepdims=False)
+        return half.reshape(tiles // 2, 16, TILE)
 
     def dual_piece(value):
         return jnp.swapaxes(value.reshape(8, 2, TILE), 0, 1).reshape(1, 16, TILE)
@@ -551,21 +601,19 @@
     def update_row(owner, row):
         return owner ^ row if quick else owner
 
-    middle, first, last = build_weights(conv_first, conv_middle, conv_last)
-    table = jnp.concatenate(
-        [
-            tile_rows.reshape(-1),
-            tile_blocks.reshape(-1),
-            jnp.stack([row, chan]).astype(jnp.int32),
-        ]
-    )
-    scalars = jnp.concatenate([dual_mixing.reshape(-1), dual_readout])
+    row_one = row.reshape(1).astype(jnp.int32)
+    chan_one = chan.reshape(1).astype(jnp.int32)
+    middle, first, last = build_weights(chan_one, conv_first, conv_middle, conv_last)
+    table = (jnp.swapaxes(tile_rows, 2, 3), jnp.swapaxes(tile_blocks, 2, 3), row_one, chan_one)
+    scalars = (dual_mixing.T, dual_readout)
     count = rows_count * stride
     wide = HID * HID
-    moved = 56 + 16 * rows_count
+    moved = 48 + 16 * rows_count
+    limit = (20 if quick else 56) * MIB
     vmem = pl.BlockSpec(memory_space=pltpu.VMEM)
     smem = pl.BlockSpec(memory_space=pltpu.SMEM)
-    sizes = (rows_count, chans, detectors, tiles, width, stride, cells, piece_slot, update_row)
+    sizes = (rows_count, chans, detectors, tiles, width, stride, cells, piece_slot, update_row,
+             tile_rows.shape[1])
     outs = [
         ((moved, TILE), F32),
         ((moved, TILE), F32),
@@ -600,75 +648,81 @@
     keep, send, new_dual, *rest = pl.pallas_call(
         functools.partial(main_kernel, sizes, quick),
         out_shape=[jax.ShapeDtypeStruct(*spec) for spec in outs],
-        in_specs=[smem, smem] + [vmem] * 5,
+        in_specs=[smem] * 6 + [vmem] * 5,
         out_specs=[vmem] * len(outs),
         scratch_shapes=[pltpu.VMEM(*spec) for spec in scratch],
-        compiler_params=pltpu.CompilerParams(vmem_limit_bytes=VMEM_LIMIT),
+        compiler_params=pltpu.CompilerParams(vmem_limit_bytes=limit),
         cost_estimate=pl.CostEstimate(
             flops=5 * 10**9, bytes_accessed=5 * 10**6, transcendentals=2 * 10**6
         ),
         name="primal_dual",
-    )(table, scalars, payload, footprints, middle, first, last)
+    )(*table, *scalars, payload, footprints, middle, first, last)
 
     mine = keep + swap(send, 1)
+    grad_shapes = [
+        jax.ShapeDtypeStruct(shape, F32)
+        for shape in ((27, 8, HID), (27, 2, 8), (27, 1, 8), (3, HID), (1, HID))
+    ]
     if quick:
 
         def piece(value, index):
-            return value[56 + 16 * index : 72 + 16 * index]
+            return value[48 + 16 * index : 64 + 16 * index]
 
         parts = [
-            swap(jnp.concatenate([mine[:56], piece(mine, k), piece(mine, k ^ 4)], axis=0), 2 * k)
+            swap(jnp.concatenate([mine[:48], piece(mine, k), piece(mine, k ^ 4)], axis=0), 2 * k)
             for k in (1, 2, 3)
         ]
-        total = mine[:56] + parts[0][:56] + parts[1][:56] + parts[2][:56]
+        total = mine[:48] + parts[0][:48] + parts[1][:48] + parts[2][:48]
         far = swap(
             jnp.concatenate([total, piece(mine, 4)] + [piece(part, 1) for part in parts], axis=0), 8
         )
-        new_volume, grads = pl.pallas_call(
+        new_volume, *grads = pl.pallas_call(
             finish_kernel,
-            out_shape=(
-                jax.ShapeDtypeStruct((16, cells), F32),
-                jax.ShapeDtypeStruct((56, TILE), F32),
-            ),
-            in_specs=[smem] + [vmem] * 6,
-            out_specs=(vmem, vmem),
+            out_shape=[jax.ShapeDtypeStruct((16, 8, TILE), F32)] + grad_shapes,
+            in_specs=[smem, smem] + [vmem] * 6,
+            out_specs=[vmem] * 6,
             scratch_shapes=[pltpu.VMEM((8, 16, TILE), F32)],
+            compiler_params=pltpu.CompilerParams(vmem_limit_bytes=8 * MIB),
             name="finish",
-        )(row.reshape(1).astype(jnp.int32), mine, *parts, far, total)
+        )(row_one, chan_one, mine, *parts, far, total)
     else:
         small = pl.pallas_call(
             functools.partial(dual_gradients_kernel, sizes),
-            out_shape=jax.ShapeDtypeStruct((HID, TILE), F32),
-            in_specs=[smem, smem] + [vmem] * 5,
+            out_shape=jax.ShapeDtypeStruct((8, TILE), F32),
+            in_specs=[smem] * 6 + [vmem] * 5,
             out_specs=vmem,
             scratch_shapes=[
                 pltpu.VMEM((detectors, 16, TILE), F32),
                 pltpu.VMEM((4, HID, 8, TILE), F32),
             ],
-            compiler_params=pltpu.CompilerParams(vmem_limit_bytes=VMEM_LIMIT),
+            compiler_params=pltpu.CompilerParams(vmem_limit_bytes=limit),
             name="dual_gradients",
-        )(table, scalars, footprints, *rest)
-        grads = lax.psum(mine[:40], ROW_AXES)
-        grads = jnp.concatenate([grads, lax.psum(small, ALL_AXES)], axis=0)
+        )(*table, *scalars, footprints, *rest)
+        total = jnp.concatenate(
+            [lax.psum(mine[:40], ROW_AXES), lax.psum(small, ALL_AXES)], axis=0
+        )
+        grads = pl.pallas_call(
+            finish_grads_kernel,
+            out_shape=grad_shapes,
+            in_specs=[smem, vmem],
+            out_specs=[vmem] * 5,
+            name="finish_grads",
+        )(chan_one, total)
         pieces = lax.all_to_all(
-            mine[56:].reshape(rows_count, 16, TILE), ROW_AXES, 0, 0, tiled=True
+            mine[48:].reshape(rows_count, 16, TILE), ROW_AXES, 0, 0, tiled=True
         )
         pieces = pieces.reshape(tiles, rows_count // tiles, 16, TILE).sum(axis=1)
         new_volume = jnp.swapaxes(pieces, 0, 1)
 
-    kernels = jnp.swapaxes(grads[:40].reshape(5, 8, TILE), 0, 1).reshape(8, 5 * TILE)
-    grad_middle = jnp.swapaxes(kernels[:, :432].reshape(8, 27, HID), 1, 2)
-    grad_first = jnp.swapaxes(kernels[:, 432:486].reshape(8, 3, 2, TAPS), 1, 2)
-    grad_last = kernels[:, 512:539]
-    small = grads[40:56]
+    grad_middle, grad_first, grad_last, grad_mixing, grad_readout = grads
     return (
         new_volume.reshape(volume.shape),
         new_dual.reshape(dual_state.shape),
-        grad_first.reshape(8, 2, 3, 3, 3),
-        grad_middle.reshape(8, HID, 3, 3, 3),
-        grad_last.reshape(1, 8, 3, 3, 3),
-        small[:, 1:4],
-        small[:, 0],
+        grad_first.reshape(3, 3, 3, 2, 8).transpose(4, 3, 0, 1, 2),
+        grad_middle.reshape(3, 3, 3, 8, HID).transpose(3, 4, 0, 1, 2),
+        grad_last.reshape(3, 3, 3, 1, 8).transpose(3, 4, 0, 1, 2),
+        grad_mixing.T,
+        grad_readout.reshape(HID),
     )
 
 

time: 70.7 us -> 51.3 us (0.73)
  local copies, waits for them, and re-layouts: 15.7 us -> 6.03 us
  other arithmetic: 7.7 us -> 1.47 us
  Pallas kernels: 18.1 us -> 13.5 us
  starting transfers between devices: 12.3 us -> 15.5 us
  waiting for transfers between devices: 15.2 us -> 13.3 us
    reshape x9 -> x0, local copies, waits for them, and re-layouts: 3.55 us -> none  [the longest x1 0.96 us: build_weights(): conv_middle.reshape(conv_middle.shape[0], HID, 27)]
    unnamed x4 -> x2, other arithmetic: 4.1 us -> 0.72 us
    ppermute x10, waiting for transfers between devices: 15.2 us -> 12.3 us  [swap(): return lax.ppermute(value, ALL_AXES, row_mask_pairs(devices, mask))]
    ppermute x10, starting transfers between devices: 12.2 us -> 14.5 us  [swap(): return lax.ppermute(value, ALL_AXES, row_mask_pairs(devices, mask))]
    slice x8 -> x2, local copies, waits for them, and re-layouts: 2.27 us -> 0.01 us  [the longest x1 0.01 us: piece(): return value[48 + 16 * index:64 + 16 * index]]
    pallas_call x1, Pallas kernels: 2.7 us -> 0.72 us  [build_weights(): pl.pallas_call(weights_kernel, out_shape=(jax.ShapeDtypeStruct((3, 3 * wi...]
    concatenate x4 -> x1, other arithmetic: 1.92 us -> 0.01 us  [body(): jnp.concatenate([mine[:48], piece(mine, k), piece(mine, k ^ 4)], axis=0)]
    unnamed x27 -> x22, local copies, waits for them, and re-layouts: 6.81 us -> 5.05 us
  transfers between devices with their start and end apart: 11 -> 13, of which waited for: 8 -> 10; matrix products, arithmetic and copies ran while one was open for 15% -> 2% of each run, Pallas kernels for 4% -> 1%
where the time goes in v1:
time: 51.3 us; the launch traced here: 50.6 us
  starting transfers between devices  15.5 us (30%)
  Pallas kernels  13.5 us (26%)
  waiting for transfers between devices  13.3 us (26%)
  local copies, waits for them, and re-layouts  6.03 us (12%)
  other arithmetic  1.47 us (3%)
  between operations  0.79 us (2%)
    ppermute x10, starting transfers between devices, swap(): return lax.ppermute(value, ALL_AXES, row_mask_pairs(devices, mask))  14.5 us
    ppermute x10, waiting for transfers between devices, swap(): return lax.ppermute(value, ALL_AXES, row_mask_pairs(devices, mask))  12.3 us
    pallas_call x1, Pallas kernels, body(): pl.pallas_call(functools.partial(main_kernel, sizes, quick), out_shape=[j...  12 us
    unnamed x22, local copies, waits for them, and re-layouts  5.05 us
    ppermute x3, waiting for transfers between devices, build_weights(): lax.ppermute(value, 'chan', [(0, 1), (1, 0)])  1.05 us
  transfers between devices with their start and end apart: 13, of which 10 were waited for; matrix products, arithmetic and copies ran while one was open for 2% of the time, Pallas kernels for 1%

profile of v1, /device:TPU:0, one launch (start us, length us, event | category | flops | bytes accessed | tf_op | source)
XLA Modules:
  0.0 50.6 jit_solution(11973611985975629091)
XLA Ops:
  0.6 0.9 %constant_dynamic-slice_fusion = (bf16[1,8,8,128]{3,1,2,0:T(8,128)(2,1)S(1)}, bf16[1,8,8,128]{3,1,2,0:T(8,128)(2,1)S(1)}) fusion(bf16[2,8,8,128]{3,1,2,0:T(8,128)(2,1)} %bitcast.72, s32[]{:T(128)S(6)} %select_n.5, bf16[2,8,8,128]{3,1,2,0:T(8,128)(2,1)} %bitcast.73), kind=kLoop, calls=%fused_computation.27 | loop fusion | bytes 65540 | tf_op jit(solution)/shard_map/dynamic-slice.1
  1.5 0.7 %maximum_bitcast_fusion = bf16[1,10,16,128]{3,2,1,0:T(8,128)(2,1)S(1)} fusion(bf16[1,16,128]{2,1,0:T(8,128)(2,1)} %bitcast.68, bf16[1,16,128]{2,1,0:T(8,128)(2,1)} %bitcast.70, bf16[4,16,128]{2,1,0:T(8,128)(2,1)S(1)} %bitcast.64, bf16[4,16,128]{2,1,0:T(8,128)(2,1)S(1)} %bitcast.66), kind=kLoop, calls=%fused_computation.7 | loop fusion | flops 61440 | bytes 81920 | tf_op jit(solution)/shard_map/broadcast_in_dim | solution.py:580
  2.2 4.1 %collective-permute-start = (bf16[1,10,16,128]{3,2,1,0:T(8,128)(2,1)S(1)}, bf16[1,10,16,128]{3,2,1,0:T(8,128)(2,1)S(1)}, u32[]{:S(2)}, u32[]{:S(2)}) collective-permute-start(bf16[1,10,16,128]{3,2,1,0:T(8,128)(2,1)S(1)} %maximum_bitcast_fusion), channel_id=1, source_target_pairs={{0,8},{1,9},{2,10},{3,11},{4,12},{5,13},{6,14},{7,15},{8,0},{9,1},... | collective-permute-start | bytes 122888 | tf_op jit(solution)/shard_map/ppermute | solution.py:586
  6.4 0.7 %constant_dynamic-update-slice_fusion.4 = (bf16[8,10,16,128]{3,2,1,0:T(8,128)(2,1)S(1)}, bf16[16,10,16,128]{3,2,1,0:T(8,128)(2,1)S(1)}) fusion(bf16[1,16,128]{2,1,0:T(8,128)(2,1)} %bitcast.69, bf16[1,16,128]{2,1,0:T(8,128)(2,1)} %bitcast.71, bf16[4,16,128]{2,1,0:T(8,128)(2,1)S(1)} %bitcast.65, bf16[4,16,128]{2,1,0:T(8,128)(2,1)S(1)} %bitcast.67), kind=kLoop, calls=%fused_computation.12 | loop fusion | flops 163838 | bytes 122880
  7.1 1.7 %collective-permute-done = bf16[1,10,16,128]{3,2,1,0:T(8,128)(2,1)S(1)} collective-permute-done((bf16[1,10,16,128]{3,2,1,0:T(8,128)(2,1)S(1)}, bf16[1,10,16,128]{3,2,1,0:T(8,128)(2,1)S(1)}, u32[]{:S(2)}, u32[]{:S(2)}) %collective-permute-start) | collective-permute-done | bytes 40992 | tf_op jit(solution)/shard_map/ppermute | solution.py:586
  8.8 1.8 %collective-permute-start.1 = (bf16[2,10,16,128]{3,2,1,0:T(8,128)(2,1)S(1)}, bf16[2,10,16,128]{3,2,1,0:T(8,128)(2,1)S(1)}, u32[]{:S(2)}, u32[]{:S(2)}) collective-permute-start(bf16[2,10,16,128]{3,2,1,0:T(8,128)(2,1)S(1)} %pad_maximum_fusion), channel_id=1, source_target_pairs={{0,2},{1,3},{2,0},{3,1},{4,6},{5,7},{6,4},{7,5},{8,10},{9,11},{10,... | collective-permute-start | bytes 245768 | tf_op jit(solution)/shard_map/ppermute | solution.py:586
  10.6 1.3 %collective-permute-start.2 = (bf16[2,10,16,128]{3,2,1,0:T(8,128)(2,1)S(1)}, bf16[2,10,16,128]{3,2,1,0:T(8,128)(2,1)S(1)}, u32[]{:S(2)}, u32[]{:S(2)}) collective-permute-start(bf16[2,10,16,128]{3,2,1,0:T(8,128)(2,1)S(1)} %pad_maximum_fusion), channel_id=1, source_target_pairs={{0,4},{1,5},{2,6},{3,7},{4,0},{5,1},{6,2},{7,3},{8,12},{9,13},{10,... | collective-permute-start | bytes 245768 | tf_op jit(solution)/shard_map/ppermute | solution.py:586
  12.4 1.0 %collective-permute-done.1 = bf16[2,10,16,128]{3,2,1,0:T(8,128)(2,1)S(1)} collective-permute-done((bf16[2,10,16,128]{3,2,1,0:T(8,128)(2,1)S(1)}, bf16[2,10,16,128]{3,2,1,0:T(8,128)(2,1)S(1)}, u32[]{:S(2)}, u32[]{:S(2)}) %collective-permute-start.1) | collective-permute-done | bytes 81952 | tf_op jit(solution)/shard_map/ppermute | solution.py:586
  13.4 1.6 %collective-permute-done.2 = bf16[2,10,16,128]{3,2,1,0:T(8,128)(2,1)S(1)} collective-permute-done((bf16[2,10,16,128]{3,2,1,0:T(8,128)(2,1)S(1)}, bf16[2,10,16,128]{3,2,1,0:T(8,128)(2,1)S(1)}, u32[]{:S(2)}, u32[]{:S(2)}) %collective-permute-start.2) | collective-permute-done | bytes 81952 | tf_op jit(solution)/shard_map/ppermute | solution.py:586
  15.0 2.1 %collective-permute-done.3 = bf16[2,10,16,128]{3,2,1,0:T(8,128)(2,1)S(1)} collective-permute-done((bf16[2,10,16,128]{3,2,1,0:T(8,128)(2,1)S(1)}, bf16[2,10,16,128]{3,2,1,0:T(8,128)(2,1)S(1)}, u32[]{:S(2)}, u32[]{:S(2)}) %collective-permute-start.3) | collective-permute-done | bytes 81952 | tf_op jit(solution)/shard_map/ppermute | solution.py:586
  18.3 1.0 %collective-permute-done.7.last_other = bf16[3,3,3,8]{3,2,1,0:T(4,128)(2,1)S(1)} collective-permute-done((bf16[3,3,3,8]{3,2,1,0:T(4,128)(2,1)}, bf16[3,3,3,8]{3,2,1,0:T(4,128)(2,1)S(1)}, u32[]{:S(2)}, u32[]{:S(2)}) %collective-permute-start.7) | collective-permute-done | bytes 464 | tf_op jit(solution)/shard_map/ppermute | solution.py:107
  19.3 0.8 %copy-done.1 = bf16[8,16,3,3,3]{1,0,4,3,2:T(8,128)(2,1)S(1)} copy-done((bf16[8,16,3,3,3]{1,0,4,3,2:T(8,128)(2,1)S(1)}, bf16[8,16,3,3,3]{1,0,4,3,2:T(8,128)(2,1)}, u32[]{:S(2)}) %copy-start.1) | copy-done | bytes 6936
  20.1 0.7 %copy-done.2 = bf16[8,2,3,3,3]{0,1,4,3,2:T(2,128)(2,1)S(1)} copy-done((bf16[8,2,3,3,3]{0,1,4,3,2:T(2,128)(2,1)S(1)}, bf16[8,2,3,3,3]{0,1,4,3,2:T(2,128)(2,1)}, u32[]{:S(2)}) %copy-start.2) | copy-done | bytes 888
  21.6 0.7 %band_weights.1 = (bf16[3,768,256]{2,1,0:T(8,128)(2,1)S(1)}, bf16[288,256]{1,0:T(8,128)(2,1)S(1)}, bf16[144,256]{1,0:T(8,128)(2,1)S(1)}) custom-call(s32[1]{0:T(128)} %bitcast.1.chan_ref, bf16[27,8,16]{2,1,0:T(8,128)(2,1)S(1)} %bitcast.56, bf16[27,2,8]{2,1,0:T(2,128)(2,1)S(1)} %bitcast.58, bf16[3,3,3,8]{3,2,1,0:T(4,128)(2,1)S(1)} %bitcast.60, ...), custom_call_target="tpu_custom_call" | custom-call | flops 100000000 | bytes 2000000 | tf_op jit(solution)/shard_map/band_weights/pallas_call | solution.py:111
  25.1 12.0 %primal_dual.1 = (f32[176,128]{1,0:T(8,128)S(1)}, f32[176,128]{1,0:T(8,128)S(1)}, f32[8,256]{1,0:T(8,128)}) custom-call(s32[4,4,1,8]{3,2,1,0:T(1,128)S(1)} %bitcast.61, s32[4,4,1,8]{3,2,1,0:T(1,128)S(1)} %bitcast.62, s32[1]{0:T(128)} %bitcast.row_ref, s32[1]{0:T(128)} %bitcast.1.chan_ref, f32[3,16]{1,0:T(4,128)S(1)} %bitcast.63, f32[16]{0:T(128)S(1)} %copy-done.7, ...), custom_call_target="tpu_custom_call" | custom-call | flops 5000000000 | bytes 5000000 | tf_op jit(solution)/shard_map/primal_dual/pallas_call | solution.py:648
  37.5 0.9 %collective-permute-done.8 = f32[176,128]{1,0:T(8,128)S(1)} collective-permute-done((f32[176,128]{1,0:T(8,128)S(1)}, f32[176,128]{1,0:T(8,128)S(1)}, u32[]{:S(2)}, u32[]{:S(2)}) %collective-permute-start.8) | collective-permute-done | bytes 90144 | tf_op jit(solution)/shard_map/ppermute | solution.py:586
  38.5 0.8 %collective-permute-start.10 = (f32[80,128]{1,0:T(8,128)S(1)}, f32[80,128]{1,0:T(8,128)S(1)}, u32[]{:S(2)}, u32[]{:S(2)}) collective-permute-start(f32[80,128]{1,0:T(8,128)S(1)} %get-tuple-element.57), channel_id=1, source_target_pairs={{0,4},{1,5},{2,6},{3,7},{4,0},{5,1},{6,2},{7,3},{8,12},{9,13},{10,... | collective-permute-start | bytes 122888 | tf_op jit(solution)/shard_map/ppermute | solution.py:586
  39.3 1.2 %collective-permute-start.11 = (f32[80,128]{1,0:T(8,128)S(1)}, f32[80,128]{1,0:T(8,128)S(1)}, u32[]{:S(2)}, u32[]{:S(2)}) collective-permute-start(f32[80,128]{1,0:T(8,128)S(1)} %get-tuple-element.56), channel_id=1, source_target_pairs={{0,6},{1,7},{2,4},{3,5},{4,2},{5,3},{6,0},{7,1},{8,14},{9,15},{10,... | collective-permute-start | bytes 122888 | tf_op jit(solution)/shard_map/ppermute | solution.py:586
  40.5 1.5 %collective-permute-start.9 = (f32[80,128]{1,0:T(8,128)S(1)}, f32[80,128]{1,0:T(8,128)S(1)}, u32[]{:S(2)}, u32[]{:S(2)}) collective-permute-start(f32[80,128]{1,0:T(8,128)S(1)} %get-tuple-element.58), channel_id=1, source_target_pairs={{0,2},{1,3},{2,0},{3,1},{4,6},{5,7},{6,4},{7,5},{8,10},{9,11},{10,... | collective-permute-start | bytes 122888 | tf_op jit(solution)/shard_map/ppermute | solution.py:586
  42.0 0.9 %collective-permute-done.10.two = f32[80,128]{1,0:T(8,128)S(1)} collective-permute-done((f32[80,128]{1,0:T(8,128)S(1)}, f32[80,128]{1,0:T(8,128)S(1)}, u32[]{:S(2)}, u32[]{:S(2)}) %collective-permute-start.10) | collective-permute-done | bytes 40992 | tf_op jit(solution)/shard_map/ppermute | solution.py:586
  43.0 1.3 %collective-permute-done.11.three = f32[80,128]{1,0:T(8,128)S(1)} collective-permute-done((f32[80,128]{1,0:T(8,128)S(1)}, f32[80,128]{1,0:T(8,128)S(1)}, u32[]{:S(2)}, u32[]{:S(2)}) %collective-permute-start.11) | collective-permute-done | bytes 40992 | tf_op jit(solution)/shard_map/ppermute | solution.py:586
  44.7 2.9 %collective-permute-start.12 = (f32[112,128]{1,0:T(8,128)S(1)}, f32[112,128]{1,0:T(8,128)S(1)}, u32[]{:S(2)}, u32[]{:S(2)}) collective-permute-start(f32[112,128]{1,0:T(8,128)S(1)} %constant_dynamic-update-slice_fusion.11), channel_id=1, source_target_pairs={{0,8},{1,9},{2,10},{3,11},{4,12},{5,13},{6,14},{7,15},{8,0},{9,1},... | collective-permute-start | bytes 172040 | tf_op jit(solution)/shard_map/ppermute | solution.py:586
  47.6 2.3 %collective-permute-done.12.far = f32[112,128]{1,0:T(8,128)S(1)} collective-permute-done((f32[112,128]{1,0:T(8,128)S(1)}, f32[112,128]{1,0:T(8,128)S(1)}, u32[]{:S(2)}, u32[]{:S(2)}) %collective-permute-start.12) | collective-permute-done | bytes 57376 | tf_op jit(solution)/shard_map/ppermute | solution.py:586
  49.9 0.8 %finish.1 = (f32[16,8,128]{2,1,0:T(8,128)}, f32[27,8,16]{2,1,0:T(8,128)}, f32[27,2,8]{2,1,0:T(2,128)}, f32[27,1,8]{2,1,0:T(1,128)}, f32[3,16]{1,0:T(4,128)}, /*index=5*/f32[1,16]{1,0:T(1,128)}) custom-call(s32[1]{0:T(128)} %bitcast.row_ref, s32[1]{0:T(128)} %bitcast.1.chan_ref, f32[176,128]{1,0:T(8,128)S(1)} %add.22.own, ...), custom_call_target="tpu_custom_call" | custom-call | tf_op jit(solution)/shard_map/finish/pallas_call | solution.py:679
  (39 shorter events, 6.1 us)
Async XLA Ops:
  0.6 21.7 %copy-start = (bf16[64,128,128]{2,1,0:T(8,128)(2,1)S(1)}, bf16[64,128,128]{2,1,0:T(8,128)(2,1)}, u32[]{:S(2)}) copy-start(bf16[64,128,128]{2,1,0:T(8,128)(2,1)} %footprints.1) | copy-start | bytes 6291460
  2.2 6.5 %collective-permute-start = (bf16[1,10,16,128]{3,2,1,0:T(8,128)(2,1)S(1)}, bf16[1,10,16,128]{3,2,1,0:T(8,128)(2,1)S(1)}, u32[]{:S(2)}, u32[]{:S(2)}) collective-permute-start(bf16[1,10,16,128]{3,2,1,0:T(8,128)(2,1)S(1)} %maximum_bitcast_fusion), channel_id=1, source_target_pairs={{0,8},{1,9},{2,10},{3,11},{4,12},{5,13},{6,14},{7,15},{8,0},{9,1},... | collective-permute-start | bytes 122888 | tf_op jit(solution)/shard_map/ppermute | solution.py:586
  8.8 4.6 %collective-permute-start.1 = (bf16[2,10,16,128]{3,2,1,0:T(8,128)(2,1)S(1)}, bf16[2,10,16,128]{3,2,1,0:T(8,128)(2,1)S(1)}, u32[]{:S(2)}, u32[]{:S(2)}) collective-permute-start(bf16[2,10,16,128]{3,2,1,0:T(8,128)(2,1)S(1)} %pad_maximum_fusion), channel_id=1, source_target_pairs={{0,2},{1,3},{2,0},{3,1},{4,6},{5,7},{6,4},{7,5},{8,10},{9,11},{10,... | collective-permute-start | bytes 245768 | tf_op jit(solution)/shard_map/ppermute | solution.py:586
  10.6 4.4 %collective-permute-start.2 = (bf16[2,10,16,128]{3,2,1,0:T(8,128)(2,1)S(1)}, bf16[2,10,16,128]{3,2,1,0:T(8,128)(2,1)S(1)}, u32[]{:S(2)}, u32[]{:S(2)}) collective-permute-start(bf16[2,10,16,128]{3,2,1,0:T(8,128)(2,1)S(1)} %pad_maximum_fusion), channel_id=1, source_target_pairs={{0,4},{1,5},{2,6},{3,7},{4,0},{5,1},{6,2},{7,3},{8,12},{9,13},{10,... | collective-permute-start | bytes 245768 | tf_op jit(solution)/shard_map/ppermute | solution.py:586
  11.8 5.3 %collective-permute-start.3 = (bf16[2,10,16,128]{3,2,1,0:T(8,128)(2,1)S(1)}, bf16[2,10,16,128]{3,2,1,0:T(8,128)(2,1)S(1)}, u32[]{:S(2)}, u32[]{:S(2)}) collective-permute-start(bf16[2,10,16,128]{3,2,1,0:T(8,128)(2,1)S(1)} %pad_maximum_fusion), channel_id=1, source_target_pairs={{0,6},{1,7},{2,4},{3,5},{4,2},{5,3},{6,0},{7,1},{8,14},{9,15},{10,... | collective-permute-start | bytes 245768 | tf_op jit(solution)/shard_map/ppermute | solution.py:586
  17.2 5.1 %collective-permute-start.4 = (bf16[8,10,16,128]{3,2,1,0:T(8,128)(2,1)S(1)}, bf16[8,10,16,128]{3,2,1,0:T(8,128)(2,1)S(1)}, u32[]{:S(2)}, u32[]{:S(2)}) collective-permute-start(bf16[8,10,16,128]{3,2,1,0:T(8,128)(2,1)S(1)} %get-tuple-element.46), channel_id=1, source_target_pairs={{0,1},{1,0},{2,3},{3,2},{4,5},{5,4},{6,7},{7,6},{8,9},{9,8},{10,11... | collective-permute-start | bytes 983048 | tf_op jit(solution)/shard_map/ppermute | solution.py:586
  17.3 2.1 %collective-permute-start.5 = (bf16[27,8,16]{2,1,0:T(8,128)(2,1)}, bf16[27,8,16]{2,1,0:T(8,128)(2,1)S(1)}, u32[]{:S(2)}, u32[]{:S(2)}) collective-permute-start(bf16[27,8,16]{2,1,0:T(8,128)(2,1)} %bitcast.55), channel_id=1, source_target_pairs={{0,1},{1,0},{2,3},{3,2},{4,5},{5,4},{6,7},{7,6},{8,9},{9,8},{10,11... | collective-permute-start | bytes 20744 | tf_op jit(solution)/shard_map/ppermute | solution.py:107
  17.8 1.6 %collective-permute-start.6 = (bf16[27,2,8]{2,1,0:T(2,128)(2,1)}, bf16[27,2,8]{2,1,0:T(2,128)(2,1)S(1)}, u32[]{:S(2)}, u32[]{:S(2)}) collective-permute-start(bf16[27,2,8]{2,1,0:T(2,128)(2,1)} %bitcast.57), channel_id=1, source_target_pairs={{0,1},{1,0},{2,3},{3,2},{4,5},{5,4},{6,7},{7,6},{8,9},{9,8},{10,11... | collective-permute-start | bytes 2600 | tf_op jit(solution)/shard_map/ppermute | solution.py:107
  17.8 1.5 %collective-permute-start.7 = (bf16[3,3,3,8]{3,2,1,0:T(4,128)(2,1)}, bf16[3,3,3,8]{3,2,1,0:T(4,128)(2,1)S(1)}, u32[]{:S(2)}, u32[]{:S(2)}) collective-permute-start(bf16[3,3,3,8]{3,2,1,0:T(4,128)(2,1)} %bitcast.59), channel_id=1, source_target_pairs={{0,1},{1,0},{2,3},{3,2},{4,5},{5,4},{6,7},{7,6},{8,9},{9,8},{10,11... | collective-permute-start | bytes 1304 | tf_op jit(solution)/shard_map/ppermute | solution.py:107
  19.3 0.8 %copy-start.1 = (bf16[8,16,3,3,3]{1,0,4,3,2:T(8,128)(2,1)S(1)}, bf16[8,16,3,3,3]{1,0,4,3,2:T(8,128)(2,1)}, u32[]{:S(2)}) copy-start(bf16[8,16,3,3,3]{1,0,4,3,2:T(8,128)(2,1)} %param.17) | copy-start | bytes 20740
  20.1 0.7 %copy-start.2 = (bf16[8,2,3,3,3]{0,1,4,3,2:T(2,128)(2,1)S(1)}, bf16[8,2,3,3,3]{0,1,4,3,2:T(2,128)(2,1)}, u32[]{:S(2)}) copy-start(bf16[8,2,3,3,3]{0,1,4,3,2:T(2,128)(2,1)} %param.16) | copy-start | bytes 2596
  20.9 0.7 %copy-start.3 = (bf16[1,8,3,3,3]{1,4,3,2,0:T(4,128)(2,1)S(1)}, bf16[1,8,3,3,3]{1,4,3,2,0:T(4,128)(2,1)}, u32[]{:S(2)}) copy-start(bf16[1,8,3,3,3]{1,4,3,2,0:T(4,128)(2,1)} %param.18) | copy-start | bytes 1300
  22.4 0.7 %copy-start.4 = (s32[4,4,8,1]{2,3,1,0:T(1,128)S(1)}, s32[4,4,8,1]{2,3,1,0:T(1,128)}, u32[]{:S(2)}) copy-start(s32[4,4,8,1]{2,3,1,0:T(1,128)} %param.22) | copy-start | bytes 1540
  23.1 0.7 %copy-start.5 = (s32[4,4,8,1]{2,3,1,0:T(1,128)S(1)}, s32[4,4,8,1]{2,3,1,0:T(1,128)}, u32[]{:S(2)}) copy-start(s32[4,4,8,1]{2,3,1,0:T(1,128)} %param.23) | copy-start | bytes 1540
  23.7 0.7 %copy-start.6 = (f32[16,3]{0,1:T(4,128)S(1)}, f32[16,3]{0,1:T(4,128)}, u32[]{:S(2)}) copy-start(f32[16,3]{0,1:T(4,128)} %param.19) | copy-start | bytes 580
  24.4 0.7 %copy-start.7 = (f32[16]{0:T(128)S(1)}, f32[16]{0:T(128)}, u32[]{:S(2)}) copy-start(f32[16]{0:T(128)} %readout.1) | copy-start | bytes 196
  37.1 1.3 %collective-permute-start.8 = (f32[176,128]{1,0:T(8,128)S(1)}, f32[176,128]{1,0:T(8,128)S(1)}, u32[]{:S(2)}, u32[]{:S(2)}) collective-permute-start(f32[176,128]{1,0:T(8,128)S(1)} %get-tuple-element.23), channel_id=1, source_target_pairs={{0,1},{1,0},{2,3},{3,2},{4,5},{5,4},{6,7},{7,6},{8,9},{9,8},{10,11... | collective-permute-start | bytes 270344 | tf_op jit(solution)/shard_map/ppermute | solution.py:586
  38.5 4.5 %collective-permute-start.10 = (f32[80,128]{1,0:T(8,128)S(1)}, f32[80,128]{1,0:T(8,128)S(1)}, u32[]{:S(2)}, u32[]{:S(2)}) collective-permute-start(f32[80,128]{1,0:T(8,128)S(1)} %get-tuple-element.57), channel_id=1, source_target_pairs={{0,4},{1,5},{2,6},{3,7},{4,0},{5,1},{6,2},{7,3},{8,12},{9,13},{10,... | collective-permute-start | bytes 122888 | tf_op jit(solution)/shard_map/ppermute | solution.py:586
  39.3 4.9 %collective-permute-start.11 = (f32[80,128]{1,0:T(8,128)S(1)}, f32[80,128]{1,0:T(8,128)S(1)}, u32[]{:S(2)}, u32[]{:S(2)}) collective-permute-start(f32[80,128]{1,0:T(8,128)S(1)} %get-tuple-element.56), channel_id=1, source_target_pairs={{0,6},{1,7},{2,4},{3,5},{4,2},{5,3},{6,0},{7,1},{8,14},{9,15},{10,... | collective-permute-start | bytes 122888 | tf_op jit(solution)/shard_map/ppermute | solution.py:586
  40.5 4.1 %collective-permute-start.9 = (f32[80,128]{1,0:T(8,128)S(1)}, f32[80,128]{1,0:T(8,128)S(1)}, u32[]{:S(2)}, u32[]{:S(2)}) collective-permute-start(f32[80,128]{1,0:T(8,128)S(1)} %get-tuple-element.58), channel_id=1, source_target_pairs={{0,2},{1,3},{2,0},{3,1},{4,6},{5,7},{6,4},{7,5},{8,10},{9,11},{10,... | collective-permute-start | bytes 122888 | tf_op jit(solution)/shard_map/ppermute | solution.py:586
  44.7 5.1 %collective-permute-start.12 = (f32[112,128]{1,0:T(8,128)S(1)}, f32[112,128]{1,0:T(8,128)S(1)}, u32[]{:S(2)}, u32[]{:S(2)}) collective-permute-start(f32[112,128]{1,0:T(8,128)S(1)} %constant_dynamic-update-slice_fusion.11), channel_id=1, source_target_pairs={{0,8},{1,9},{2,10},{3,11},{4,12},{5,13},{6,14},{7,15},{8,0},{9,1},... | collective-permute-start | bytes 172040 | tf_op jit(solution)/shard_map/ppermute | solution.py:586

commit v2 on v1

--- a/solution.py
+++ b/solution.py
@@ -40,9 +40,28 @@
             step(index)
 
 
-def weights_kernel(chan_ref, middle_own, first_own, last_own, middle_other, first_other, last_other,
-                   middle, first, last):
+def in_hbm(value):
+    return pltpu.with_memory_space_constraint(value, pltpu.HBM)
+
+
+def fetch(sources, targets, arrivals):
+    copies = [
+        pltpu.make_async_copy(source, target, arrivals.at[k])
+        for k, (source, target) in enumerate(zip(sources, targets))
+    ]
+    for copy in copies:
+        copy.start()
+    return copies
+
+
+def weights_kernel(chan_ref, middle_from, first_from, last_from,
+                   middle_other, first_other, last_other,
+                   middle, first, last, middle_own, first_own, last_own, arrivals):
     wide = HID * HID
+    for copy in fetch(
+        (middle_from, first_from, last_from), (middle_own, first_own, last_own), arrivals
+    ):
+        copy.wait()
     chan = chan_ref[0]
     lane_z = iota((HID, wide), 1) >> 4
     row_z = iota((HID, wide), 0)
@@ -98,14 +117,17 @@
         last[tap * HID : (tap + 1) * HID, :] = banded(rows, -1)
 
 
-def build_weights(chan, conv_first, conv_middle, conv_last):
-    own = (
+def own_weights(conv_first, conv_middle, conv_last):
+    return (
         conv_middle.transpose(2, 3, 4, 0, 1).reshape(27, 8, HID),
         conv_first.transpose(2, 3, 4, 1, 0).reshape(27, 2, 8),
         conv_last.transpose(0, 2, 3, 4, 1).reshape(3, 3, 3, 8),
     )
-    other = tuple(lax.ppermute(value, "chan", [(0, 1), (1, 0)]) for value in own)
+
+
+def build_weights(chan, own, other):
     wide = HID * HID
+    hbm = pl.BlockSpec(memory_space=pltpu.HBM)
     smem = pl.BlockSpec(memory_space=pltpu.SMEM)
     vmem = pl.BlockSpec(memory_space=pltpu.VMEM)
     return pl.pallas_call(
@@ -115,12 +137,14 @@
             jax.ShapeDtypeStruct((2 * TAPS * HID, wide), BF16),
             jax.ShapeDtypeStruct((TAPS * HID, wide), BF16),
         ),
-        in_specs=[smem] + [vmem] * 6,
+        in_specs=[smem] + [hbm] * 3 + [vmem] * 3,
         out_specs=(vmem, vmem, vmem),
+        scratch_shapes=[pltpu.VMEM(value.shape, value.dtype) for value in own]
+        + [pltpu.SemaphoreType.DMA((3,))],
         compiler_params=pltpu.CompilerParams(vmem_limit_bytes=16 * MIB),
         cost_estimate=pl.CostEstimate(flops=10**8, bytes_accessed=2 * 10**6, transcendentals=0),
         name="band_weights",
-    )(chan, *own, *other)
+    )(chan, *(in_hbm(value) for value in own), *other)
 
 
 def sigmoid(value):
@@ -128,7 +152,7 @@
 
 
 def projector(sizes, table, footprints):
-    rows_count, per_view = (sizes[0], sizes[9])
+    rows_count, per_view = (sizes[0], sizes[-1])
     groups = rows_count // 8
 
     def tile_of(tile, owner):
@@ -165,14 +189,14 @@
 
 
 def dual_gradients(sizes, table, scalars, footprints, proj, dual, meas, grad_tiles, grad, sums):
-    rows_count, chans, detectors, tiles, width = sizes[:5]
-    low = (table[2][0] * chans + table[3][0]) * width
+    detectors, width = (sizes[2], sizes[4])
+    own_tile = lax.div(sizes[7][2](table[2][0], table[3][0]) * width, TILE)
     tile_of, _, project = projector(sizes, table, footprints)
     batch, mixed_of, stack_of = dual_reader(scalars, proj, dual, meas)
 
     def project_grad(tile):
         def pick(t, o):
-            return grad_tiles[o, (tile_of(t, o) == lax.div(low, TILE)).astype(jnp.int32)]
+            return grad_tiles[o, (tile_of(t, o) == own_tile).astype(jnp.int32)]
 
         grad[tile] = project(tile, pick)
 
@@ -201,7 +225,7 @@
     return jnp.transpose(filled)[0:8]
 
 
-def dual_gradients_kernel(sizes, rows_ref, blocks_ref, row_ref, chan_ref, mixing, readout,
+def dual_gradients_kernel(sizes, rows_ref, blocks_ref, mixing, readout, row_ref, chan_ref,
                           footprints, proj, dual, meas, grad_tiles, out, grad, sums):
     table = (rows_ref, blocks_ref, row_ref, chan_ref)
     out[...] = dual_gradients(
@@ -209,35 +233,80 @@
     )
 
 
-def main_kernel(sizes, whole, rows_ref, blocks_ref, row_ref, chan_ref, mixing, readout, payload, footprints, middle, first, last,
+def pack_kernel(chan_ref, volume_from, cotangent_from, dual_from, measured_from, out,
+                volume, cotangent, dual, measured, arrivals):
+    copies = fetch(
+        (volume_from, cotangent_from, dual_from, measured_from),
+        (volume, cotangent, dual, measured),
+        arrivals,
+    )
+    chan = chan_ref[0]
+    blocks = volume.shape[1] // (2 * TILE)
+
+    def block(rows, k):
+        begin = 2 * k * TILE
+        pair = [rows[:, begin : begin + TILE], rows[:, begin + TILE : begin + 2 * TILE]]
+        return jnp.concatenate(pair, axis=0).astype(BF16)
+
+    for copy in copies:
+        copy.wait()
+    for index, source in enumerate((volume, cotangent)):
+        value = source[...].astype(F32)
+        half = jnp.where(chan == 0, value[:8], value[8:])
+        for k in range(blocks):
+            out[0, index * blocks + k] = block(half, k)
+    out[0, 2 * blocks] = block(dual[...].astype(F32), 0)
+    out[0, 2 * blocks + 1] = block(measured[...].astype(F32), 0)
+
+
+def main_kernel(sizes, whole, rows_from, blocks_from, mixing_from, readout_from,
+                footprints_from, row_ref, chan_ref, payload, payload_other, middle, first, last,
                 keep, send, dual_out, proj, dual, meas, grad_tiles,
-                vol, cot, dual_half, dual_new, back, field, col_in, col_cot,
-                act_wide, grad_wide, slope_first, slope_middle, row_tiles, sums):
-    rows_count, chans, detectors, tiles, width, stride, cells, piece_slot, update_row, _ = sizes
+                vol, dual_half, dual_new, back, field, col_in, col_cot,
+                act_wide, grad_wide, slope_first, slope_middle, row_tiles, sums,
+                rows_ref, blocks_ref, mixing, readout, footprints, arrivals):
+    rows_count, chans, detectors, tiles, width, stride, cells, places, updates, _ = sizes
+    piece_slot, update_row, chunk_of, flip_of = places
+    copies = fetch(
+        (rows_from, blocks_from, mixing_from, readout_from, footprints_from),
+        (rows_ref, blocks_ref, mixing, readout, footprints),
+        arrivals,
+    )
     table = (rows_ref, blocks_ref, row_ref, chan_ref)
     scalars = (mixing, readout)
     row = row_ref[0]
     chan = chan_ref[0]
-    low = (row * chans + chan) * width
+    low = chunk_of(row, chan) * width
     count = rows_count * stride
-    lanes = count + TILE
+    pad = -(-(stride + 1) // TILE) * TILE
+    lanes = count + pad
+
+    flip = flip_of(chan)
+
+    def halves_of(owner, k):
+        slot = piece_slot(owner, row)
+        mine = payload[slot, k].astype(F32)
+        theirs = payload_other[slot, k].astype(F32)
+        return jnp.where(flip == 0, mine, theirs), jnp.where(flip == 0, theirs, mine)
 
     def place(owner):
-        slots = [piece_slot(owner, part, row, chan) for part in range(2)]
-        for field_index, target in ((0, vol), (1, cot)):
-            for k in range(tiles // 2):
-                halves = [payload[slot, field_index * (tiles // 2) + k].astype(F32) for slot in slots]
-                for t in range(2):
-                    whole_tile = jnp.concatenate([h[t * 8 : (t + 1) * 8] for h in halves], axis=0)
-                    target[owner * tiles + 2 * k + t] = whole_tile.astype(BF16)
+        for k in range(tiles // 2):
+            halves = halves_of(owner, k)
+            for t in range(2):
+                whole_tile = jnp.concatenate([h[t * 8 : (t + 1) * 8] for h in halves], axis=0)
+                vol[owner * tiles + 2 * k + t] = whole_tile.astype(BF16)
         for k, target in ((tiles, dual), (tiles + 1, meas)):
-            for part in range(2):
-                piece = payload[slots[part], k].astype(F32)
-                for t in range(2):
-                    target[owner * 2 + t, part * 8 : (part + 1) * 8, :] = piece[t * 8 : (t + 1) * 8]
+            halves = halves_of(owner, k)
+            for t in range(2):
+                for part in range(2):
+                    target[owner * 2 + t, part * 8 : (part + 1) * 8, :] = halves[part][
+                        t * 8 : (t + 1) * 8
+                    ]
 
     repeat(rows_count, place)
 
+    for copy in copies:
+        copy.wait()
     tile_of, block_of, project = projector(sizes, table, footprints)
 
     def project_volume(tile):
@@ -264,7 +333,9 @@
 
     window = width + 2 * REACH
     tile_low = lax.div(low - REACH + TILE, TILE) - 1
-    offset = low - REACH - tile_low * TILE
+    aligned = width % TILE == 0
+    offset = TILE - REACH if aligned else low - REACH - tile_low * TILE
+    sides = 3 if aligned else 2
 
     def backproject(group):
         owners = [group * 8 + o for o in range(8)]
@@ -276,48 +347,54 @@
             for o in range(8):
                 place_of = tile_of(tile, owners[o]) - tile_low
                 product = products[:, o * TILE : (o + 1) * TILE]
-                for side in range(2):
-                    out.append(totals[2 * o + side] + jnp.where(place_of == side, product, 0.0))
+                for side in range(sides):
+                    out.append(totals[sides * o + side] + jnp.where(place_of == side, product, 0.0))
             return tuple(out)
 
-        totals = tuple(jnp.zeros((16, TILE), F32) for _ in range(16))
+        totals = tuple(jnp.zeros((16, TILE), F32) for _ in range(8 * sides))
         if detectors <= 16:
             for tile in range(detectors):
                 totals = add(tile, totals)
         else:
             totals = lax.fori_loop(0, detectors, add, totals)
         for o in range(8):
-            for side in range(2):
-                back[owners[o], side] = totals[2 * o + side]
+            for side in range(sides):
+                back[owners[o], side] = totals[sides * o + side]
 
     repeat(rows_count // 8, backproject)
 
     lane = iota((3 * 16, TILE), 1)
-    clip_low = jnp.clip(tile_low, 0, tiles - 1)
-    clip_high = jnp.clip(tile_low + 1, 0, tiles - 1)
+    clipped = [jnp.clip(tile_low + side, 0, tiles - 1) for side in range(sides)]
     pieces = [None] * (lanes // TILE)
     for y in range(rows_count):
-        sides = []
-        for side, clipped in ((0, clip_low), (1, clip_high)):
-            sides.append(
-                jnp.concatenate(
-                    [
-                        vol[y * tiles + clipped].astype(F32),
-                        back[y, side].astype(BF16).astype(F32),
-                        cot[y * tiles + clipped].astype(F32),
-                    ],
-                    axis=0,
-                )
+        moved = []
+        for side in range(sides):
+            halves = halves_of(y, tiles // 2 + (clipped[side] >> 1))
+            odd = (clipped[side] & 1) == 1
+            merged = jnp.concatenate(
+                [
+                    vol[y * tiles + clipped[side]].astype(F32),
+                    back[y, side].astype(BF16).astype(F32),
+                    jnp.where(odd, halves[0][8:], halves[0][:8]),
+                    jnp.where(odd, halves[1][8:], halves[1][:8]),
+                ],
+                axis=0,
             )
-        merged = jnp.where(lane >= offset, sides[0], sides[1])
-        shift = lax.rem(y * stride - offset + TILE * (count // TILE + 1), TILE)
-        merged = pltpu.roll(merged, shift, 1)
+            if aligned:
+                shift = (y * stride - offset) % TILE
+            else:
+                shift = lax.rem(y * stride - offset + TILE * (count // TILE + 1), TILE)
+            moved.append(pltpu.roll(merged, shift, 1))
         for t in range(y * stride // TILE, (y * stride + window - 1) // TILE + 1):
             column = lane + (t * TILE - y * stride)
             cell = column + (low - REACH)
             inside = (column >= 0) & (column < window) & (cell >= 0) & (cell < cells)
-            taken = jnp.where(inside, merged, 0.0)
-            pieces[t] = taken if pieces[t] is None else pieces[t] + taken
+            for side in range(sides):
+                least = t * TILE - y * stride + offset
+                if aligned and (least + TILE <= side * TILE or least >= (side + 1) * TILE):
+                    continue
+                taken = jnp.where(inside & ((column + offset) >> 7 == side), moved[side], 0.0)
+                pieces[t] = taken if pieces[t] is None else pieces[t] + taken
     for t in range(lanes // TILE):
         field[:, t * TILE : (t + 1) * TILE] = (
             jnp.zeros((3 * 16, TILE), F32) if pieces[t] is None else pieces[t]
@@ -375,7 +452,7 @@
     middle_half = middle_act.astype(BF16)
 
     def gather_taps(products, sign):
-        padded = jnp.concatenate([products, jnp.zeros((TAPS * HID, TILE), F32)], axis=1)
+        padded = jnp.concatenate([products, jnp.zeros((TAPS * HID, pad), F32)], axis=1)
         total = None
         for tap in range(TAPS):
             part = rolled(padded[tap * HID : (tap + 1) * HID], sign * shift_of(tap))
@@ -392,7 +469,10 @@
                 inside = (column >= begin) & (column < begin + width)
                 part = jnp.where(inside, value[:, t * TILE : (t + 1) * TILE], 0.0)
                 merged = part if merged is None else merged + part
-            shift = lax.rem(low - begin + TILE * (count // TILE + 1), TILE)
+            if aligned:
+                shift = -begin % TILE
+            else:
+                shift = lax.rem(low - begin + TILE * (count // TILE + 1), TILE)
             target(y, pltpu.roll(merged, shift, 1))
 
     update = gather_taps(dot(last[...], middle_half, NT), -1) + field[0:16, :]
@@ -501,7 +581,7 @@
         keep[pl.ds(begin, 16), :] = tile
         send[pl.ds(begin, 16), :] = tile
 
-    repeat(rows_count, put_update)
+    repeat(updates, put_update)
 
 
 def write_grads(chan, grads, middle, first, last, mixing, readout):
@@ -523,16 +603,18 @@
     readout[...] = grads[40:41, :HID]
 
 
-def finish_kernel(row_ref, chan_ref, own, one, two, three, far, total, volume, *rest):
+def finish_kernel(row_ref, chan_ref, keep, near, one, two, three, volume, *rest):
     grads, slots = (rest[:-1], rest[-1])
     row = row_ref[0]
-    write_grads(chan_ref[0], total[...] + far[0:48, :], *grads)
+    chan = chan_ref[0]
+    total = keep[0:48, :] + near[0:48, :] + one[0:48, :] + two[0:48, :] + three[0:48, :]
+    write_grads(chan, total, *grads)
     for k, (source, begin) in enumerate(
-        ((own, 48), (one, 48), (two, 48), (three, 48), (far, 48), (far, 64), (far, 80), (far, 96))
+        ((keep, 48), (near, 48), (one, 48), (one, 64), (two, 48), (two, 64), (three, 48), (three, 64))
     ):
         slots[k] = source[begin : begin + 16, :]
     for tile in range(8):
-        volume[:, tile, :] = slots[tile ^ row]
+        volume[:, tile, :] = slots[(((tile >> 1) ^ (row & 3)) << 1) + ((tile & 1) ^ chan)]
 
 
 def finish_grads_kernel(chan_ref, total, *grads):
@@ -562,57 +644,86 @@
     devices = rows_count * chans
     cells = volume.shape[2]
     tiles = cells // TILE
-    width = cells // devices
+    quick = rows_count == 8 and chans == 2 and tiles == 8
+    copies = 2 if quick else 1
+    width = cells * copies // devices
     stride = -(-(width + 2 * REACH) // 16) * 16
     detectors = tile_rows.shape[0] * tile_rows.shape[1]
     chan = lax.axis_index("chan")
     row = lax.axis_index("view") * slabs + lax.axis_index("slab")
-    quick = rows_count == 8 and chans == 2
-
-    def chan_half(value):
-        shaped = jnp.swapaxes(value.reshape(2, 8, tiles, TILE), 1, 2)
-        half = lax.dynamic_index_in_dim(shaped, chan, 0, keepdims=False)
-        return half.reshape(tiles // 2, 16, TILE)
-
-    def dual_piece(value):
-        return jnp.swapaxes(value.reshape(8, 2, TILE), 0, 1).reshape(1, 16, TILE)
-
-    payload = jnp.concatenate(
-        [chan_half(volume), chan_half(cotangent), dual_piece(dual_state), dual_piece(measured)],
-        axis=0,
-    )[None]
+
+    row_one = row.reshape(1).astype(jnp.int32)
+    chan_one = chan.reshape(1).astype(jnp.int32)
+    vmem = pl.BlockSpec(memory_space=pltpu.VMEM)
+    smem = pl.BlockSpec(memory_space=pltpu.SMEM)
+    hbm = pl.BlockSpec(memory_space=pltpu.HBM)
+    raw = (
+        volume.reshape(16, cells),
+        cotangent.reshape(16, cells),
+        dual_state.reshape(8, 2 * TILE),
+        measured.reshape(8, 2 * TILE),
+    )
+    payload = pl.pallas_call(
+        pack_kernel,
+        out_shape=jax.ShapeDtypeStruct((1, tiles + 2, 16, TILE), BF16),
+        in_specs=[smem] + [hbm] * 4,
+        out_specs=vmem,
+        scratch_shapes=[pltpu.VMEM(value.shape, value.dtype) for value in raw]
+        + [pltpu.SemaphoreType.DMA((4,))],
+        compiler_params=pltpu.CompilerParams(vmem_limit_bytes=4 * MIB),
+        name="pack",
+    )(chan_one, *(in_hbm(value) for value in raw))
 
     def swap(value, mask):
         return lax.ppermute(value, ALL_AXES, row_mask_pairs(devices, mask))
 
+    own = own_weights(conv_first, conv_middle, conv_last)
     if quick:
-        payload = jnp.concatenate([payload, swap(payload, 8)], axis=0)
-        payload = jnp.concatenate([payload] + [swap(payload, k) for k in (2, 4, 6)], axis=0)
-        payload = jnp.concatenate([payload, swap(payload, 1)], axis=0)
+        far_payload = swap(payload, 8)
+        other = tuple(swap(value, 1) for value in own)
+        payload = jnp.concatenate([payload, far_payload], axis=0)
+        payload, other = lax.optimization_barrier((payload, other))
+        pieces = [swap(payload, k) for k in (2, 4, 6)]
+        weights = build_weights(chan_one, own, other)
+        pieces[0], weights = lax.optimization_barrier((pieces[0], weights))
+        payload = jnp.concatenate([payload] + pieces, axis=0)
+        payload_other = swap(payload, 1)
     else:
         payload = lax.all_gather(payload, ALL_AXES, axis=0, tiled=True)
-
-    def piece_slot(owner, part, row, chan):
+        payload = payload.reshape(rows_count, chans, *payload.shape[1:])
+        payload, payload_other = (payload[:, 0], payload[:, 1])
+        weights = build_weights(chan_one, own, tuple(swap(value, 1) for value in own))
+    middle, first, last = weights
+
+    def piece_slot(owner, row):
         if not quick:
-            return owner * chans + part
+            return owner
         mask = owner ^ row
-        return (mask & 3) * 2 + (mask >> 2) + rows_count * (part ^ chan)
+        return (mask & 3) * 2 + (mask >> 2)
 
     def update_row(owner, row):
         return owner ^ row if quick else owner
 
-    row_one = row.reshape(1).astype(jnp.int32)
-    chan_one = chan.reshape(1).astype(jnp.int32)
-    middle, first, last = build_weights(chan_one, conv_first, conv_middle, conv_last)
-    table = (jnp.swapaxes(tile_rows, 2, 3), jnp.swapaxes(tile_blocks, 2, 3), row_one, chan_one)
-    scalars = (dual_mixing.T, dual_readout)
+    def chunk_of(row, chan):
+        return ((row & 3) if quick else row) * chans + chan
+
+    def flip_of(chan):
+        return chan if quick else 0
+
+    updates = 4 if quick else rows_count
+    table = (
+        jnp.swapaxes(tile_rows, 2, 3),
+        jnp.swapaxes(tile_blocks, 2, 3),
+        dual_mixing.T,
+        dual_readout,
+    )
     count = rows_count * stride
     wide = HID * HID
-    moved = 48 + 16 * rows_count
+    moved = 48 + 16 * updates
+    pad = -(-(stride + 1) // TILE) * TILE
     limit = (20 if quick else 56) * MIB
-    vmem = pl.BlockSpec(memory_space=pltpu.VMEM)
-    smem = pl.BlockSpec(memory_space=pltpu.SMEM)
-    sizes = (rows_count, chans, detectors, tiles, width, stride, cells, piece_slot, update_row,
+    sizes = (rows_count, chans, detectors, tiles, width, stride, cells,
+             (piece_slot, update_row, chunk_of, flip_of), updates,
              tile_rows.shape[1])
     outs = [
         ((moved, TILE), F32),
@@ -627,11 +738,10 @@
     ]
     scratch = [
         ((rows_count * tiles, 16, TILE), BF16),
-        ((rows_count * tiles, 16, TILE), BF16),
         ((detectors, 16, TILE), BF16),
         ((detectors, 16, TILE), F32),
-        ((rows_count, 2, 16, TILE), F32),
-        ((48, count + TILE), F32),
+        ((rows_count, 3, 16, TILE), F32),
+        ((48, count + pad), F32),
         ((2 * TAPS * HID, count), BF16),
         ((TAPS * HID, count), BF16),
         ((count + 2 * stride, 3 * wide), BF16),
@@ -648,44 +758,54 @@
     keep, send, new_dual, *rest = pl.pallas_call(
         functools.partial(main_kernel, sizes, quick),
         out_shape=[jax.ShapeDtypeStruct(*spec) for spec in outs],
-        in_specs=[smem] * 6 + [vmem] * 5,
+        in_specs=[hbm] * 5 + [smem] * 2 + [vmem] * 5,
         out_specs=[vmem] * len(outs),
-        scratch_shapes=[pltpu.VMEM(*spec) for spec in scratch],
+        scratch_shapes=[pltpu.VMEM(*spec) for spec in scratch]
+        + [pltpu.SMEM(value.shape, value.dtype) for value in table]
+        + [pltpu.VMEM(footprints.shape, BF16), pltpu.SemaphoreType.DMA((5,))],
         compiler_params=pltpu.CompilerParams(vmem_limit_bytes=limit),
         cost_estimate=pl.CostEstimate(
             flops=5 * 10**9, bytes_accessed=5 * 10**6, transcendentals=2 * 10**6
         ),
         name="primal_dual",
-    )(*table, *scalars, payload, footprints, middle, first, last)
-
-    mine = keep + swap(send, 1)
+    )(
+        *(in_hbm(value) for value in (*table, footprints)),
+        row_one,
+        chan_one,
+        payload,
+        payload_other,
+        middle,
+        first,
+        last,
+    )
+
+    near = swap(send, 1)
     grad_shapes = [
         jax.ShapeDtypeStruct(shape, F32)
         for shape in ((27, 8, HID), (27, 2, 8), (27, 1, 8), (3, HID), (1, HID))
     ]
     if quick:
 
+        sums = keep[:48] + near[:48]
+
         def piece(value, index):
             return value[48 + 16 * index : 64 + 16 * index]
 
         parts = [
-            swap(jnp.concatenate([mine[:48], piece(mine, k), piece(mine, k ^ 4)], axis=0), 2 * k)
+            swap(jnp.concatenate([sums, piece(keep, k), piece(near, k)], axis=0), 2 * k)
             for k in (1, 2, 3)
         ]
-        total = mine[:48] + parts[0][:48] + parts[1][:48] + parts[2][:48]
-        far = swap(
-            jnp.concatenate([total, piece(mine, 4)] + [piece(part, 1) for part in parts], axis=0), 8
-        )
         new_volume, *grads = pl.pallas_call(
             finish_kernel,
             out_shape=[jax.ShapeDtypeStruct((16, 8, TILE), F32)] + grad_shapes,
-            in_specs=[smem, smem] + [vmem] * 6,
+            in_specs=[smem, smem] + [vmem] * 5,
             out_specs=[vmem] * 6,
             scratch_shapes=[pltpu.VMEM((8, 16, TILE), F32)],
             compiler_params=pltpu.CompilerParams(vmem_limit_bytes=8 * MIB),
             name="finish",
-        )(row_one, chan_one, mine, *parts, far, total)
+        )(row_one, chan_one, keep, near, *parts)
     else:
+        mine = keep + near
         small = pl.pallas_call(
             functools.partial(dual_gradients_kernel, sizes),
             out_shape=jax.ShapeDtypeStruct((8, TILE), F32),
@@ -697,7 +817,7 @@
             ],
             compiler_params=pltpu.CompilerParams(vmem_limit_bytes=limit),
             name="dual_gradients",
-        )(*table, *scalars, footprints, *rest)
+        )(*table, row_one, chan_one, footprints, *rest)
         total = jnp.concatenate(
             [lax.psum(mine[:40], ROW_AXES), lax.psum(small, ALL_AXES)], axis=0
         )

time: 51.3 us -> 42.2 us (0.82)
  local copies, waits for them, and re-layouts: 6.03 us -> 0.06 us
  Pallas kernels: 13.5 us -> 18.7 us
  starting transfers between devices: 15.5 us -> 12 us
  waiting for transfers between devices: 13.3 us -> 10.4 us
  other arithmetic: 1.47 us -> 0.03 us
    unnamed x22 -> x3, local copies, waits for them, and re-layouts: 5.05 us -> 0.04 us
    pallas_call x1, Pallas kernels: 12 us -> 15.5 us  [body(): pl.pallas_call(functools.partial(main_kernel, sizes, quick), out_shape=[j...]
    ppermute x10 -> x12, starting transfers between devices: 14.5 us -> 12 us  [swap(): return lax.ppermute(value, ALL_AXES, row_mask_pairs(devices, mask))]
    ppermute x10 -> x12, waiting for transfers between devices: 12.3 us -> 10.4 us  [swap(): return lax.ppermute(value, ALL_AXES, row_mask_pairs(devices, mask))]
    ppermute x3 -> x0, waiting for transfers between devices: 1.05 us -> none  [build_weights(): lax.ppermute(value, 'chan', [(0, 1), (1, 0)])]
    ppermute x3 -> x0, starting transfers between devices: 1.01 us -> none  [build_weights(): lax.ppermute(value, 'chan', [(0, 1), (1, 0)])]
    another operation x1 -> x0, local copies, waits for them, and re-layouts: 0.89 us -> none
    pallas_call x1, Pallas kernels: 0.72 us -> 1.57 us  [build_weights(): pl.pallas_call(weights_kernel, out_shape=(jax.ShapeDtypeStruct((3, 3 * wi...]
  transfers between devices with their start and end apart: 13 -> 12, of which waited for: 10 -> 8; matrix products, arithmetic and copies ran while one was open for 2% -> 0% of each run, Pallas kernels for 1% -> 4%
where the time goes in v2:
time: 42.2 us; the launch traced here: 41.9 us
  Pallas kernels  18.7 us (44%)
  starting transfers between devices  12 us (28%)
  waiting for transfers between devices  10.4 us (25%)
  between operations  0.75 us (2%)
    pallas_call x1, Pallas kernels, body(): pl.pallas_call(functools.partial(main_kernel, sizes, quick), out_shape=[j...  15.5 us
    ppermute x12, starting transfers between devices, swap(): return lax.ppermute(value, ALL_AXES, row_mask_pairs(devices, mask))  12 us
    ppermute x12, waiting for transfers between devices, swap(): return lax.ppermute(value, ALL_AXES, row_mask_pairs(devices, mask))  10.4 us
    pallas_call x1, Pallas kernels, build_weights(): pl.pallas_call(weights_kernel, out_shape=(jax.ShapeDtypeStruct((3, 3 * wi...  1.57 us
  transfers between devices with their start and end apart: 12, of which 8 were waited for; matrix products, arithmetic and copies ran while one was open for 0% of the time, Pallas kernels for 4%

profile of v2, /device:TPU:0, one launch (start us, length us, event | category | flops | bytes accessed | tf_op | source)
XLA Modules:
  0.0 41.9 jit_solution(31185379902509101)
XLA Ops:
  0.6 0.8 %pack.1 = bf16[1,10,16,128]{3,2,1,0:T(8,128)(2,1)S(1)} custom-call(s32[1]{0:T(128)} %bitcast.1.chan_ref, bf16[16,1024]{1,0:T(8,128)(2,1)} %bitcast.35, bf16[16,1024]{1,0:T(8,128)(2,1)} %bitcast.36, bf16[8,256]{1,0:T(8,128)(2,1)} %bitcast.37, bf16[8,256]{1,0:T(8,128)(2,1)} %bitcast.38), custom_call_target="tpu_custom_call" | custom-call | tf_op jit(solution)/shard_map/pack/pallas_call | solution.py:666
  1.5 4.1 %collective-permute-start = (bf16[1,10,16,128]{3,2,1,0:T(8,128)(2,1)S(1)}, bf16[1,10,16,128]{3,2,1,0:T(8,128)(2,1)S(1)}, u32[]{:S(2)}, u32[]{:S(2)}) collective-permute-start(bf16[1,10,16,128]{3,2,1,0:T(8,128)(2,1)S(1)} %pack.1), channel_id=1, source_target_pairs={{0,8},{1,9},{2,10},{3,11},{4,12},{5,13},{6,14},{7,15},{8,0},{9,1},... | collective-permute-start | bytes 122888 | tf_op jit(solution)/shard_map/ppermute | solution.py:678
  5.6 0.0 collective-permute-start.1
  5.6 0.5 %collective-permute-start.2 = (bf16[27,2,8]{2,1,0:T(2,128)(2,1)}, bf16[27,2,8]{2,1,0:T(2,128)(2,1)S(1)}, u32[]{:S(2)}, u32[]{:S(2)}) collective-permute-start(bf16[27,2,8]{2,1,0:T(2,128)(2,1)} %bitcast.44), channel_id=1, source_target_pairs={{0,1},{1,0},{2,3},{3,2},{4,5},{5,4},{6,7},{7,6},{8,9},{9,8},{10,11... | collective-permute-start | bytes 2600 | tf_op jit(solution)/shard_map/ppermute | solution.py:678
  6.1 0.0 collective-permute-start.3
  6.1 1.9 %collective-permute-done = bf16[1,10,16,128]{3,2,1,0:T(8,128)(2,1)S(1)} collective-permute-done((bf16[1,10,16,128]{3,2,1,0:T(8,128)(2,1)S(1)}, bf16[1,10,16,128]{3,2,1,0:T(8,128)(2,1)S(1)}, u32[]{:S(2)}, u32[]{:S(2)}) %collective-permute-start) | collective-permute-done | bytes 40992 | tf_op jit(solution)/shard_map/ppermute | solution.py:678
  8.0 1.8 %collective-permute-start.4 = (bf16[2,10,16,128]{3,2,1,0:T(8,128)(2,1)S(1)}, bf16[2,10,16,128]{3,2,1,0:T(8,128)(2,1)S(1)}, u32[]{:S(2)}, u32[]{:S(2)}) collective-permute-start(bf16[2,10,16,128]{3,2,1,0:T(8,128)(2,1)S(1)} %pad_maximum_fusion), channel_id=1, source_target_pairs={{0,2},{1,3},{2,0},{3,1},{4,6},{5,7},{6,4},{7,5},{8,10},{9,11},{10,... | collective-permute-start | bytes 245768 | tf_op jit(solution)/shard_map/ppermute | solution.py:678
  9.8 1.3 %collective-permute-start.5 = (bf16[2,10,16,128]{3,2,1,0:T(8,128)(2,1)S(1)}, bf16[2,10,16,128]{3,2,1,0:T(8,128)(2,1)S(1)}, u32[]{:S(2)}, u32[]{:S(2)}) collective-permute-start(bf16[2,10,16,128]{3,2,1,0:T(8,128)(2,1)S(1)} %pad_maximum_fusion), channel_id=1, source_target_pairs={{0,4},{1,5},{2,6},{3,7},{4,0},{5,1},{6,2},{7,3},{8,12},{9,13},{10,... | collective-permute-start | bytes 245768 | tf_op jit(solution)/shard_map/ppermute | solution.py:678
  11.1 0.5 %collective-permute-start.6 = (bf16[2,10,16,128]{3,2,1,0:T(8,128)(2,1)S(1)}, bf16[2,10,16,128]{3,2,1,0:T(8,128)(2,1)S(1)}, u32[]{:S(2)}, u32[]{:S(2)}) collective-permute-start(bf16[2,10,16,128]{3,2,1,0:T(8,128)(2,1)S(1)} %pad_maximum_fusion), channel_id=1, source_target_pairs={{0,6},{1,7},{2,4},{3,5},{4,2},{5,3},{6,0},{7,1},{8,14},{9,15},{10,... | collective-permute-start | bytes 245768 | tf_op jit(solution)/shard_map/ppermute | solution.py:678
  11.6 1.6 %band_weights.1 = (bf16[3,768,256]{2,1,0:T(8,128)(2,1)S(1)}, bf16[288,256]{1,0:T(8,128)(2,1)S(1)}, bf16[144,256]{1,0:T(8,128)(2,1)S(1)}) custom-call(s32[1]{0:T(128)} %bitcast.1.chan_ref, bf16[27,8,16]{2,1,0:T(8,128)(2,1)} %bitcast.42, bf16[27,2,8]{2,1,0:T(2,128)(2,1)} %bitcast.45, bf16[3,3,3,8]{3,2,1,0:T(4,128)(2,1)} %bitcast.48, ...), custom_call_target="tpu_custom_call" | custom-call | flops 100000000 | bytes 2000000 | tf_op jit(solution)/shard_map/band_weights/pallas_call | solution.py:133
  13.2 1.3 %collective-permute-done.5 = bf16[2,10,16,128]{3,2,1,0:T(8,128)(2,1)S(1)} collective-permute-done((bf16[2,10,16,128]{3,2,1,0:T(8,128)(2,1)S(1)}, bf16[2,10,16,128]{3,2,1,0:T(8,128)(2,1)S(1)}, u32[]{:S(2)}, u32[]{:S(2)}) %collective-permute-start.5) | collective-permute-done | bytes 81952 | tf_op jit(solution)/shard_map/ppermute | solution.py:678
  14.5 1.9 %collective-permute-done.6 = bf16[2,10,16,128]{3,2,1,0:T(8,128)(2,1)S(1)} collective-permute-done((bf16[2,10,16,128]{3,2,1,0:T(8,128)(2,1)S(1)}, bf16[2,10,16,128]{3,2,1,0:T(8,128)(2,1)S(1)}, u32[]{:S(2)}, u32[]{:S(2)}) %collective-permute-start.6) | collective-permute-done | bytes 81952 | tf_op jit(solution)/shard_map/ppermute | solution.py:678
  16.4 0.1 collective-permute-start.7
  16.5 1.6 %collective-permute-done.7.payload_other = bf16[8,10,16,128]{3,2,1,0:T(8,128)(2,1)S(1)} collective-permute-done((bf16[8,10,16,128]{3,2,1,0:T(8,128)(2,1)S(1)}, bf16[8,10,16,128]{3,2,1,0:T(8,128)(2,1)S(1)}, u32[]{:S(2)}, u32[]{:S(2)}) %collective-permute-start.7) | collective-permute-done | bytes 327712 | tf_op jit(solution)/shard_map/ppermute | solution.py:678
  18.1 15.5 %primal_dual.1 = (f32[112,128]{1,0:T(8,128)S(1)}, f32[112,128]{1,0:T(8,128)S(1)}, f32[8,256]{1,0:T(8,128)}) custom-call(s32[4,4,1,8]{3,2,1,0:T(1,128)} %bitcast.49, s32[4,4,1,8]{3,2,1,0:T(1,128)} %bitcast.50, f32[3,16]{1,0:T(4,128)} %bitcast.51, f32[16]{0:T(128)} %readout_from.1, bf16[64,128,128]{2,1,0:T(8,128)(2,1)} %footprints_from.1, s32[1]{0:T(128)} %bitcast.row_ref, ...), custom_call_target="tpu_custom_call" | custom-call | flops 5000000000 | bytes 5000000 | tf_op jit(solution)/shard_map/primal_dual/pallas_call | solution.py:758
  33.6 0.2 collective-permute-start.8
  33.8 1.1 %collective-permute-done.8.near = f32[112,128]{1,0:T(8,128)S(1)} collective-permute-done((f32[112,128]{1,0:T(8,128)S(1)}, f32[112,128]{1,0:T(8,128)S(1)}, u32[]{:S(2)}, u32[]{:S(2)}) %collective-permute-start.8) | collective-permute-done | bytes 57376 | tf_op jit(solution)/shard_map/ppermute | solution.py:678
  35.0 0.8 %collective-permute-start.10 = (f32[80,128]{1,0:T(8,128)S(1)}, f32[80,128]{1,0:T(8,128)S(1)}, u32[]{:S(2)}, u32[]{:S(2)}) collective-permute-start(f32[80,128]{1,0:T(8,128)S(1)} %get-tuple-element.61), channel_id=1, source_target_pairs={{0,4},{1,5},{2,6},{3,7},{4,0},{5,1},{6,2},{7,3},{8,12},{9,13},{10,... | collective-permute-start | bytes 122888 | tf_op jit(solution)/shard_map/ppermute | solution.py:678
  35.8 1.2 %collective-permute-start.11 = (f32[80,128]{1,0:T(8,128)S(1)}, f32[80,128]{1,0:T(8,128)S(1)}, u32[]{:S(2)}, u32[]{:S(2)}) collective-permute-start(f32[80,128]{1,0:T(8,128)S(1)} %get-tuple-element.60), channel_id=1, source_target_pairs={{0,6},{1,7},{2,4},{3,5},{4,2},{5,3},{6,0},{7,1},{8,14},{9,15},{10,... | collective-permute-start | bytes 122888 | tf_op jit(solution)/shard_map/ppermute | solution.py:678
  37.0 1.5 %collective-permute-start.9 = (f32[80,128]{1,0:T(8,128)S(1)}, f32[80,128]{1,0:T(8,128)S(1)}, u32[]{:S(2)}, u32[]{:S(2)}) collective-permute-start(f32[80,128]{1,0:T(8,128)S(1)} %get-tuple-element.62), channel_id=1, source_target_pairs={{0,2},{1,3},{2,0},{3,1},{4,6},{5,7},{6,4},{7,5},{8,10},{9,11},{10,... | collective-permute-start | bytes 122888 | tf_op jit(solution)/shard_map/ppermute | solution.py:678
  38.5 0.9 %collective-permute-done.10.two = f32[80,128]{1,0:T(8,128)S(1)} collective-permute-done((f32[80,128]{1,0:T(8,128)S(1)}, f32[80,128]{1,0:T(8,128)S(1)}, u32[]{:S(2)}, u32[]{:S(2)}) %collective-permute-start.10) | collective-permute-done | bytes 40992 | tf_op jit(solution)/shard_map/ppermute | solution.py:678
  39.4 1.3 %collective-permute-done.11.three = f32[80,128]{1,0:T(8,128)S(1)} collective-permute-done((f32[80,128]{1,0:T(8,128)S(1)}, f32[80,128]{1,0:T(8,128)S(1)}, u32[]{:S(2)}, u32[]{:S(2)}) %collective-permute-start.11) | collective-permute-done | bytes 40992 | tf_op jit(solution)/shard_map/ppermute | solution.py:678
  40.7 0.4 %collective-permute-done.9.one = f32[80,128]{1,0:T(8,128)S(1)} collective-permute-done((f32[80,128]{1,0:T(8,128)S(1)}, f32[80,128]{1,0:T(8,128)S(1)}, u32[]{:S(2)}, u32[]{:S(2)}) %collective-permute-start.9) | collective-permute-done | bytes 40992 | tf_op jit(solution)/shard_map/ppermute | solution.py:678
  41.1 0.8 %finish.1 = (f32[16,8,128]{2,1,0:T(8,128)}, f32[27,8,16]{2,1,0:T(8,128)}, f32[27,2,8]{2,1,0:T(2,128)}, f32[27,1,8]{2,1,0:T(1,128)}, f32[3,16]{1,0:T(4,128)}, /*index=5*/f32[1,16]{1,0:T(1,128)}) custom-call(s32[1]{0:T(128)} %bitcast.row_ref, s32[1]{0:T(128)} %bitcast.1.chan_ref, f32[112,128]{1,0:T(8,128)S(1)} %get-tuple-element.38.keep, ...), custom_call_target="tpu_custom_call" | custom-call | tf_op jit(solution)/shard_map/finish/pallas_call | solution.py:798
  (13 shorter events, 0.1 us)
Async XLA Ops:
  1.5 6.5 %collective-permute-start = (bf16[1,10,16,128]{3,2,1,0:T(8,128)(2,1)S(1)}, bf16[1,10,16,128]{3,2,1,0:T(8,128)(2,1)S(1)}, u32[]{:S(2)}, u32[]{:S(2)}) collective-permute-start(bf16[1,10,16,128]{3,2,1,0:T(8,128)(2,1)S(1)} %pack.1), channel_id=1, source_target_pairs={{0,8},{1,9},{2,10},{3,11},{4,12},{5,13},{6,14},{7,15},{8,0},{9,1},... | collective-permute-start | bytes 122888 | tf_op jit(solution)/shard_map/ppermute | solution.py:678
  5.6 2.5 %collective-permute-start.1 = (bf16[27,8,16]{2,1,0:T(8,128)(2,1)}, bf16[27,8,16]{2,1,0:T(8,128)(2,1)S(1)}, u32[]{:S(2)}, u32[]{:S(2)}) collective-permute-start(bf16[27,8,16]{2,1,0:T(8,128)(2,1)} %bitcast.41), channel_id=1, source_target_pairs={{0,1},{1,0},{2,3},{3,2},{4,5},{5,4},{6,7},{7,6},{8,9},{9,8},{10,11... | collective-permute-start | bytes 20744 | tf_op jit(solution)/shard_map/ppermute | solution.py:678
  5.6 2.4 %collective-permute-start.2 = (bf16[27,2,8]{2,1,0:T(2,128)(2,1)}, bf16[27,2,8]{2,1,0:T(2,128)(2,1)S(1)}, u32[]{:S(2)}, u32[]{:S(2)}) collective-permute-start(bf16[27,2,8]{2,1,0:T(2,128)(2,1)} %bitcast.44), channel_id=1, source_target_pairs={{0,1},{1,0},{2,3},{3,2},{4,5},{5,4},{6,7},{7,6},{8,9},{9,8},{10,11... | collective-permute-start | bytes 2600 | tf_op jit(solution)/shard_map/ppermute | solution.py:678
  6.1 1.9 %collective-permute-start.3 = (bf16[3,3,3,8]{3,2,1,0:T(4,128)(2,1)}, bf16[3,3,3,8]{3,2,1,0:T(4,128)(2,1)S(1)}, u32[]{:S(2)}, u32[]{:S(2)}) collective-permute-start(bf16[3,3,3,8]{3,2,1,0:T(4,128)(2,1)} %bitcast.47), channel_id=1, source_target_pairs={{0,1},{1,0},{2,3},{3,2},{4,5},{5,4},{6,7},{7,6},{8,9},{9,8},{10,11... | collective-permute-start | bytes 1304 | tf_op jit(solution)/shard_map/ppermute | solution.py:678
  8.0 5.1 %collective-permute-start.4 = (bf16[2,10,16,128]{3,2,1,0:T(8,128)(2,1)S(1)}, bf16[2,10,16,128]{3,2,1,0:T(8,128)(2,1)S(1)}, u32[]{:S(2)}, u32[]{:S(2)}) collective-permute-start(bf16[2,10,16,128]{3,2,1,0:T(8,128)(2,1)S(1)} %pad_maximum_fusion), channel_id=1, source_target_pairs={{0,2},{1,3},{2,0},{3,1},{4,6},{5,7},{6,4},{7,5},{8,10},{9,11},{10,... | collective-permute-start | bytes 245768 | tf_op jit(solution)/shard_map/ppermute | solution.py:678
  9.8 4.7 %collective-permute-start.5 = (bf16[2,10,16,128]{3,2,1,0:T(8,128)(2,1)S(1)}, bf16[2,10,16,128]{3,2,1,0:T(8,128)(2,1)S(1)}, u32[]{:S(2)}, u32[]{:S(2)}) collective-permute-start(bf16[2,10,16,128]{3,2,1,0:T(8,128)(2,1)S(1)} %pad_maximum_fusion), channel_id=1, source_target_pairs={{0,4},{1,5},{2,6},{3,7},{4,0},{5,1},{6,2},{7,3},{8,12},{9,13},{10,... | collective-permute-start | bytes 245768 | tf_op jit(solution)/shard_map/ppermute | solution.py:678
  11.1 5.3 %collective-permute-start.6 = (bf16[2,10,16,128]{3,2,1,0:T(8,128)(2,1)S(1)}, bf16[2,10,16,128]{3,2,1,0:T(8,128)(2,1)S(1)}, u32[]{:S(2)}, u32[]{:S(2)}) collective-permute-start(bf16[2,10,16,128]{3,2,1,0:T(8,128)(2,1)S(1)} %pad_maximum_fusion), channel_id=1, source_target_pairs={{0,6},{1,7},{2,4},{3,5},{4,2},{5,3},{6,0},{7,1},{8,14},{9,15},{10,... | collective-permute-start | bytes 245768 | tf_op jit(solution)/shard_map/ppermute | solution.py:678
  16.4 1.7 %collective-permute-start.7 = (bf16[8,10,16,128]{3,2,1,0:T(8,128)(2,1)S(1)}, bf16[8,10,16,128]{3,2,1,0:T(8,128)(2,1)S(1)}, u32[]{:S(2)}, u32[]{:S(2)}) collective-permute-start(bf16[8,10,16,128]{3,2,1,0:T(8,128)(2,1)S(1)} %constant_dynamic-update-slice_fusion.payload), channel_id=1, source_target_pairs={{0,1},{1,0},{2,3},{3,2},{4,5},{5,4},{6,7},{7,6},{8,9},{9,8},{10,11... | collective-permute-start | bytes 983048 | tf_op jit(solution)/shard_map/ppermute | solution.py:678
  33.6 1.3 %collective-permute-start.8 = (f32[112,128]{1,0:T(8,128)S(1)}, f32[112,128]{1,0:T(8,128)S(1)}, u32[]{:S(2)}, u32[]{:S(2)}) collective-permute-start(f32[112,128]{1,0:T(8,128)S(1)} %get-tuple-element.39), channel_id=1, source_target_pairs={{0,1},{1,0},{2,3},{3,2},{4,5},{5,4},{6,7},{7,6},{8,9},{9,8},{10,11... | collective-permute-start | bytes 172040 | tf_op jit(solution)/shard_map/ppermute | solution.py:678
  35.0 4.4 %collective-permute-start.10 = (f32[80,128]{1,0:T(8,128)S(1)}, f32[80,128]{1,0:T(8,128)S(1)}, u32[]{:S(2)}, u32[]{:S(2)}) collective-permute-start(f32[80,128]{1,0:T(8,128)S(1)} %get-tuple-element.61), channel_id=1, source_target_pairs={{0,4},{1,5},{2,6},{3,7},{4,0},{5,1},{6,2},{7,3},{8,12},{9,13},{10,... | collective-permute-start | bytes 122888 | tf_op jit(solution)/shard_map/ppermute | solution.py:678
  35.8 4.9 %collective-permute-start.11 = (f32[80,128]{1,0:T(8,128)S(1)}, f32[80,128]{1,0:T(8,128)S(1)}, u32[]{:S(2)}, u32[]{:S(2)}) collective-permute-start(f32[80,128]{1,0:T(8,128)S(1)} %get-tuple-element.60), channel_id=1, source_target_pairs={{0,6},{1,7},{2,4},{3,5},{4,2},{5,3},{6,0},{7,1},{8,14},{9,15},{10,... | collective-permute-start | bytes 122888 | tf_op jit(solution)/shard_map/ppermute | solution.py:678
  37.0 4.1 %collective-permute-start.9 = (f32[80,128]{1,0:T(8,128)S(1)}, f32[80,128]{1,0:T(8,128)S(1)}, u32[]{:S(2)}, u32[]{:S(2)}) collective-permute-start(f32[80,128]{1,0:T(8,128)S(1)} %get-tuple-element.62), channel_id=1, source_target_pairs={{0,2},{1,3},{2,0},{3,1},{4,6},{5,7},{6,4},{7,5},{8,10},{9,11},{10,... | collective-permute-start | bytes 122888 | tf_op jit(solution)/shard_map/ppermute | solution.py:678

commit v3 on v2

--- a/solution.py
+++ b/solution.py
@@ -25,6 +25,13 @@
     return lax.dot_general(left, right, dims, precision=precision, preferred_element_type=F32)
 
 
+def exact_parts(value):
+    high = value.astype(BF16)
+    rest = value - high.astype(F32)
+    middle = rest.astype(BF16)
+    return high, middle, (rest - middle.astype(F32)).astype(BF16)
+
+
 def iota(shape, dim):
     return lax.broadcasted_iota(jnp.int32, shape, dim)
 
@@ -42,6 +49,10 @@
 
 def in_hbm(value):
     return pltpu.with_memory_space_constraint(value, pltpu.HBM)
+
+
+def own_row():
+    return lax.axis_index("view") * lax.axis_size("slab") + lax.axis_index("slab")
 
 
 def fetch(sources, targets, arrivals):
@@ -54,15 +65,21 @@
     return copies
 
 
-def weights_kernel(chan_ref, middle_from, first_from, last_from,
+def weights_kernel(middle_from, first_from, last_from, footprints_from,
+                   rows_from, blocks_from, mixing_from, readout_from,
                    middle_other, first_other, last_other,
-                   middle, first, last, middle_own, first_own, last_own, arrivals):
+                   middle, first, last, footprints, rows, blocks, mixing, readout,
+                   middle_own, first_own, last_own, arrivals):
     wide = HID * HID
-    for copy in fetch(
-        (middle_from, first_from, last_from), (middle_own, first_own, last_own), arrivals
-    ):
+    copies = fetch(
+        (middle_from, first_from, last_from, footprints_from,
+         rows_from, blocks_from, mixing_from, readout_from),
+        (middle_own, first_own, last_own, footprints, rows, blocks, mixing, readout),
+        arrivals,
+    )
+    for copy in copies[:3]:
         copy.wait()
-    chan = chan_ref[0]
+    chan = lax.axis_index("chan")
     lane_z = iota((HID, wide), 1) >> 4
     row_z = iota((HID, wide), 0)
 
@@ -115,6 +132,8 @@
         dy, dx = (tap // 3, tap % 3)
         rows = [last_lines[depth * 3 + dy][dx : dx + 1] for depth in range(3)]
         last[tap * HID : (tap + 1) * HID, :] = banded(rows, -1)
+    for copy in copies[3:]:
+        copy.wait()
 
 
 def own_weights(conv_first, conv_middle, conv_last):
@@ -125,10 +144,9 @@
     )
 
 
-def build_weights(chan, own, other):
+def build_weights(own, other, passed):
     wide = HID * HID
     hbm = pl.BlockSpec(memory_space=pltpu.HBM)
-    smem = pl.BlockSpec(memory_space=pltpu.SMEM)
     vmem = pl.BlockSpec(memory_space=pltpu.VMEM)
     return pl.pallas_call(
         weights_kernel,
@@ -136,15 +154,16 @@
             jax.ShapeDtypeStruct((3, 3 * wide, wide), BF16),
             jax.ShapeDtypeStruct((2 * TAPS * HID, wide), BF16),
             jax.ShapeDtypeStruct((TAPS * HID, wide), BF16),
+            *(jax.ShapeDtypeStruct(value.shape, value.dtype) for value in passed),
         ),
-        in_specs=[smem] + [hbm] * 3 + [vmem] * 3,
-        out_specs=(vmem, vmem, vmem),
+        in_specs=[hbm] * 8 + [vmem] * 3,
+        out_specs=[vmem] * 8,
         scratch_shapes=[pltpu.VMEM(value.shape, value.dtype) for value in own]
-        + [pltpu.SemaphoreType.DMA((3,))],
+        + [pltpu.SemaphoreType.DMA((8,))],
         compiler_params=pltpu.CompilerParams(vmem_limit_bytes=16 * MIB),
         cost_estimate=pl.CostEstimate(flops=10**8, bytes_accessed=2 * 10**6, transcendentals=0),
         name="band_weights",
-    )(chan, *(in_hbm(value) for value in own), *other)
+    )(*(in_hbm(value) for value in (*own, *passed)), *other)
 
 
 def sigmoid(value):
@@ -188,9 +207,10 @@
     return batch, mixed_of, stack_of
 
 
-def dual_gradients(sizes, table, scalars, footprints, proj, dual, meas, grad_tiles, grad, sums):
+def dual_gradients(sizes, table, scalars, footprints, proj, dual, meas, grad_tiles, grad, sums,
+                   cache=()):
     detectors, width = (sizes[2], sizes[4])
-    own_tile = lax.div(sizes[7][2](table[2][0], table[3][0]) * width, TILE)
+    own_tile = lax.div(sizes[7][2](own_row(), lax.axis_index("chan")) * width, TILE)
     tile_of, _, project = projector(sizes, table, footprints)
     batch, mixed_of, stack_of = dual_reader(scalars, proj, dual, meas)
 
@@ -205,77 +225,99 @@
 
     def dual_sums(chunk):
         span, parts = stack_of(chunk)
-        pulled_in = grad[span]
+        pulled = grad[span]
+        weighted = [pulled * part for part in parts]
         for m in range(HID):
-            mixed = mixed_of(m, parts)
-            gate = sigmoid(mixed)
-            slope = gate * (1.0 + mixed * (1.0 - gate))
-            pulled = pulled_in * slope * scalars[1][m]
-            terms = [pulled_in * (mixed * gate)] + [pulled * part for part in parts]
+            if cache:
+                active, slope = (cache[0][m, span], cache[1][m, span])
+            else:
+                mixed = mixed_of(m, parts)
+                gate = sigmoid(mixed)
+                active = mixed * gate
+                slope = gate * (1.0 + (mixed - active))
+            terms = [pulled * active] + [value * slope for value in weighted]
             for k, term in enumerate(terms):
                 sums[k, m] += jnp.sum(term.reshape(batch * 2, 8, TILE), axis=0)
 
     repeat(detectors // batch, dual_sums)
-    lane_out = iota((HID, TILE), 1)
-    small = jnp.zeros((HID, TILE), F32)
-    for k in range(4):
-        column = jnp.sum(jnp.sum(sums[k], axis=1), axis=1, keepdims=True)
-        small = jnp.where(lane_out == k, column, small)
-    filled = jnp.concatenate([small, jnp.zeros((TILE - HID, TILE), F32)], axis=0)
-    return jnp.transpose(filled)[0:8]
-
-
-def dual_gradients_kernel(sizes, rows_ref, blocks_ref, mixing, readout, row_ref, chan_ref,
+
+    eight = 4 * HID * 8
+    ones = jnp.ones((TILE, TILE), BF16)
+    lines = sum(dot(part, ones) for part in exact_parts(sums[...].reshape(eight, TILE)))
+    lane = iota((8, TILE), 1)
+    out = jnp.zeros((8, TILE), F32)
+    for k in range(4 * HID):
+        out = jnp.where(lane == k, lines[8 * k : 8 * k + 8], out)
+    return out
+
+
+def dual_gradients_kernel(sizes, rows_ref, blocks_ref, mixing, readout,
                           footprints, proj, dual, meas, grad_tiles, out, grad, sums):
-    table = (rows_ref, blocks_ref, row_ref, chan_ref)
+    table = (rows_ref, blocks_ref)
     out[...] = dual_gradients(
         sizes, table, (mixing, readout), footprints, proj, dual, meas, grad_tiles, grad, sums
     )
 
 
-def pack_kernel(chan_ref, volume_from, cotangent_from, dual_from, measured_from, out,
-                volume, cotangent, dual, measured, arrivals):
+def pack_kernel(routed, volume_from, cotangent_from, dual_from, measured_from,
+                out, volume, cotangent, dual, measured, arrivals):
     copies = fetch(
         (volume_from, cotangent_from, dual_from, measured_from),
         (volume, cotangent, dual, measured),
         arrivals,
     )
-    chan = chan_ref[0]
-    blocks = volume.shape[1] // (2 * TILE)
-
-    def block(rows, k):
-        begin = 2 * k * TILE
-        pair = [rows[:, begin : begin + TILE], rows[:, begin + TILE : begin + 2 * TILE]]
-        return jnp.concatenate(pair, axis=0).astype(BF16)
+    chan = lax.axis_index("chan")
+    row = own_row()
+    tiles = volume.shape[1] // TILE
+    near = tiles // 2
+
+    def pair(value):
+        return jnp.concatenate([value[:, :TILE], value[:, TILE:]], axis=0).astype(BF16)
+
+    def tile_at(source, index):
+        return source[:, pl.ds(pl.multiple_of(index * TILE, TILE), TILE)]
 
     for copy in copies:
         copy.wait()
-    for index, source in enumerate((volume, cotangent)):
-        value = source[...].astype(F32)
-        half = jnp.where(chan == 0, value[:8], value[8:])
-        for k in range(blocks):
-            out[0, index * blocks + k] = block(half, k)
-    out[0, 2 * blocks] = block(dual[...].astype(F32), 0)
-    out[0, 2 * blocks + 1] = block(measured[...].astype(F32), 0)
+    for k in range(near):
+        out[0, k] = tile_at(volume, chan * near + k)
+    out[0, near] = pair(dual[...].astype(F32))
+    out[0, near + 1] = pair(measured[...].astype(F32))
+    if not routed:
+        for k in range(near):
+            out[0, near + 2 + k] = tile_at(cotangent, chan * near + k)
+        return
+    lane = iota((16, TILE), 1)
+    beside = jnp.zeros((16, TILE), F32)
+    for k in range(4):
+        out[0, near + 2 + k] = tile_at(cotangent, (((row & 3) ^ k) << 1) + chan)
+        lower = tile_at(cotangent, jnp.maximum(2 * k + chan - 1, 0)).astype(F32)
+        upper = tile_at(cotangent, jnp.minimum(2 * k + chan + 1, tiles - 1)).astype(F32)
+        spot = jnp.where(lane >= TILE // 2, lower, upper)
+        spot = spot if k == 0 else pltpu.roll(spot, 32 * k, 1)
+        first = (32 * k - REACH) % TILE
+        mine = (lane >= 32 * k) & (lane < 32 * k + REACH) | (lane >= first) & (lane < first + REACH)
+        beside = jnp.where(mine, spot, beside)
+    out[0, near + 6] = beside.astype(BF16)
 
 
 def main_kernel(sizes, whole, rows_from, blocks_from, mixing_from, readout_from,
-                footprints_from, row_ref, chan_ref, payload, payload_other, middle, first, last,
+                payload, payload_other, routed, middle, first, last, footprints,
                 keep, send, dual_out, proj, dual, meas, grad_tiles,
                 vol, dual_half, dual_new, back, field, col_in, col_cot,
                 act_wide, grad_wide, slope_first, slope_middle, row_tiles, sums,
-                rows_ref, blocks_ref, mixing, readout, footprints, arrivals):
+                rows_ref, blocks_ref, mixing, readout, arrivals, *cache):
     rows_count, chans, detectors, tiles, width, stride, cells, places, updates, _ = sizes
     piece_slot, update_row, chunk_of, flip_of = places
     copies = fetch(
-        (rows_from, blocks_from, mixing_from, readout_from, footprints_from),
-        (rows_ref, blocks_ref, mixing, readout, footprints),
+        (rows_from, blocks_from, mixing_from, readout_from),
+        (rows_ref, blocks_ref, mixing, readout),
         arrivals,
     )
-    table = (rows_ref, blocks_ref, row_ref, chan_ref)
+    table = (rows_ref, blocks_ref)
     scalars = (mixing, readout)
-    row = row_ref[0]
-    chan = chan_ref[0]
+    row = own_row()
+    chan = lax.axis_index("chan")
     low = chunk_of(row, chan) * width
     count = rows_count * stride
     pad = -(-(stride + 1) // TILE) * TILE
@@ -283,25 +325,28 @@
 
     flip = flip_of(chan)
 
-    def halves_of(owner, k):
+    near = tiles // 2
+
+    def place(owner):
         slot = piece_slot(owner, row)
-        mine = payload[slot, k].astype(F32)
-        theirs = payload_other[slot, k].astype(F32)
-        return jnp.where(flip == 0, mine, theirs), jnp.where(flip == 0, theirs, mine)
-
-    def place(owner):
-        for k in range(tiles // 2):
-            halves = halves_of(owner, k)
-            for t in range(2):
-                whole_tile = jnp.concatenate([h[t * 8 : (t + 1) * 8] for h in halves], axis=0)
-                vol[owner * tiles + 2 * k + t] = whole_tile.astype(BF16)
-        for k, target in ((tiles, dual), (tiles + 1, meas)):
-            halves = halves_of(owner, k)
-            for t in range(2):
-                for part in range(2):
-                    target[owner * 2 + t, part * 8 : (part + 1) * 8, :] = halves[part][
-                        t * 8 : (t + 1) * 8
-                    ]
+        for source, part in ((payload, flip), (payload_other, 1 - flip)):
+            for k in range(near):
+                vol[owner * tiles + part * near + k] = source[slot, k]
+            span = pl.ds(pl.multiple_of(part * 8, 8), 8)
+            for k, target in ((near, dual), (near + 1, meas)):
+                piece = source[slot, k].astype(F32)
+                for t in range(2):
+                    target[owner * 2 + t, span, :] = piece[t * 8 : (t + 1) * 8]
+
+    def cotangent_tile(owner, side, tile):
+        slot = piece_slot(owner, row)
+        if not whole:
+            pair = [source[slot, near + 2 + (tile & (near - 1))] for source in (payload, payload_other)]
+            return jnp.where(tile < near, pair[0].astype(F32), pair[1].astype(F32))
+        begin = (slot >> 1) * 4 + (slot & 1)
+        if side == 1:
+            return routed[begin].astype(F32)
+        return pltpu.roll(routed[begin + 2].astype(F32), (TILE - 32 * (row & 3)) & (TILE - 1), 1)
 
     repeat(rows_count, place)
 
@@ -321,7 +366,12 @@
         total = parts[0]
         for m in range(HID):
             mixed = mixed_of(m, parts)
-            total = total + scalars[1][m] * (mixed * sigmoid(mixed))
+            gate = sigmoid(mixed)
+            active = mixed * gate
+            total = total + scalars[1][m] * active
+            if whole:
+                cache[0][m, span] = active
+                cache[1][m, span] = gate * (1.0 + (mixed - active))
         dual_new[span] = total
         dual_half[span] = total.astype(BF16)
 
@@ -369,14 +419,11 @@
     for y in range(rows_count):
         moved = []
         for side in range(sides):
-            halves = halves_of(y, tiles // 2 + (clipped[side] >> 1))
-            odd = (clipped[side] & 1) == 1
             merged = jnp.concatenate(
                 [
                     vol[y * tiles + clipped[side]].astype(F32),
                     back[y, side].astype(BF16).astype(F32),
-                    jnp.where(odd, halves[0][8:], halves[0][:8]),
-                    jnp.where(odd, halves[1][8:], halves[1][:8]),
+                    cotangent_tile(y, side, clipped[side]),
                 ],
                 axis=0,
             )
@@ -435,7 +482,7 @@
 
     first_pre = dot(col_in[...], first[...], TN)
     gate = sigmoid(first_pre)
-    slope_first[...] = gate * (1.0 + first_pre * (1.0 - gate))
+    slope_first[...] = gate * (1.0 + (first_pre - first_pre * gate))
     widen(act_wide, masked(valid, first_pre * gate), 1)
     middle_pre = None
     for dy in range(3):
@@ -447,7 +494,7 @@
             )
             middle_pre = part if middle_pre is None else middle_pre + part
     gate = sigmoid(middle_pre)
-    slope_middle[...] = gate * (1.0 + middle_pre * (1.0 - gate))
+    slope_middle[...] = gate * (1.0 + (middle_pre - middle_pre * gate))
     middle_act = masked(valid, middle_pre * gate)
     middle_half = middle_act.astype(BF16)
 
@@ -509,8 +556,7 @@
     lane_group = iota((HID, TILE), 1) >> 4
     out_tiles = [jnp.zeros((HID, TILE), F32) for _ in range(4)]
 
-    def fold_lanes(value):
-        value = value[:, :TILE] + value[:, TILE:]
+    def fold_groups(value):
         for amount in (64, 32, 16):
             value = value + pltpu.roll(value, amount, 1)
         return value
@@ -522,10 +568,13 @@
     for tap in range(TAPS):
         plane = grads_middle[tap // 3][:, (tap % 3) * wide : (tap % 3 + 1) * wide]
         for depth in range(3):
-            total = jnp.zeros((HID, wide), F32)
-            for z in range(HID):
-                total = total + jnp.where(lane_z == z + depth - 1, plane[z * HID : (z + 1) * HID], 0.0)
-            put(depth * TAPS + tap, fold_lanes(total))
+            total = jnp.zeros((HID, TILE), F32)
+            for z in range(max(0, 1 - depth), min(HID, HID + 1 - depth)):
+                other = z + depth - 1
+                half = other // 8
+                block = plane[z * HID : (z + 1) * HID, half * TILE : (half + 1) * TILE]
+                total = total + jnp.where(lane_group == other % 8, block, 0.0)
+            put(depth * TAPS + tap, fold_groups(total))
 
     lane_in = iota((HID, 2 * TAPS * HID), 1) & (HID - 1)
     folds = []
@@ -535,12 +584,14 @@
             total = total + jnp.where(lane_in == z + depth - 1, grad_first[z * HID : (z + 1) * HID], 0.0)
         folds.append(total)
     source = iota((2 * TAPS * HID, TILE), 0) >> 4
-    target = iota((2 * TAPS * HID, TILE), 1)
+    channel = (source >= TAPS).astype(jnp.int32)
+    fold = ((source - TAPS * channel) * 2 + channel == iota((2 * TAPS * HID, TILE), 1)).astype(BF16)
+    folded = sum(dot(part, fold) for part in exact_parts(jnp.concatenate(folds, axis=0)))
     for depth in range(3):
-        channel = (source >= TAPS).astype(jnp.int32)
-        fold = (target == 48 + (depth * TAPS + source - TAPS * channel) * 2 + channel).astype(F32)
-        out_tiles[3] = out_tiles[3] + dot(folds[depth], fold, precision=lax.Precision.HIGHEST)
-
+        block = folded[depth * HID : (depth + 1) * HID]
+        out_tiles[3] = out_tiles[3] + pltpu.roll(block, 48 + depth * 2 * TAPS, 1)
+
+    lane_z = iota((HID, wide), 1) >> 4
     row_z = iota((HID, wide), 0)
     lines = []
     for depth in range(3):
@@ -549,7 +600,8 @@
             part = jnp.where(keep_last, grad_last[tap * HID : (tap + 1) * HID], 0.0)
             lines.append(jnp.sum(part, axis=0, keepdims=True))
     lines.append(jnp.zeros((32 - 27, wide), F32))
-    lines = fold_lanes(jnp.concatenate(lines, axis=0))
+    lines = jnp.concatenate(lines, axis=0)
+    lines = fold_groups(lines[:, :TILE] + lines[:, TILE:])
     row_eight = iota((8, TILE), 0)
     packed_last = jnp.zeros((8, TILE), F32)
     for r in range(4):
@@ -560,7 +612,7 @@
 
     if whole:
         small = dual_gradients(
-            sizes, table, scalars, footprints, proj, dual, meas, grad_tiles, dual_new, sums
+            sizes, table, scalars, footprints, proj, dual, meas, grad_tiles, dual_new, sums, cache
         )
     else:
         small = jnp.zeros((8, TILE), F32)
@@ -584,7 +636,7 @@
     repeat(updates, put_update)
 
 
-def write_grads(chan, grads, middle, first, last, mixing, readout):
+def write_grads(chan, grads, scale, middle, first, last, mixing, readout):
     for k in range(27):
         block = grads[(k // 8) * 8 : (k // 8 + 1) * 8]
         block = block if k % 8 == 0 else pltpu.roll(block, TILE - 16 * (k % 8), 1)
@@ -599,16 +651,19 @@
         for r in range(4):
             if r * 8 + group < 27:
                 last[r * 8 + group] = moved[r : r + 1, :8]
-    mixing[...] = grads[41:44, :HID]
-    readout[...] = grads[40:41, :HID]
-
-
-def finish_kernel(row_ref, chan_ref, keep, near, one, two, three, volume, *rest):
+    small = jnp.broadcast_to(jnp.sum(grads[40:48], axis=0, keepdims=True), (8, TILE))
+    readout[...] = small[0:1, :HID]
+    for k in range(3):
+        moved = pltpu.roll(small, TILE - HID * (k + 1), 1)
+        mixing[k : k + 1, :] = moved[0:1, :HID] * scale[0:1, :HID]
+
+
+def finish_kernel(scale, keep, near, one, two, three, volume, *rest):
     grads, slots = (rest[:-1], rest[-1])
-    row = row_ref[0]
-    chan = chan_ref[0]
+    row = own_row()
+    chan = lax.axis_index("chan")
     total = keep[0:48, :] + near[0:48, :] + one[0:48, :] + two[0:48, :] + three[0:48, :]
-    write_grads(chan, total, *grads)
+    write_grads(chan, total, scale, *grads)
     for k, (source, begin) in enumerate(
         ((keep, 48), (near, 48), (one, 48), (one, 64), (two, 48), (two, 64), (three, 48), (three, 64))
     ):
@@ -617,8 +672,8 @@
         volume[:, tile, :] = slots[(((tile >> 1) ^ (row & 3)) << 1) + ((tile & 1) ^ chan)]
 
 
-def finish_grads_kernel(chan_ref, total, *grads):
-    write_grads(chan_ref[0], total[...], *grads)
+def finish_grads_kernel(scale, total, *grads):
+    write_grads(lax.axis_index("chan"), total[...], scale[...], *grads)
 
 
 def row_mask_pairs(devices, mask):
@@ -649,11 +704,7 @@
     width = cells * copies // devices
     stride = -(-(width + 2 * REACH) // 16) * 16
     detectors = tile_rows.shape[0] * tile_rows.shape[1]
-    chan = lax.axis_index("chan")
-    row = lax.axis_index("view") * slabs + lax.axis_index("slab")
-
-    row_one = row.reshape(1).astype(jnp.int32)
-    chan_one = chan.reshape(1).astype(jnp.int32)
+
     vmem = pl.BlockSpec(memory_space=pltpu.VMEM)
     smem = pl.BlockSpec(memory_space=pltpu.SMEM)
     hbm = pl.BlockSpec(memory_space=pltpu.HBM)
@@ -664,36 +715,57 @@
         measured.reshape(8, 2 * TILE),
     )
     payload = pl.pallas_call(
-        pack_kernel,
-        out_shape=jax.ShapeDtypeStruct((1, tiles + 2, 16, TILE), BF16),
-        in_specs=[smem] + [hbm] * 4,
+        functools.partial(pack_kernel, quick),
+        out_shape=jax.ShapeDtypeStruct((1, tiles // 2 + 2 + (5 if quick else tiles // 2), 16, TILE), BF16),
+        in_specs=[hbm] * 4,
         out_specs=vmem,
         scratch_shapes=[pltpu.VMEM(value.shape, value.dtype) for value in raw]
         + [pltpu.SemaphoreType.DMA((4,))],
         compiler_params=pltpu.CompilerParams(vmem_limit_bytes=4 * MIB),
         name="pack",
-    )(chan_one, *(in_hbm(value) for value in raw))
+    )(*(in_hbm(value) for value in raw))
 
     def swap(value, mask):
         return lax.ppermute(value, ALL_AXES, row_mask_pairs(devices, mask))
 
+    table = (
+        jnp.swapaxes(tile_rows, 2, 3),
+        jnp.swapaxes(tile_blocks, 2, 3),
+        dual_mixing.T,
+        dual_readout,
+    )
     own = own_weights(conv_first, conv_middle, conv_last)
     if quick:
         far_payload = swap(payload, 8)
         other = tuple(swap(value, 1) for value in own)
-        payload = jnp.concatenate([payload, far_payload], axis=0)
-        payload, other = lax.optimization_barrier((payload, other))
-        pieces = [swap(payload, k) for k in (2, 4, 6)]
-        weights = build_weights(chan_one, own, other)
+        payload, far_payload, other = lax.optimization_barrier((payload, far_payload, other))
+
+        def bound_for(k):
+            sources = (payload[0], far_payload[0])
+            return jnp.concatenate(
+                [source[:6] for source in sources]
+                + [source[6 + k : 7 + k] for source in sources]
+                + [source[10:] for source in sources],
+                axis=0,
+            )
+
+        pieces = [swap(bound_for(k), 2 * k) for k in (1, 2, 3)]
+        weights = build_weights(own, other, (footprints, *table))
         pieces[0], weights = lax.optimization_barrier((pieces[0], weights))
-        payload = jnp.concatenate([payload] + pieces, axis=0)
+        pieces = [bound_for(0)] + pieces
+        payload = jnp.concatenate([piece[:12] for piece in pieces], axis=0)
+        payload = payload.reshape(rows_count, 6, 16, TILE)
+        routed = jnp.concatenate([piece[12:] for piece in pieces], axis=0)
         payload_other = swap(payload, 1)
     else:
         payload = lax.all_gather(payload, ALL_AXES, axis=0, tiled=True)
         payload = payload.reshape(rows_count, chans, *payload.shape[1:])
         payload, payload_other = (payload[:, 0], payload[:, 1])
-        weights = build_weights(chan_one, own, tuple(swap(value, 1) for value in own))
-    middle, first, last = weights
+        routed = payload[0, :1]
+        weights = build_weights(
+            own, tuple(swap(value, 1) for value in own), (footprints, *table)
+        )
+    middle, first, last, footprints, *table = weights
 
     def piece_slot(owner, row):
         if not quick:
@@ -711,17 +783,11 @@
         return chan if quick else 0
 
     updates = 4 if quick else rows_count
-    table = (
-        jnp.swapaxes(tile_rows, 2, 3),
-        jnp.swapaxes(tile_blocks, 2, 3),
-        dual_mixing.T,
-        dual_readout,
-    )
     count = rows_count * stride
     wide = HID * HID
     moved = 48 + 16 * updates
     pad = -(-(stride + 1) // TILE) * TILE
-    limit = (20 if quick else 56) * MIB
+    limit = (24 if quick else 56) * MIB
     sizes = (rows_count, chans, detectors, tiles, width, stride, cells,
              (piece_slot, update_row, chunk_of, flip_of), updates,
              tile_rows.shape[1])
@@ -758,28 +824,30 @@
     keep, send, new_dual, *rest = pl.pallas_call(
         functools.partial(main_kernel, sizes, quick),
         out_shape=[jax.ShapeDtypeStruct(*spec) for spec in outs],
-        in_specs=[hbm] * 5 + [smem] * 2 + [vmem] * 5,
+        in_specs=[vmem] * 11,
         out_specs=[vmem] * len(outs),
         scratch_shapes=[pltpu.VMEM(*spec) for spec in scratch]
         + [pltpu.SMEM(value.shape, value.dtype) for value in table]
-        + [pltpu.VMEM(footprints.shape, BF16), pltpu.SemaphoreType.DMA((5,))],
+        + [pltpu.SemaphoreType.DMA((4,))]
+        + [pltpu.VMEM((HID, detectors, 16, TILE), F32) for _ in range(2 if quick else 0)],
         compiler_params=pltpu.CompilerParams(vmem_limit_bytes=limit),
         cost_estimate=pl.CostEstimate(
             flops=5 * 10**9, bytes_accessed=5 * 10**6, transcendentals=2 * 10**6
         ),
         name="primal_dual",
     )(
-        *(in_hbm(value) for value in (*table, footprints)),
-        row_one,
-        chan_one,
+        *table,
         payload,
         payload_other,
+        routed,
         middle,
         first,
         last,
+        footprints,
     )
 
     near = swap(send, 1)
+    scale = dual_readout.reshape(1, HID)
     grad_shapes = [
         jax.ShapeDtypeStruct(shape, F32)
         for shape in ((27, 8, HID), (27, 2, 8), (27, 1, 8), (3, HID), (1, HID))
@@ -798,18 +866,18 @@
         new_volume, *grads = pl.pallas_call(
             finish_kernel,
             out_shape=[jax.ShapeDtypeStruct((16, 8, TILE), F32)] + grad_shapes,
-            in_specs=[smem, smem] + [vmem] * 5,
+            in_specs=[vmem] * 6,
             out_specs=[vmem] * 6,
             scratch_shapes=[pltpu.VMEM((8, 16, TILE), F32)],
             compiler_params=pltpu.CompilerParams(vmem_limit_bytes=8 * MIB),
             name="finish",
-        )(row_one, chan_one, keep, near, *parts)
+        )(scale, keep, near, *parts)
     else:
         mine = keep + near
         small = pl.pallas_call(
             functools.partial(dual_gradients_kernel, sizes),
             out_shape=jax.ShapeDtypeStruct((8, TILE), F32),
-            in_specs=[smem] * 6 + [vmem] * 5,
+            in_specs=[smem] * 4 + [vmem] * 5,
             out_specs=vmem,
             scratch_shapes=[
                 pltpu.VMEM((detectors, 16, TILE), F32),
@@ -817,17 +885,17 @@
             ],
             compiler_params=pltpu.CompilerParams(vmem_limit_bytes=limit),
             name="dual_gradients",
-        )(*table, row_one, chan_one, footprints, *rest)
+        )(*table, footprints, *rest)
         total = jnp.concatenate(
             [lax.psum(mine[:40], ROW_AXES), lax.psum(small, ALL_AXES)], axis=0
         )
         grads = pl.pallas_call(
             finish_grads_kernel,
             out_shape=grad_shapes,
-            in_specs=[smem, vmem],
+            in_specs=[vmem, vmem],
             out_specs=[vmem] * 5,
             name="finish_grads",
-        )(chan_one, total)
+        )(scale, total)
         pieces = lax.all_to_all(
             mine[48:].reshape(rows_count, 16, TILE), ROW_AXES, 0, 0, tiled=True
         )

time: 42.2 us -> 40.4 us (0.957)
  Pallas kernels: 18.7 us -> 17.5 us
  waiting for transfers between devices: 10.4 us -> 9.79 us
    pallas_call x1, Pallas kernels: 15.5 us -> 14 us  [body(): pl.pallas_call(functools.partial(main_kernel, sizes, quick), out_shape=[j...]
    ppermute x12, waiting for transfers between devices: 10.4 us -> 9.79 us  [swap(): return lax.ppermute(value, ALL_AXES, row_mask_pairs(devices, mask))]
where the time goes in v3:
time: 40.4 us; the launch traced here: 40.2 us
  Pallas kernels  17.5 us (43%)
  starting transfers between devices  12 us (30%)
  waiting for transfers between devices  9.79 us (24%)
  between operations  0.77 us (2%)
    pallas_call x1, Pallas kernels, body(): pl.pallas_call(functools.partial(main_kernel, sizes, quick), out_shape=[j...  14 us
    ppermute x12, starting transfers between devices, swap(): return lax.ppermute(value, ALL_AXES, row_mask_pairs(devices, mask))  12 us
    ppermute x12, waiting for transfers between devices, swap(): return lax.ppermute(value, ALL_AXES, row_mask_pairs(devices, mask))  9.79 us
    pallas_call x1, Pallas kernels, build_weights(): pl.pallas_call(weights_kernel, out_shape=(jax.ShapeDtypeStruct((3, 3 * wi...  1.73 us
    pallas_call x1, Pallas kernels, body(): pl.pallas_call(functools.partial(pack_kernel, quick), out_shape=jax.Shape...  0.91 us
    pallas_call x1, Pallas kernels, body(): pl.pallas_call(finish_kernel, out_shape=[jax.ShapeDtypeStruct((16, 8, TIL...  0.82 us
  transfers between devices with their start and end apart: 12, of which 8 were waited for; matrix products, arithmetic and copies ran while one was open for 0% of the time, Pallas kernels for 4%

profile of v3, /device:TPU:0, one launch (start us, length us, event | category | flops | bytes accessed | tf_op | source)
XLA Modules:
  0.0 40.2 jit_solution(15565740110266422415)
XLA Ops:
  0.6 0.9 %pack.1 = bf16[1,11,16,128]{3,2,1,0:T(8,128)(2,1)S(1)} custom-call(bf16[16,1024]{1,0:T(8,128)(2,1)} %bitcast.76, bf16[16,1024]{1,0:T(8,128)(2,1)} %bitcast.77, bf16[8,256]{1,0:T(8,128)(2,1)} %bitcast.84, bf16[8,256]{1,0:T(8,128)(2,1)} %bitcast.85), custom_call_target="tpu_custom_call" | custom-call | tf_op jit(solution)/shard_map/pack/pallas_call | solution.py:717
  1.5 4.1 %collective-permute-start = (bf16[1,11,16,128]{3,2,1,0:T(8,128)(2,1)S(1)}, bf16[1,11,16,128]{3,2,1,0:T(8,128)(2,1)S(1)}, u32[]{:S(2)}, u32[]{:S(2)}) collective-permute-start(bf16[1,11,16,128]{3,2,1,0:T(8,128)(2,1)S(1)} %pack.1), channel_id=1, source_target_pairs={{0,8},{1,9},{2,10},{3,11},{4,12},{5,13},{6,14},{7,15},{8,0},{9,1},... | collective-permute-start | bytes 135176 | tf_op jit(solution)/shard_map/ppermute | solution.py:729
  5.7 0.5 %collective-permute-start.2 = (bf16[27,2,8]{2,1,0:T(2,128)(2,1)}, bf16[27,2,8]{2,1,0:T(2,128)(2,1)S(1)}, u32[]{:S(2)}, u32[]{:S(2)}) collective-permute-start(bf16[27,2,8]{2,1,0:T(2,128)(2,1)} %bitcast.78), channel_id=1, source_target_pairs={{0,1},{1,0},{2,3},{3,2},{4,5},{5,4},{6,7},{7,6},{8,9},{9,8},{10,11... | collective-permute-start | bytes 2600 | tf_op jit(solution)/shard_map/ppermute | solution.py:729
  6.2 1.4 %collective-permute-done.3.last_other = bf16[3,3,3,8]{3,2,1,0:T(4,128)(2,1)S(1)} collective-permute-done((bf16[3,3,3,8]{3,2,1,0:T(4,128)(2,1)}, bf16[3,3,3,8]{3,2,1,0:T(4,128)(2,1)S(1)}, u32[]{:S(2)}, u32[]{:S(2)}) %collective-permute-start.3) | collective-permute-done | bytes 464 | tf_op jit(solution)/shard_map/ppermute | solution.py:729
  7.6 0.6 %collective-permute-done = bf16[1,11,16,128]{3,2,1,0:T(8,128)(2,1)S(1)} collective-permute-done((bf16[1,11,16,128]{3,2,1,0:T(8,128)(2,1)S(1)}, bf16[1,11,16,128]{3,2,1,0:T(8,128)(2,1)S(1)}, u32[]{:S(2)}, u32[]{:S(2)}) %collective-permute-start) | collective-permute-done | bytes 45088 | tf_op jit(solution)/shard_map/ppermute | solution.py:729
  8.3 1.8 %collective-permute-start.4 = (bf16[16,16,128]{2,1,0:T(8,128)(2,1)S(1)}, bf16[16,16,128]{2,1,0:T(8,128)(2,1)S(1)}, u32[]{:S(2)}, u32[]{:S(2)}) collective-permute-start(bf16[16,16,128]{2,1,0:T(8,128)(2,1)S(1)} %get-tuple-element.85), channel_id=1, source_target_pairs={{0,2},{1,3},{2,0},{3,1},{4,6},{5,7},{6,4},{7,5},{8,10},{9,11},{10,... | collective-permute-start | bytes 196616 | tf_op jit(solution)/shard_map/ppermute | solution.py:729
  10.1 1.2 %collective-permute-start.5 = (bf16[16,16,128]{2,1,0:T(8,128)(2,1)S(1)}, bf16[16,16,128]{2,1,0:T(8,128)(2,1)S(1)}, u32[]{:S(2)}, u32[]{:S(2)}) collective-permute-start(bf16[16,16,128]{2,1,0:T(8,128)(2,1)S(1)} %get-tuple-element.83), channel_id=1, source_target_pairs={{0,4},{1,5},{2,6},{3,7},{4,0},{5,1},{6,2},{7,3},{8,12},{9,13},{10,... | collective-permute-start | bytes 196616 | tf_op jit(solution)/shard_map/ppermute | solution.py:729
  11.3 0.6 %collective-permute-start.6 = (bf16[16,16,128]{2,1,0:T(8,128)(2,1)S(1)}, bf16[16,16,128]{2,1,0:T(8,128)(2,1)S(1)}, u32[]{:S(2)}, u32[]{:S(2)}) collective-permute-start(bf16[16,16,128]{2,1,0:T(8,128)(2,1)S(1)} %get-tuple-element.84), channel_id=1, source_target_pairs={{0,6},{1,7},{2,4},{3,5},{4,2},{5,3},{6,0},{7,1},{8,14},{9,15},{10,... | collective-permute-start | bytes 196616 | tf_op jit(solution)/shard_map/ppermute | solution.py:729
  11.9 1.7 %band_weights.1 = (bf16[3,768,256]{2,1,0:T(8,128)(2,1)S(1)}, bf16[288,256]{1,0:T(8,128)(2,1)S(1)}, bf16[144,256]{1,0:T(8,128)(2,1)S(1)}, bf16[64,128,128]{2,1,0:...) custom-call(bf16[27,8,16]{2,1,0:T(8,128)(2,1)} %bitcast.75, ...), custom_call_target="tpu_custom_call" | custom-call | flops 100000000 | bytes 2000000 | tf_op jit(solution)/shard_map/band_weights/pallas_call | solution.py:151
  13.6 0.0 collective-permute-done.4
  13.6 0.8 %collective-permute-done.5 = bf16[16,16,128]{2,1,0:T(8,128)(2,1)S(1)} collective-permute-done((bf16[16,16,128]{2,1,0:T(8,128)(2,1)S(1)}, bf16[16,16,128]{2,1,0:T(8,128)(2,1)S(1)}, u32[]{:S(2)}, u32[]{:S(2)}) %collective-permute-start.5) | collective-permute-done | bytes 65568 | tf_op jit(solution)/shard_map/ppermute | solution.py:729
  14.4 2.0 %collective-permute-done.6 = bf16[16,16,128]{2,1,0:T(8,128)(2,1)S(1)} collective-permute-done((bf16[16,16,128]{2,1,0:T(8,128)(2,1)S(1)}, bf16[16,16,128]{2,1,0:T(8,128)(2,1)S(1)}, u32[]{:S(2)}, u32[]{:S(2)}) %collective-permute-start.6) | collective-permute-done | bytes 65568 | tf_op jit(solution)/shard_map/ppermute | solution.py:729
  16.5 0.1 collective-permute-start.7
  16.6 0.0 copy-start
  16.6 1.4 %collective-permute-done.7.payload_other = bf16[8,6,16,128]{3,2,1,0:T(8,128)(2,1)S(1)} collective-permute-done((bf16[8,6,16,128]{3,2,1,0:T(8,128)(2,1)S(1)}, bf16[8,6,16,128]{3,2,1,0:T(8,128)(2,1)S(1)}, u32[]{:S(2)}, u32[]{:S(2)}) %collective-permute-start.7) | collective-permute-done | bytes 196640 | tf_op jit(solution)/shard_map/ppermute | solution.py:729
  18.0 14.0 %primal_dual.1 = (f32[112,128]{1,0:T(8,128)S(1)}, f32[112,128]{1,0:T(8,128)S(1)}, f32[8,256]{1,0:T(8,128)}) custom-call(s32[4,4,1,8]{3,2,1,0:T(1,128)S(1)} %get-tuple-element.51.rows_from, s32[4,4,1,8]{3,2,1,0:T(1,128)S(1)} %get-tuple-element.52.blocks_from, f32[3,16]{1,0:T(4,128)S(1)} %get-tuple-element.53.mixing_from, ...), custom_call_target="tpu_custom_call" | custom-call | flops 5000000000 | bytes 5000000 | tf_op jit(solution)/shard_map/primal_dual/pallas_call | solution.py:824
  32.0 0.2 collective-permute-start.8
  32.2 1.1 %collective-permute-done.8.near = f32[112,128]{1,0:T(8,128)S(1)} collective-permute-done((f32[112,128]{1,0:T(8,128)S(1)}, f32[112,128]{1,0:T(8,128)S(1)}, u32[]{:S(2)}, u32[]{:S(2)}) %collective-permute-start.8) | collective-permute-done | bytes 57376 | tf_op jit(solution)/shard_map/ppermute | solution.py:729
  33.3 0.8 %collective-permute-start.11 = (f32[80,128]{1,0:T(8,128)S(1)}, f32[80,128]{1,0:T(8,128)S(1)}, u32[]{:S(2)}, u32[]{:S(2)}) collective-permute-start(f32[80,128]{1,0:T(8,128)S(1)} %get-tuple-element.100), channel_id=1, source_target_pairs={{0,6},{1,7},{2,4},{3,5},{4,2},{5,3},{6,0},{7,1},{8,14},{9,15},{10,... | collective-permute-start | bytes 122888 | tf_op jit(solution)/shard_map/ppermute | solution.py:729
  34.1 1.3 %collective-permute-start.10 = (f32[80,128]{1,0:T(8,128)S(1)}, f32[80,128]{1,0:T(8,128)S(1)}, u32[]{:S(2)}, u32[]{:S(2)}) collective-permute-start(f32[80,128]{1,0:T(8,128)S(1)} %get-tuple-element.101), channel_id=1, source_target_pairs={{0,4},{1,5},{2,6},{3,7},{4,0},{5,1},{6,2},{7,3},{8,12},{9,13},{10,... | collective-permute-start | bytes 122888 | tf_op jit(solution)/shard_map/ppermute | solution.py:729
  35.4 1.5 %collective-permute-start.9 = (f32[80,128]{1,0:T(8,128)S(1)}, f32[80,128]{1,0:T(8,128)S(1)}, u32[]{:S(2)}, u32[]{:S(2)}) collective-permute-start(f32[80,128]{1,0:T(8,128)S(1)} %get-tuple-element.102), channel_id=1, source_target_pairs={{0,2},{1,3},{2,0},{3,1},{4,6},{5,7},{6,4},{7,5},{8,10},{9,11},{10,... | collective-permute-start | bytes 122888 | tf_op jit(solution)/shard_map/ppermute | solution.py:729
  36.9 1.6 %collective-permute-done.11.three = f32[80,128]{1,0:T(8,128)S(1)} collective-permute-done((f32[80,128]{1,0:T(8,128)S(1)}, f32[80,128]{1,0:T(8,128)S(1)}, u32[]{:S(2)}, u32[]{:S(2)}) %collective-permute-start.11) | collective-permute-done | bytes 40992 | tf_op jit(solution)/shard_map/ppermute | solution.py:729
  38.4 0.9 %collective-permute-done.9.one = f32[80,128]{1,0:T(8,128)S(1)} collective-permute-done((f32[80,128]{1,0:T(8,128)S(1)}, f32[80,128]{1,0:T(8,128)S(1)}, u32[]{:S(2)}, u32[]{:S(2)}) %collective-permute-start.9) | collective-permute-done | bytes 40992 | tf_op jit(solution)/shard_map/ppermute | solution.py:729
  39.4 0.8 %finish.1 = (f32[16,8,128]{2,1,0:T(8,128)}, f32[27,8,16]{2,1,0:T(8,128)}, f32[27,2,8]{2,1,0:T(2,128)}, f32[27,1,8]{2,1,0:T(1,128)}, f32[3,16]{1,0:T(4,128)}, /*index=5*/f32[1,16]{1,0:T(1,128)}) custom-call(f32[1,16]{1,0:T(1,128)S(1)} %bitcast.73, f32[112,128]{1,0:T(8,128)S(1)} %get-tuple-element.60.keep, f32[112,128]{1,0:T(8,128)S(1)} %collective-permute-done.8.near, ...), custom_call_target="tpu_custom_call" | custom-call | tf_op jit(solution)/shard_map/finish/pallas_call | solution.py:866
  (26 shorter events, 0.2 us)
Async XLA Ops:
  1.5 6.6 %collective-permute-start = (bf16[1,11,16,128]{3,2,1,0:T(8,128)(2,1)S(1)}, bf16[1,11,16,128]{3,2,1,0:T(8,128)(2,1)S(1)}, u32[]{:S(2)}, u32[]{:S(2)}) collective-permute-start(bf16[1,11,16,128]{3,2,1,0:T(8,128)(2,1)S(1)} %pack.1), channel_id=1, source_target_pairs={{0,8},{1,9},{2,10},{3,11},{4,12},{5,13},{6,14},{7,15},{8,0},{9,1},... | collective-permute-start | bytes 135176 | tf_op jit(solution)/shard_map/ppermute | solution.py:729
  5.6 1.9 %collective-permute-start.1 = (bf16[27,8,16]{2,1,0:T(8,128)(2,1)}, bf16[27,8,16]{2,1,0:T(8,128)(2,1)S(1)}, u32[]{:S(2)}, u32[]{:S(2)}) collective-permute-start(bf16[27,8,16]{2,1,0:T(8,128)(2,1)} %bitcast.74), channel_id=1, source_target_pairs={{0,1},{1,0},{2,3},{3,2},{4,5},{5,4},{6,7},{7,6},{8,9},{9,8},{10,11... | collective-permute-start | bytes 20744 | tf_op jit(solution)/shard_map/ppermute | solution.py:729
  5.7 1.9 %collective-permute-start.2 = (bf16[27,2,8]{2,1,0:T(2,128)(2,1)}, bf16[27,2,8]{2,1,0:T(2,128)(2,1)S(1)}, u32[]{:S(2)}, u32[]{:S(2)}) collective-permute-start(bf16[27,2,8]{2,1,0:T(2,128)(2,1)} %bitcast.78), channel_id=1, source_target_pairs={{0,1},{1,0},{2,3},{3,2},{4,5},{5,4},{6,7},{7,6},{8,9},{9,8},{10,11... | collective-permute-start | bytes 2600 | tf_op jit(solution)/shard_map/ppermute | solution.py:729
  6.2 1.4 %collective-permute-start.3 = (bf16[3,3,3,8]{3,2,1,0:T(4,128)(2,1)}, bf16[3,3,3,8]{3,2,1,0:T(4,128)(2,1)S(1)}, u32[]{:S(2)}, u32[]{:S(2)}) collective-permute-start(bf16[3,3,3,8]{3,2,1,0:T(4,128)(2,1)} %bitcast.80), channel_id=1, source_target_pairs={{0,1},{1,0},{2,3},{3,2},{4,5},{5,4},{6,7},{7,6},{8,9},{9,8},{10,11... | collective-permute-start | bytes 1304 | tf_op jit(solution)/shard_map/ppermute | solution.py:729
  8.3 5.3 %collective-permute-start.4 = (bf16[16,16,128]{2,1,0:T(8,128)(2,1)S(1)}, bf16[16,16,128]{2,1,0:T(8,128)(2,1)S(1)}, u32[]{:S(2)}, u32[]{:S(2)}) collective-permute-start(bf16[16,16,128]{2,1,0:T(8,128)(2,1)S(1)} %get-tuple-element.85), channel_id=1, source_target_pairs={{0,2},{1,3},{2,0},{3,1},{4,6},{5,7},{6,4},{7,5},{8,10},{9,11},{10,... | collective-permute-start | bytes 196616 | tf_op jit(solution)/shard_map/ppermute | solution.py:729
  10.1 4.4 %collective-permute-start.5 = (bf16[16,16,128]{2,1,0:T(8,128)(2,1)S(1)}, bf16[16,16,128]{2,1,0:T(8,128)(2,1)S(1)}, u32[]{:S(2)}, u32[]{:S(2)}) collective-permute-start(bf16[16,16,128]{2,1,0:T(8,128)(2,1)S(1)} %get-tuple-element.83), channel_id=1, source_target_pairs={{0,4},{1,5},{2,6},{3,7},{4,0},{5,1},{6,2},{7,3},{8,12},{9,13},{10,... | collective-permute-start | bytes 196616 | tf_op jit(solution)/shard_map/ppermute | solution.py:729
  11.3 5.2 %collective-permute-start.6 = (bf16[16,16,128]{2,1,0:T(8,128)(2,1)S(1)}, bf16[16,16,128]{2,1,0:T(8,128)(2,1)S(1)}, u32[]{:S(2)}, u32[]{:S(2)}) collective-permute-start(bf16[16,16,128]{2,1,0:T(8,128)(2,1)S(1)} %get-tuple-element.84), channel_id=1, source_target_pairs={{0,6},{1,7},{2,4},{3,5},{4,2},{5,3},{6,0},{7,1},{8,14},{9,15},{10,... | collective-permute-start | bytes 196616 | tf_op jit(solution)/shard_map/ppermute | solution.py:729
  16.5 1.5 %collective-permute-start.7 = (bf16[8,6,16,128]{3,2,1,0:T(8,128)(2,1)S(1)}, bf16[8,6,16,128]{3,2,1,0:T(8,128)(2,1)S(1)}, u32[]{:S(2)}, u32[]{:S(2)}) collective-permute-start(bf16[8,6,16,128]{3,2,1,0:T(8,128)(2,1)S(1)} %bitcast.71), channel_id=1, source_target_pairs={{0,1},{1,0},{2,3},{3,2},{4,5},{5,4},{6,7},{7,6},{8,9},{9,8},{10,11... | collective-permute-start | bytes 589832 | tf_op jit(solution)/shard_map/ppermute | solution.py:729
  16.6 22.8 %copy-start = (f32[16]{0:T(128)S(1)}, f32[16]{0:T(128)}, u32[]{:S(2)}) copy-start(f32[16]{0:T(128)} %readout_from.1) | copy-start | bytes 196
  32.0 1.3 %collective-permute-start.8 = (f32[112,128]{1,0:T(8,128)S(1)}, f32[112,128]{1,0:T(8,128)S(1)}, u32[]{:S(2)}, u32[]{:S(2)}) collective-permute-start(f32[112,128]{1,0:T(8,128)S(1)} %get-tuple-element.61), channel_id=1, source_target_pairs={{0,1},{1,0},{2,3},{3,2},{4,5},{5,4},{6,7},{7,6},{8,9},{9,8},{10,11... | collective-permute-start | bytes 172040 | tf_op jit(solution)/shard_map/ppermute | solution.py:729
  33.3 5.1 %collective-permute-start.11 = (f32[80,128]{1,0:T(8,128)S(1)}, f32[80,128]{1,0:T(8,128)S(1)}, u32[]{:S(2)}, u32[]{:S(2)}) collective-permute-start(f32[80,128]{1,0:T(8,128)S(1)} %get-tuple-element.100), channel_id=1, source_target_pairs={{0,6},{1,7},{2,4},{3,5},{4,2},{5,3},{6,0},{7,1},{8,14},{9,15},{10,... | collective-permute-start | bytes 122888 | tf_op jit(solution)/shard_map/ppermute | solution.py:729
  34.1 4.4 %collective-permute-start.10 = (f32[80,128]{1,0:T(8,128)S(1)}, f32[80,128]{1,0:T(8,128)S(1)}, u32[]{:S(2)}, u32[]{:S(2)}) collective-permute-start(f32[80,128]{1,0:T(8,128)S(1)} %get-tuple-element.101), channel_id=1, source_target_pairs={{0,4},{1,5},{2,6},{3,7},{4,0},{5,1},{6,2},{7,3},{8,12},{9,13},{10,... | collective-permute-start | bytes 122888 | tf_op jit(solution)/shard_map/ppermute | solution.py:729
  35.4 4.0 %collective-permute-start.9 = (f32[80,128]{1,0:T(8,128)S(1)}, f32[80,128]{1,0:T(8,128)S(1)}, u32[]{:S(2)}, u32[]{:S(2)}) collective-permute-start(f32[80,128]{1,0:T(8,128)S(1)} %get-tuple-element.102), channel_id=1, source_target_pairs={{0,2},{1,3},{2,0},{3,1},{4,6},{5,7},{6,4},{7,5},{8,10},{9,11},{10,... | collective-permute-start | bytes 122888 | tf_op jit(solution)/shard_map/ppermute | solution.py:729

commit v4 on v3

--- a/solution.py
+++ b/solution.py
@@ -350,6 +350,67 @@
 
     repeat(rows_count, place)
 
+    window = width + 2 * REACH
+    tile_low = lax.div(low - REACH + TILE, TILE) - 1
+    aligned = width % TILE == 0
+    offset = TILE - REACH if aligned else low - REACH - tile_low * TILE
+    sides = 3 if aligned else 2
+
+    clipped = [jnp.clip(tile_low + side, 0, tiles - 1) for side in range(sides)]
+
+    def fill(pick, begin):
+        pieces = [None] * (lanes // TILE)
+        for y in range(rows_count):
+            moved = []
+            for side in range(sides):
+                if aligned:
+                    shift = (y * stride - offset) % TILE
+                else:
+                    shift = lax.rem(y * stride - offset + TILE * (count // TILE + 1), TILE)
+                moved.append(pltpu.roll(pick(y, side), shift, 1))
+            lane = iota(moved[0].shape, 1)
+            for t in range(y * stride // TILE, (y * stride + window - 1) // TILE + 1):
+                column = lane + (t * TILE - y * stride)
+                cell = column + (low - REACH)
+                inside = (column >= 0) & (column < window) & (cell >= 0) & (cell < cells)
+                for side in range(sides):
+                    least = t * TILE - y * stride + offset
+                    if aligned and (least + TILE <= side * TILE or least >= (side + 1) * TILE):
+                        continue
+                    taken = jnp.where(inside & ((column + offset) >> 7 == side), moved[side], 0.0)
+                    pieces[t] = taken if pieces[t] is None else pieces[t] + taken
+        height = next(piece.shape[0] for piece in pieces if piece is not None)
+        for t in range(lanes // TILE):
+            field[begin : begin + height, t * TILE : (t + 1) * TILE] = (
+                jnp.zeros((height, TILE), F32) if pieces[t] is None else pieces[t]
+            )
+
+    def shift_of(tap):
+        return stride * (tap // 3 - 1) + (tap % 3 - 1)
+
+    def rolled(value, amount):
+        amount = amount % lanes
+        return value if amount == 0 else pltpu.roll(value, amount, 1)
+
+    def spread(begin, target, target_begin, sign):
+        for tap in range(TAPS):
+            part = rolled(field[begin : begin + HID, :], sign * shift_of(tap))
+            at = target_begin + tap * HID
+            target[at : at + HID, :] = part[:, :count].astype(BF16)
+
+    def volume_and_cotangent(y, side):
+        return jnp.concatenate(
+            [
+                vol[y * tiles + clipped[side]].astype(F32),
+                cotangent_tile(y, side, clipped[side]),
+            ],
+            axis=0,
+        )
+
+    fill(volume_and_cotangent, 0)
+    spread(0, col_in, 0, -1)
+    spread(16, col_cot, 0, 1)
+
     for copy in copies:
         copy.wait()
     tile_of, block_of, project = projector(sizes, table, footprints)
@@ -381,12 +442,6 @@
             row * 2 + t, pl.ds(pl.multiple_of(chan * 8, 8), 8), :
         ]
 
-    window = width + 2 * REACH
-    tile_low = lax.div(low - REACH + TILE, TILE) - 1
-    aligned = width % TILE == 0
-    offset = TILE - REACH if aligned else low - REACH - tile_low * TILE
-    sides = 3 if aligned else 2
-
     def backproject(group):
         owners = [group * 8 + o for o in range(8)]
 
@@ -413,54 +468,8 @@
 
     repeat(rows_count // 8, backproject)
 
-    lane = iota((3 * 16, TILE), 1)
-    clipped = [jnp.clip(tile_low + side, 0, tiles - 1) for side in range(sides)]
-    pieces = [None] * (lanes // TILE)
-    for y in range(rows_count):
-        moved = []
-        for side in range(sides):
-            merged = jnp.concatenate(
-                [
-                    vol[y * tiles + clipped[side]].astype(F32),
-                    back[y, side].astype(BF16).astype(F32),
-                    cotangent_tile(y, side, clipped[side]),
-                ],
-                axis=0,
-            )
-            if aligned:
-                shift = (y * stride - offset) % TILE
-            else:
-                shift = lax.rem(y * stride - offset + TILE * (count // TILE + 1), TILE)
-            moved.append(pltpu.roll(merged, shift, 1))
-        for t in range(y * stride // TILE, (y * stride + window - 1) // TILE + 1):
-            column = lane + (t * TILE - y * stride)
-            cell = column + (low - REACH)
-            inside = (column >= 0) & (column < window) & (cell >= 0) & (cell < cells)
-            for side in range(sides):
-                least = t * TILE - y * stride + offset
-                if aligned and (least + TILE <= side * TILE or least >= (side + 1) * TILE):
-                    continue
-                taken = jnp.where(inside & ((column + offset) >> 7 == side), moved[side], 0.0)
-                pieces[t] = taken if pieces[t] is None else pieces[t] + taken
-    for t in range(lanes // TILE):
-        field[:, t * TILE : (t + 1) * TILE] = (
-            jnp.zeros((3 * 16, TILE), F32) if pieces[t] is None else pieces[t]
-        )
-
-    def shift_of(tap):
-        return stride * (tap // 3 - 1) + (tap % 3 - 1)
-
-    def rolled(value, amount):
-        amount = amount % lanes
-        return value if amount == 0 else pltpu.roll(value, amount, 1)
-
-    for tap in range(TAPS):
-        for channel in range(2):
-            begin = (channel * TAPS + tap) * HID
-            part = rolled(field[channel * 16 : (channel + 1) * 16, :], -shift_of(tap))
-            col_in[begin : begin + HID, :] = part[:, :count].astype(BF16)
-        part = rolled(field[32:48, :], shift_of(tap))
-        col_cot[tap * HID : (tap + 1) * HID, :] = part[:, :count].astype(BF16)
+    fill(lambda y, side: back[y, side].astype(BF16).astype(F32), 32)
+    spread(32, col_in, TAPS * HID, -1)
 
     wide = HID * HID
     place_x = iota((stride, wide), 0)
@@ -532,9 +541,9 @@
     middle_grad = masked(valid, dot(col_cot[...], last[...], TN) * slope_middle[...])
     grad_last = dot(col_cot[...], masked(own, middle_act).astype(BF16))
     widen(grad_wide, middle_grad, -1)
-    turned = jnp.transpose(masked(own, middle_grad)).astype(BF16)
+    turned = masked(own, middle_grad).astype(BF16)
     grads_middle = [
-        dot(turned, act_wide[stride * dy : stride * dy + count, :]) for dy in range(3)
+        dot(turned, act_wide[stride * dy : stride * dy + count, :], TN) for dy in range(3)
     ]
     first_sum = None
     for dy in range(3):
@@ -542,8 +551,7 @@
         first_sum = part if first_sum is None else first_sum + part
     first_grad = masked(valid, first_sum * slope_first[...])
     first_half = first_grad.astype(BF16)
-    turned = jnp.transpose(masked(own, first_grad)).astype(BF16)
-    grad_first = dot(turned, col_in[...], NT)
+    grad_first = dot(col_in[...], masked(own, first_grad).astype(BF16))
     back_grad = gather_taps(dot(first[TAPS * HID :, :], first_half, NT), 1)
 
     def put_grad(y, tile):
@@ -576,39 +584,29 @@
                 total = total + jnp.where(lane_group == other % 8, block, 0.0)
             put(depth * TAPS + tap, fold_groups(total))
 
-    lane_in = iota((HID, 2 * TAPS * HID), 1) & (HID - 1)
-    folds = []
-    for depth in range(3):
-        total = jnp.zeros((HID, 2 * TAPS * HID), F32)
-        for z in range(HID):
-            total = total + jnp.where(lane_in == z + depth - 1, grad_first[z * HID : (z + 1) * HID], 0.0)
-        folds.append(total)
-    source = iota((2 * TAPS * HID, TILE), 0) >> 4
-    channel = (source >= TAPS).astype(jnp.int32)
-    fold = ((source - TAPS * channel) * 2 + channel == iota((2 * TAPS * HID, TILE), 1)).astype(BF16)
-    folded = sum(dot(part, fold) for part in exact_parts(jnp.concatenate(folds, axis=0)))
-    for depth in range(3):
-        block = folded[depth * HID : (depth + 1) * HID]
-        out_tiles[3] = out_tiles[3] + pltpu.roll(block, 48 + depth * 2 * TAPS, 1)
-
     lane_z = iota((HID, wide), 1) >> 4
     row_z = iota((HID, wide), 0)
     lines = []
+
+    def add_line(product, begin, apart):
+        part = jnp.where(lane_z - row_z == apart, product[begin : begin + HID], 0.0)
+        lines.append(jnp.sum(part[:, :TILE] + part[:, TILE:], axis=0, keepdims=True))
+
     for depth in range(3):
-        keep_last = lane_z == row_z + depth - 1
         for tap in range(TAPS):
-            part = jnp.where(keep_last, grad_last[tap * HID : (tap + 1) * HID], 0.0)
-            lines.append(jnp.sum(part, axis=0, keepdims=True))
-    lines.append(jnp.zeros((32 - 27, wide), F32))
-    lines = jnp.concatenate(lines, axis=0)
-    lines = fold_groups(lines[:, :TILE] + lines[:, TILE:])
+            for channel in range(2):
+                add_line(grad_first, (channel * TAPS + tap) * HID, 1 - depth)
+    for depth in range(3):
+        for tap in range(TAPS):
+            add_line(grad_last, tap * HID, depth - 1)
+    lines.append(jnp.zeros((88 - len(lines), TILE), F32))
+    lines = fold_groups(jnp.concatenate(lines, axis=0))
     row_eight = iota((8, TILE), 0)
-    packed_last = jnp.zeros((8, TILE), F32)
-    for r in range(4):
+    row_packed = iota((HID, TILE), 0)
+    packed = jnp.zeros((HID, TILE), F32)
+    for r in range(11):
         picked = jnp.where(row_eight == iota((8, TILE), 1) >> 4, lines[r * 8 : (r + 1) * 8], 0.0)
-        packed_last = jnp.where(
-            row_eight == r, jnp.sum(picked, axis=0, keepdims=True), packed_last
-        )
+        packed = jnp.where(row_packed == r, jnp.sum(picked, axis=0, keepdims=True), packed)
 
     if whole:
         small = dual_gradients(
@@ -624,11 +622,11 @@
             pl.ds(pl.multiple_of((chans - 1 - chan) * 8, 8), 8), 0:TILE
         ]
     for target in (keep, send):
-        target[32:40, :] = packed_last
-        target[40:48, :] = small
+        target[32:48, :] = packed
+        target[48:56, :] = small
 
     def put_update(y):
-        begin = pl.multiple_of(48 + y * 16, 8)
+        begin = pl.multiple_of(56 + y * 16, 8)
         tile = row_tiles[update_row(y, row)]
         keep[pl.ds(begin, 16), :] = tile
         send[pl.ds(begin, 16), :] = tile
@@ -641,31 +639,31 @@
         block = grads[(k // 8) * 8 : (k // 8 + 1) * 8]
         block = block if k % 8 == 0 else pltpu.roll(block, TILE - 16 * (k % 8), 1)
         middle[k] = block[:, :HID]
-    filled = jnp.concatenate([grads[24:32], jnp.zeros((TILE - 8, TILE), F32)], axis=0)
-    turned = jnp.transpose(filled)
-    for k in range(27):
-        first[k] = turned[48 + 2 * k : 50 + 2 * k, :8]
-    block = pltpu.roll(grads[32:40], lax.rem(TILE - 8 * chan, TILE), 1)
+    block = pltpu.roll(grads[32:48], lax.rem(TILE - 8 * chan, TILE), 1)
     for group in range(8):
         moved = block if group == 0 else pltpu.roll(block, TILE - 16 * group, 1)
-        for r in range(4):
-            if r * 8 + group < 27:
-                last[r * 8 + group] = moved[r : r + 1, :8]
-    small = jnp.broadcast_to(jnp.sum(grads[40:48], axis=0, keepdims=True), (8, TILE))
+        for r in range(11):
+            line = r * 8 + group
+            if line < 54:
+                first[line // 2, line % 2 : line % 2 + 1, :] = moved[r : r + 1, :8]
+            elif line < 81:
+                last[line - 54] = moved[r : r + 1, :8]
+    small = jnp.broadcast_to(jnp.sum(grads[48:56], axis=0, keepdims=True), (8, TILE))
     readout[...] = small[0:1, :HID]
     for k in range(3):
         moved = pltpu.roll(small, TILE - HID * (k + 1), 1)
         mixing[k : k + 1, :] = moved[0:1, :HID] * scale[0:1, :HID]
 
 
-def finish_kernel(scale, keep, near, one, two, three, volume, *rest):
+def finish_kernel(scale, dual_in, keep, near, one, two, three, volume, dual, *rest):
     grads, slots = (rest[:-1], rest[-1])
+    dual[...] = dual_in[...]
     row = own_row()
     chan = lax.axis_index("chan")
-    total = keep[0:48, :] + near[0:48, :] + one[0:48, :] + two[0:48, :] + three[0:48, :]
+    total = keep[0:56, :] + near[0:56, :] + one[0:56, :] + two[0:56, :] + three[0:56, :]
     write_grads(chan, total, scale, *grads)
     for k, (source, begin) in enumerate(
-        ((keep, 48), (near, 48), (one, 48), (one, 64), (two, 48), (two, 64), (three, 48), (three, 64))
+        ((keep, 56), (near, 56), (one, 56), (one, 72), (two, 56), (two, 72), (three, 56), (three, 72))
     ):
         slots[k] = source[begin : begin + 16, :]
     for tile in range(8):
@@ -785,7 +783,7 @@
     updates = 4 if quick else rows_count
     count = rows_count * stride
     wide = HID * HID
-    moved = 48 + 16 * updates
+    moved = 56 + 16 * updates
     pad = -(-(stride + 1) // TILE) * TILE
     limit = (24 if quick else 56) * MIB
     sizes = (rows_count, chans, detectors, tiles, width, stride, cells,
@@ -854,24 +852,28 @@
     ]
     if quick:
 
-        sums = keep[:48] + near[:48]
+        sums = keep[:56] + near[:56]
 
         def piece(value, index):
-            return value[48 + 16 * index : 64 + 16 * index]
+            return value[56 + 16 * index : 72 + 16 * index]
 
         parts = [
             swap(jnp.concatenate([sums, piece(keep, k), piece(near, k)], axis=0), 2 * k)
             for k in (1, 2, 3)
         ]
-        new_volume, *grads = pl.pallas_call(
+        new_volume, new_dual, *grads = pl.pallas_call(
             finish_kernel,
-            out_shape=[jax.ShapeDtypeStruct((16, 8, TILE), F32)] + grad_shapes,
-            in_specs=[vmem] * 6,
-            out_specs=[vmem] * 6,
+            out_shape=[
+                jax.ShapeDtypeStruct((16, 8, TILE), F32),
+                jax.ShapeDtypeStruct((8, 2 * TILE), F32),
+            ]
+            + grad_shapes,
+            in_specs=[vmem] * 7,
+            out_specs=[vmem] * 7,
             scratch_shapes=[pltpu.VMEM((8, 16, TILE), F32)],
             compiler_params=pltpu.CompilerParams(vmem_limit_bytes=8 * MIB),
             name="finish",
-        )(scale, keep, near, *parts)
+        )(scale, new_dual, keep, near, *parts)
     else:
         mine = keep + near
         small = pl.pallas_call(
@@ -887,7 +889,7 @@
             name="dual_gradients",
         )(*table, footprints, *rest)
         total = jnp.concatenate(
-            [lax.psum(mine[:40], ROW_AXES), lax.psum(small, ALL_AXES)], axis=0
+            [lax.psum(mine[:48], ROW_AXES), lax.psum(small, ALL_AXES)], axis=0
         )
         grads = pl.pallas_call(
             finish_grads_kernel,
@@ -897,7 +899,7 @@
             name="finish_grads",
         )(scale, total)
         pieces = lax.all_to_all(
-            mine[48:].reshape(rows_count, 16, TILE), ROW_AXES, 0, 0, tiled=True
+            mine[56:].reshape(rows_count, 16, TILE), ROW_AXES, 0, 0, tiled=True
         )
         pieces = pieces.reshape(tiles, rows_count // tiles, 16, TILE).sum(axis=1)
         new_volume = jnp.swapaxes(pieces, 0, 1)

time: 40.4 us -> 39.7 us (0.983)
  Pallas kernels: 17.5 us -> 16.7 us
    pallas_call x1, Pallas kernels: 14 us -> 13.3 us  [body(): pl.pallas_call(functools.partial(main_kernel, sizes, quick), out_shape=[j...]
where the time goes in v4:
time: 39.7 us; the launch traced here: 39.5 us
  Pallas kernels  16.7 us (42%)
  starting transfers between devices  12 us (30%)
  waiting for transfers between devices  9.84 us (25%)
  between operations  0.77 us (2%)
    pallas_call x1, Pallas kernels, body(): pl.pallas_call(functools.partial(main_kernel, sizes, quick), out_shape=[j...  13.3 us
    ppermute x12, starting transfers between devices, swap(): return lax.ppermute(value, ALL_AXES, row_mask_pairs(devices, mask))  12 us
    ppermute x12, waiting for transfers between devices, swap(): return lax.ppermute(value, ALL_AXES, row_mask_pairs(devices, mask))  9.84 us
    pallas_call x1, Pallas kernels, build_weights(): pl.pallas_call(weights_kernel, out_shape=(jax.ShapeDtypeStruct((3, 3 * wi...  1.73 us
    pallas_call x1, Pallas kernels, body(): pl.pallas_call(functools.partial(pack_kernel, quick), out_shape=jax.Shape...  0.91 us
  transfers between devices with their start and end apart: 12, of which 8 were waited for; matrix products, arithmetic and copies ran while one was open for 0% of the time, Pallas kernels for 4%

profile of v4, /device:TPU:0, one launch (start us, length us, event | category | flops | bytes accessed | tf_op | source)
XLA Modules:
  0.0 39.5 jit_solution(13577151713553626631)
XLA Ops:
  0.6 0.9 %pack.1 = bf16[1,11,16,128]{3,2,1,0:T(8,128)(2,1)S(1)} custom-call(bf16[16,1024]{1,0:T(8,128)(2,1)} %bitcast.76, bf16[16,1024]{1,0:T(8,128)(2,1)} %bitcast.77, bf16[8,256]{1,0:T(8,128)(2,1)} %bitcast.84, bf16[8,256]{1,0:T(8,128)(2,1)} %bitcast.85), custom_call_target="tpu_custom_call" | custom-call | tf_op jit(solution)/shard_map/pack/pallas_call | solution.py:715
  1.5 4.1 %collective-permute-start = (bf16[1,11,16,128]{3,2,1,0:T(8,128)(2,1)S(1)}, bf16[1,11,16,128]{3,2,1,0:T(8,128)(2,1)S(1)}, u32[]{:S(2)}, u32[]{:S(2)}) collective-permute-start(bf16[1,11,16,128]{3,2,1,0:T(8,128)(2,1)S(1)} %pack.1), channel_id=1, source_target_pairs={{0,8},{1,9},{2,10},{3,11},{4,12},{5,13},{6,14},{7,15},{8,0},{9,1},... | collective-permute-start | bytes 135176 | tf_op jit(solution)/shard_map/ppermute | solution.py:727
  5.7 0.5 %collective-permute-start.2 = (bf16[27,2,8]{2,1,0:T(2,128)(2,1)}, bf16[27,2,8]{2,1,0:T(2,128)(2,1)S(1)}, u32[]{:S(2)}, u32[]{:S(2)}) collective-permute-start(bf16[27,2,8]{2,1,0:T(2,128)(2,1)} %bitcast.78), channel_id=1, source_target_pairs={{0,1},{1,0},{2,3},{3,2},{4,5},{5,4},{6,7},{7,6},{8,9},{9,8},{10,11... | collective-permute-start | bytes 2600 | tf_op jit(solution)/shard_map/ppermute | solution.py:727
  6.2 0.0 collective-permute-start.3
  6.2 1.4 %collective-permute-done.3.last_other = bf16[3,3,3,8]{3,2,1,0:T(4,128)(2,1)S(1)} collective-permute-done((bf16[3,3,3,8]{3,2,1,0:T(4,128)(2,1)}, bf16[3,3,3,8]{3,2,1,0:T(4,128)(2,1)S(1)}, u32[]{:S(2)}, u32[]{:S(2)}) %collective-permute-start.3) | collective-permute-done | bytes 464 | tf_op jit(solution)/shard_map/ppermute | solution.py:727
  7.6 0.6 %collective-permute-done = bf16[1,11,16,128]{3,2,1,0:T(8,128)(2,1)S(1)} collective-permute-done((bf16[1,11,16,128]{3,2,1,0:T(8,128)(2,1)S(1)}, bf16[1,11,16,128]{3,2,1,0:T(8,128)(2,1)S(1)}, u32[]{:S(2)}, u32[]{:S(2)}) %collective-permute-start) | collective-permute-done | bytes 45088 | tf_op jit(solution)/shard_map/ppermute | solution.py:727
  8.3 1.8 %collective-permute-start.4 = (bf16[16,16,128]{2,1,0:T(8,128)(2,1)S(1)}, bf16[16,16,128]{2,1,0:T(8,128)(2,1)S(1)}, u32[]{:S(2)}, u32[]{:S(2)}) collective-permute-start(bf16[16,16,128]{2,1,0:T(8,128)(2,1)S(1)} %get-tuple-element.87), channel_id=1, source_target_pairs={{0,2},{1,3},{2,0},{3,1},{4,6},{5,7},{6,4},{7,5},{8,10},{9,11},{10,... | collective-permute-start | bytes 196616 | tf_op jit(solution)/shard_map/ppermute | solution.py:727
  10.1 1.2 %collective-permute-start.5 = (bf16[16,16,128]{2,1,0:T(8,128)(2,1)S(1)}, bf16[16,16,128]{2,1,0:T(8,128)(2,1)S(1)}, u32[]{:S(2)}, u32[]{:S(2)}) collective-permute-start(bf16[16,16,128]{2,1,0:T(8,128)(2,1)S(1)} %get-tuple-element.85), channel_id=1, source_target_pairs={{0,4},{1,5},{2,6},{3,7},{4,0},{5,1},{6,2},{7,3},{8,12},{9,13},{10,... | collective-permute-start | bytes 196616 | tf_op jit(solution)/shard_map/ppermute | solution.py:727
  11.3 0.6 %collective-permute-start.6 = (bf16[16,16,128]{2,1,0:T(8,128)(2,1)S(1)}, bf16[16,16,128]{2,1,0:T(8,128)(2,1)S(1)}, u32[]{:S(2)}, u32[]{:S(2)}) collective-permute-start(bf16[16,16,128]{2,1,0:T(8,128)(2,1)S(1)} %get-tuple-element.86), channel_id=1, source_target_pairs={{0,6},{1,7},{2,4},{3,5},{4,2},{5,3},{6,0},{7,1},{8,14},{9,15},{10,... | collective-permute-start | bytes 196616 | tf_op jit(solution)/shard_map/ppermute | solution.py:727
  11.9 1.7 %band_weights.1 = (bf16[3,768,256]{2,1,0:T(8,128)(2,1)S(1)}, bf16[288,256]{1,0:T(8,128)(2,1)S(1)}, bf16[144,256]{1,0:T(8,128)(2,1)S(1)}, bf16[64,128,128]{2,1,0:...) custom-call(bf16[27,8,16]{2,1,0:T(8,128)(2,1)} %bitcast.75, ...), custom_call_target="tpu_custom_call" | custom-call | flops 100000000 | bytes 2000000 | tf_op jit(solution)/shard_map/band_weights/pallas_call | solution.py:151
  13.6 0.8 %collective-permute-done.5 = bf16[16,16,128]{2,1,0:T(8,128)(2,1)S(1)} collective-permute-done((bf16[16,16,128]{2,1,0:T(8,128)(2,1)S(1)}, bf16[16,16,128]{2,1,0:T(8,128)(2,1)S(1)}, u32[]{:S(2)}, u32[]{:S(2)}) %collective-permute-start.5) | collective-permute-done | bytes 65568 | tf_op jit(solution)/shard_map/ppermute | solution.py:727
  14.4 2.0 %collective-permute-done.6 = bf16[16,16,128]{2,1,0:T(8,128)(2,1)S(1)} collective-permute-done((bf16[16,16,128]{2,1,0:T(8,128)(2,1)S(1)}, bf16[16,16,128]{2,1,0:T(8,128)(2,1)S(1)}, u32[]{:S(2)}, u32[]{:S(2)}) %collective-permute-start.6) | collective-permute-done | bytes 65568 | tf_op jit(solution)/shard_map/ppermute | solution.py:727
  16.5 0.1 collective-permute-start.7
  16.6 0.0 copy-start
  16.6 1.4 %collective-permute-done.7.payload_other = bf16[8,6,16,128]{3,2,1,0:T(8,128)(2,1)S(1)} collective-permute-done((bf16[8,6,16,128]{3,2,1,0:T(8,128)(2,1)S(1)}, bf16[8,6,16,128]{3,2,1,0:T(8,128)(2,1)S(1)}, u32[]{:S(2)}, u32[]{:S(2)}) %collective-permute-start.7) | collective-permute-done | bytes 196640 | tf_op jit(solution)/shard_map/ppermute | solution.py:727
  18.0 13.3 %primal_dual.1 = (f32[120,128]{1,0:T(8,128)S(1)}, f32[120,128]{1,0:T(8,128)S(1)}, f32[8,256]{1,0:T(8,128)S(1)}) custom-call(s32[4,4,1,8]{3,2,1,0:T(1,128)S(1)} %get-tuple-element.52.rows_from, s32[4,4,1,8]{3,2,1,0:T(1,128)S(1)} %get-tuple-element.53.blocks_from, f32[3,16]{1,0:T(4,128)S(1)} %get-tuple-element.54.mixing_from, ...), custom_call_target="tpu_custom_call" | custom-call | flops 5000000000 | bytes 5000000 | tf_op jit(solution)/shard_map/primal_dual/pallas_call | solution.py:822
  31.3 0.2 collective-permute-start.8
  31.5 1.1 %collective-permute-done.8.near = f32[120,128]{1,0:T(8,128)S(1)} collective-permute-done((f32[120,128]{1,0:T(8,128)S(1)}, f32[120,128]{1,0:T(8,128)S(1)}, u32[]{:S(2)}, u32[]{:S(2)}) %collective-permute-start.8) | collective-permute-done | bytes 61472 | tf_op jit(solution)/shard_map/ppermute | solution.py:727
  32.6 0.8 %collective-permute-start.11 = (f32[88,128]{1,0:T(8,128)S(1)}, f32[88,128]{1,0:T(8,128)S(1)}, u32[]{:S(2)}, u32[]{:S(2)}) collective-permute-start(f32[88,128]{1,0:T(8,128)S(1)} %get-tuple-element.102), channel_id=1, source_target_pairs={{0,6},{1,7},{2,4},{3,5},{4,2},{5,3},{6,0},{7,1},{8,14},{9,15},{10,... | collective-permute-start | bytes 135176 | tf_op jit(solution)/shard_map/ppermute | solution.py:727
  33.4 1.3 %collective-permute-start.10 = (f32[88,128]{1,0:T(8,128)S(1)}, f32[88,128]{1,0:T(8,128)S(1)}, u32[]{:S(2)}, u32[]{:S(2)}) collective-permute-start(f32[88,128]{1,0:T(8,128)S(1)} %get-tuple-element.103), channel_id=1, source_target_pairs={{0,4},{1,5},{2,6},{3,7},{4,0},{5,1},{6,2},{7,3},{8,12},{9,13},{10,... | collective-permute-start | bytes 135176 | tf_op jit(solution)/shard_map/ppermute | solution.py:727
  34.7 1.5 %collective-permute-start.9 = (f32[88,128]{1,0:T(8,128)S(1)}, f32[88,128]{1,0:T(8,128)S(1)}, u32[]{:S(2)}, u32[]{:S(2)}) collective-permute-start(f32[88,128]{1,0:T(8,128)S(1)} %get-tuple-element.104), channel_id=1, source_target_pairs={{0,2},{1,3},{2,0},{3,1},{4,6},{5,7},{6,4},{7,5},{8,10},{9,11},{10,... | collective-permute-start | bytes 135176 | tf_op jit(solution)/shard_map/ppermute | solution.py:727
  36.2 1.7 %collective-permute-done.11.three = f32[88,128]{1,0:T(8,128)S(1)} collective-permute-done((f32[88,128]{1,0:T(8,128)S(1)}, f32[88,128]{1,0:T(8,128)S(1)}, u32[]{:S(2)}, u32[]{:S(2)}) %collective-permute-start.11) | collective-permute-done | bytes 45088 | tf_op jit(solution)/shard_map/ppermute | solution.py:727
  37.8 0.9 %collective-permute-done.9.one = f32[88,128]{1,0:T(8,128)S(1)} collective-permute-done((f32[88,128]{1,0:T(8,128)S(1)}, f32[88,128]{1,0:T(8,128)S(1)}, u32[]{:S(2)}, u32[]{:S(2)}) %collective-permute-start.9) | collective-permute-done | bytes 45088 | tf_op jit(solution)/shard_map/ppermute | solution.py:727
  38.7 0.8 %finish.1 = (f32[16,8,128]{2,1,0:T(8,128)}, f32[8,256]{1,0:T(8,128)}, f32[27,8,16]{2,1,0:T(8,128)}, f32[27,2,8]{2,1,0:T(2,128)}, f32[27,1,8]{2,1,0:T(1,128)}, /*index=5*/f32[3,16]{1,0:T(4,128)}, f32[1,16]{1,0:T(1,128)}) custom-call(f32[1,16]{1,0:T(1,128)S(1)} %bitcast.73, f32[8,256]{1,0:T(8,128)S(1)} %get-tuple-element.61.dual_in, ...), custom_call_target="tpu_custom_call" | custom-call | tf_op jit(solution)/shard_map/finish/pallas_call | solution.py:864
  (26 shorter events, 0.2 us)
Async XLA Ops:
  1.5 6.6 %collective-permute-start = (bf16[1,11,16,128]{3,2,1,0:T(8,128)(2,1)S(1)}, bf16[1,11,16,128]{3,2,1,0:T(8,128)(2,1)S(1)}, u32[]{:S(2)}, u32[]{:S(2)}) collective-permute-start(bf16[1,11,16,128]{3,2,1,0:T(8,128)(2,1)S(1)} %pack.1), channel_id=1, source_target_pairs={{0,8},{1,9},{2,10},{3,11},{4,12},{5,13},{6,14},{7,15},{8,0},{9,1},... | collective-permute-start | bytes 135176 | tf_op jit(solution)/shard_map/ppermute | solution.py:727
  5.6 1.9 %collective-permute-start.1 = (bf16[27,8,16]{2,1,0:T(8,128)(2,1)}, bf16[27,8,16]{2,1,0:T(8,128)(2,1)S(1)}, u32[]{:S(2)}, u32[]{:S(2)}) collective-permute-start(bf16[27,8,16]{2,1,0:T(8,128)(2,1)} %bitcast.74), channel_id=1, source_target_pairs={{0,1},{1,0},{2,3},{3,2},{4,5},{5,4},{6,7},{7,6},{8,9},{9,8},{10,11... | collective-permute-start | bytes 20744 | tf_op jit(solution)/shard_map/ppermute | solution.py:727
  5.7 1.9 %collective-permute-start.2 = (bf16[27,2,8]{2,1,0:T(2,128)(2,1)}, bf16[27,2,8]{2,1,0:T(2,128)(2,1)S(1)}, u32[]{:S(2)}, u32[]{:S(2)}) collective-permute-start(bf16[27,2,8]{2,1,0:T(2,128)(2,1)} %bitcast.78), channel_id=1, source_target_pairs={{0,1},{1,0},{2,3},{3,2},{4,5},{5,4},{6,7},{7,6},{8,9},{9,8},{10,11... | collective-permute-start | bytes 2600 | tf_op jit(solution)/shard_map/ppermute | solution.py:727
  6.2 1.4 %collective-permute-start.3 = (bf16[3,3,3,8]{3,2,1,0:T(4,128)(2,1)}, bf16[3,3,3,8]{3,2,1,0:T(4,128)(2,1)S(1)}, u32[]{:S(2)}, u32[]{:S(2)}) collective-permute-start(bf16[3,3,3,8]{3,2,1,0:T(4,128)(2,1)} %bitcast.80), channel_id=1, source_target_pairs={{0,1},{1,0},{2,3},{3,2},{4,5},{5,4},{6,7},{7,6},{8,9},{9,8},{10,11... | collective-permute-start | bytes 1304 | tf_op jit(solution)/shard_map/ppermute | solution.py:727
  8.3 5.3 %collective-permute-start.4 = (bf16[16,16,128]{2,1,0:T(8,128)(2,1)S(1)}, bf16[16,16,128]{2,1,0:T(8,128)(2,1)S(1)}, u32[]{:S(2)}, u32[]{:S(2)}) collective-permute-start(bf16[16,16,128]{2,1,0:T(8,128)(2,1)S(1)} %get-tuple-element.87), channel_id=1, source_target_pairs={{0,2},{1,3},{2,0},{3,1},{4,6},{5,7},{6,4},{7,5},{8,10},{9,11},{10,... | collective-permute-start | bytes 196616 | tf_op jit(solution)/shard_map/ppermute | solution.py:727
  10.1 4.4 %collective-permute-start.5 = (bf16[16,16,128]{2,1,0:T(8,128)(2,1)S(1)}, bf16[16,16,128]{2,1,0:T(8,128)(2,1)S(1)}, u32[]{:S(2)}, u32[]{:S(2)}) collective-permute-start(bf16[16,16,128]{2,1,0:T(8,128)(2,1)S(1)} %get-tuple-element.85), channel_id=1, source_target_pairs={{0,4},{1,5},{2,6},{3,7},{4,0},{5,1},{6,2},{7,3},{8,12},{9,13},{10,... | collective-permute-start | bytes 196616 | tf_op jit(solution)/shard_map/ppermute | solution.py:727
  11.3 5.2 %collective-permute-start.6 = (bf16[16,16,128]{2,1,0:T(8,128)(2,1)S(1)}, bf16[16,16,128]{2,1,0:T(8,128)(2,1)S(1)}, u32[]{:S(2)}, u32[]{:S(2)}) collective-permute-start(bf16[16,16,128]{2,1,0:T(8,128)(2,1)S(1)} %get-tuple-element.86), channel_id=1, source_target_pairs={{0,6},{1,7},{2,4},{3,5},{4,2},{5,3},{6,0},{7,1},{8,14},{9,15},{10,... | collective-permute-start | bytes 196616 | tf_op jit(solution)/shard_map/ppermute | solution.py:727
  16.5 1.5 %collective-permute-start.7 = (bf16[8,6,16,128]{3,2,1,0:T(8,128)(2,1)S(1)}, bf16[8,6,16,128]{3,2,1,0:T(8,128)(2,1)S(1)}, u32[]{:S(2)}, u32[]{:S(2)}) collective-permute-start(bf16[8,6,16,128]{3,2,1,0:T(8,128)(2,1)S(1)} %bitcast.71), channel_id=1, source_target_pairs={{0,1},{1,0},{2,3},{3,2},{4,5},{5,4},{6,7},{7,6},{8,9},{9,8},{10,11... | collective-permute-start | bytes 589832 | tf_op jit(solution)/shard_map/ppermute | solution.py:727
  16.6 22.2 %copy-start = (f32[16]{0:T(128)S(1)}, f32[16]{0:T(128)}, u32[]{:S(2)}) copy-start(f32[16]{0:T(128)} %readout_from.1) | copy-start | bytes 196
  31.3 1.3 %collective-permute-start.8 = (f32[120,128]{1,0:T(8,128)S(1)}, f32[120,128]{1,0:T(8,128)S(1)}, u32[]{:S(2)}, u32[]{:S(2)}) collective-permute-start(f32[120,128]{1,0:T(8,128)S(1)} %get-tuple-element.63), channel_id=1, source_target_pairs={{0,1},{1,0},{2,3},{3,2},{4,5},{5,4},{6,7},{7,6},{8,9},{9,8},{10,11... | collective-permute-start | bytes 184328 | tf_op jit(solution)/shard_map/ppermute | solution.py:727
  32.6 5.2 %collective-permute-start.11 = (f32[88,128]{1,0:T(8,128)S(1)}, f32[88,128]{1,0:T(8,128)S(1)}, u32[]{:S(2)}, u32[]{:S(2)}) collective-permute-start(f32[88,128]{1,0:T(8,128)S(1)} %get-tuple-element.102), channel_id=1, source_target_pairs={{0,6},{1,7},{2,4},{3,5},{4,2},{5,3},{6,0},{7,1},{8,14},{9,15},{10,... | collective-permute-start | bytes 135176 | tf_op jit(solution)/shard_map/ppermute | solution.py:727
  33.4 4.5 %collective-permute-start.10 = (f32[88,128]{1,0:T(8,128)S(1)}, f32[88,128]{1,0:T(8,128)S(1)}, u32[]{:S(2)}, u32[]{:S(2)}) collective-permute-start(f32[88,128]{1,0:T(8,128)S(1)} %get-tuple-element.103), channel_id=1, source_target_pairs={{0,4},{1,5},{2,6},{3,7},{4,0},{5,1},{6,2},{7,3},{8,12},{9,13},{10,... | collective-permute-start | bytes 135176 | tf_op jit(solution)/shard_map/ppermute | solution.py:727
  34.7 4.0 %collective-permute-start.9 = (f32[88,128]{1,0:T(8,128)S(1)}, f32[88,128]{1,0:T(8,128)S(1)}, u32[]{:S(2)}, u32[]{:S(2)}) collective-permute-start(f32[88,128]{1,0:T(8,128)S(1)} %get-tuple-element.104), channel_id=1, source_target_pairs={{0,2},{1,3},{2,0},{3,1},{4,6},{5,7},{6,4},{7,5},{8,10},{9,11},{10,... | collective-permute-start | bytes 135176 | tf_op jit(solution)/shard_map/ppermute | solution.py:727

commit v5 on v4

--- a/solution.py
+++ b/solution.py
@@ -302,7 +302,8 @@
 
 
 def main_kernel(sizes, whole, rows_from, blocks_from, mixing_from, readout_from,
-                payload, payload_other, routed, middle, first, last, footprints,
+                payload, payload_other, payload_late, routed,
+                middle, first, last, footprints,
                 keep, send, dual_out, proj, dual, meas, grad_tiles,
                 vol, dual_half, dual_new, back, field, col_in, col_cot,
                 act_wide, grad_wide, slope_first, slope_middle, row_tiles, sums,
@@ -327,14 +328,16 @@
 
     near = tiles // 2
 
-    def place(owner):
-        slot = piece_slot(owner, row)
-        for source, part in ((payload, flip), (payload_other, 1 - flip)):
+    def place(slot):
+        owner = row ^ ((slot >> 1) + ((slot & 1) << 2)) if whole else slot
+        late = whole and slot >= 2
+        received = payload_late if late else payload_other
+        for source, part, at in ((payload, flip, slot), (received, 1 - flip, slot - 2 * late)):
             for k in range(near):
-                vol[owner * tiles + part * near + k] = source[slot, k]
+                vol[owner * tiles + part * near + k] = source[at, k]
             span = pl.ds(pl.multiple_of(part * 8, 8), 8)
             for k, target in ((near, dual), (near + 1, meas)):
-                piece = source[slot, k].astype(F32)
+                piece = source[at, k].astype(F32)
                 for t in range(2):
                     target[owner * 2 + t, span, :] = piece[t * 8 : (t + 1) * 8]
 
@@ -749,17 +752,22 @@
 
         pieces = [swap(bound_for(k), 2 * k) for k in (1, 2, 3)]
         weights = build_weights(own, other, (footprints, *table))
-        pieces[0], weights = lax.optimization_barrier((pieces[0], weights))
-        pieces = [bound_for(0)] + pieces
+        mine = bound_for(0)
+        early = swap(mine[:12], 1)
+        pieces[0], weights, early = lax.optimization_barrier((pieces[0], weights, early))
+        late = swap(jnp.concatenate([piece[:12] for piece in pieces], axis=0), 1)
+        pieces = [mine] + pieces
         payload = jnp.concatenate([piece[:12] for piece in pieces], axis=0)
         payload = payload.reshape(rows_count, 6, 16, TILE)
         routed = jnp.concatenate([piece[12:] for piece in pieces], axis=0)
-        payload_other = swap(payload, 1)
+        payload_other = early.reshape(2, 6, 16, TILE)
+        payload_late = late.reshape(6, 6, 16, TILE)
     else:
         payload = lax.all_gather(payload, ALL_AXES, axis=0, tiled=True)
         payload = payload.reshape(rows_count, chans, *payload.shape[1:])
         payload, payload_other = (payload[:, 0], payload[:, 1])
         routed = payload[0, :1]
+        payload_late = routed
         weights = build_weights(
             own, tuple(swap(value, 1) for value in own), (footprints, *table)
         )
@@ -822,7 +830,7 @@
     keep, send, new_dual, *rest = pl.pallas_call(
         functools.partial(main_kernel, sizes, quick),
         out_shape=[jax.ShapeDtypeStruct(*spec) for spec in outs],
-        in_specs=[vmem] * 11,
+        in_specs=[vmem] * 12,
         out_specs=[vmem] * len(outs),
         scratch_shapes=[pltpu.VMEM(*spec) for spec in scratch]
         + [pltpu.SMEM(value.shape, value.dtype) for value in table]
@@ -837,6 +845,7 @@
         *table,
         payload,
         payload_other,
+        payload_late,
         routed,
         middle,
         first,

time: 39.7 us -> 40.3 us (1.015)
    ppermute x12 -> x13, waiting for transfers between devices: 9.84 us -> 10.2 us  [swap(): return lax.ppermute(value, ALL_AXES, row_mask_pairs(devices, mask))]
    ppermute x12 -> x13, starting transfers between devices: 12 us -> 12.1 us  [swap(): return lax.ppermute(value, ALL_AXES, row_mask_pairs(devices, mask))]
  transfers between devices with their start and end apart: 12 -> 13, of which waited for: 8 -> 9; matrix products, arithmetic and copies ran while one was open for 0% -> 0% of each run, Pallas kernels for 4% -> 4%
where the time goes in v5:
time: 40.3 us; the launch traced here: 40.1 us
  Pallas kernels  16.8 us (42%)
  starting transfers between devices  12.1 us (30%)
  waiting for transfers between devices  10.2 us (25%)
  between operations  0.79 us (2%)
    pallas_call x1, Pallas kernels, body(): pl.pallas_call(functools.partial(main_kernel, sizes, quick), out_shape=[j...  13.3 us
    ppermute x13, starting transfers between devices, swap(): return lax.ppermute(value, ALL_AXES, row_mask_pairs(devices, mask))  12.1 us
    ppermute x13, waiting for transfers between devices, swap(): return lax.ppermute(value, ALL_AXES, row_mask_pairs(devices, mask))  10.2 us
    pallas_call x1, Pallas kernels, build_weights(): pl.pallas_call(weights_kernel, out_shape=(jax.ShapeDtypeStruct((3, 3 * wi...  1.73 us
    pallas_call x1, Pallas kernels, body(): pl.pallas_call(functools.partial(pack_kernel, quick), out_shape=jax.Shape...  0.91 us
  transfers between devices with their start and end apart: 13, of which 9 were waited for; matrix products, arithmetic and copies ran while one was open for 0% of the time, Pallas kernels for 4%

profile of v5, /device:TPU:0, one launch (start us, length us, event | category | flops | bytes accessed | tf_op | source)
XLA Modules:
  0.0 40.1 jit_solution(4966964028036362287)
XLA Ops:
  0.6 0.9 %pack.1 = bf16[1,11,16,128]{3,2,1,0:T(8,128)(2,1)S(1)} custom-call(bf16[16,1024]{1,0:T(8,128)(2,1)} %bitcast.89, bf16[16,1024]{1,0:T(8,128)(2,1)} %bitcast.90, bf16[8,256]{1,0:T(8,128)(2,1)} %bitcast.97, bf16[8,256]{1,0:T(8,128)(2,1)} %bitcast.98), custom_call_target="tpu_custom_call" | custom-call | tf_op jit(solution)/shard_map/pack/pallas_call | solution.py:718
  1.5 4.1 %collective-permute-start = (bf16[1,11,16,128]{3,2,1,0:T(8,128)(2,1)S(1)}, bf16[1,11,16,128]{3,2,1,0:T(8,128)(2,1)S(1)}, u32[]{:S(2)}, u32[]{:S(2)}) collective-permute-start(bf16[1,11,16,128]{3,2,1,0:T(8,128)(2,1)S(1)} %pack.1), channel_id=1, source_target_pairs={{0,8},{1,9},{2,10},{3,11},{4,12},{5,13},{6,14},{7,15},{8,0},{9,1},... | collective-permute-start | bytes 135176 | tf_op jit(solution)/shard_map/ppermute | solution.py:730
  5.7 0.5 %collective-permute-start.2 = (bf16[27,2,8]{2,1,0:T(2,128)(2,1)}, bf16[27,2,8]{2,1,0:T(2,128)(2,1)S(1)}, u32[]{:S(2)}, u32[]{:S(2)}) collective-permute-start(bf16[27,2,8]{2,1,0:T(2,128)(2,1)} %bitcast.91), channel_id=1, source_target_pairs={{0,1},{1,0},{2,3},{3,2},{4,5},{5,4},{6,7},{7,6},{8,9},{9,8},{10,11... | collective-permute-start | bytes 2600 | tf_op jit(solution)/shard_map/ppermute | solution.py:730
  6.2 0.0 collective-permute-start.3
  6.2 1.4 %collective-permute-done.3.last_other = bf16[3,3,3,8]{3,2,1,0:T(4,128)(2,1)S(1)} collective-permute-done((bf16[3,3,3,8]{3,2,1,0:T(4,128)(2,1)}, bf16[3,3,3,8]{3,2,1,0:T(4,128)(2,1)S(1)}, u32[]{:S(2)}, u32[]{:S(2)}) %collective-permute-start.3) | collective-permute-done | bytes 464 | tf_op jit(solution)/shard_map/ppermute | solution.py:730
  7.6 0.6 %collective-permute-done = bf16[1,11,16,128]{3,2,1,0:T(8,128)(2,1)S(1)} collective-permute-done((bf16[1,11,16,128]{3,2,1,0:T(8,128)(2,1)S(1)}, bf16[1,11,16,128]{3,2,1,0:T(8,128)(2,1)S(1)}, u32[]{:S(2)}, u32[]{:S(2)}) %collective-permute-start) | collective-permute-done | bytes 45088 | tf_op jit(solution)/shard_map/ppermute | solution.py:730
  8.3 1.8 %collective-permute-start.4 = (bf16[16,16,128]{2,1,0:T(8,128)(2,1)S(1)}, bf16[16,16,128]{2,1,0:T(8,128)(2,1)S(1)}, u32[]{:S(2)}, u32[]{:S(2)}) collective-permute-start(bf16[16,16,128]{2,1,0:T(8,128)(2,1)S(1)} %get-tuple-element.95), channel_id=1, source_target_pairs={{0,2},{1,3},{2,0},{3,1},{4,6},{5,7},{6,4},{7,5},{8,10},{9,11},{10,... | collective-permute-start | bytes 196616 | tf_op jit(solution)/shard_map/ppermute | solution.py:730
  10.1 1.3 %collective-permute-start.7 = (bf16[16,16,128]{2,1,0:T(8,128)(2,1)S(1)}, bf16[16,16,128]{2,1,0:T(8,128)(2,1)S(1)}, u32[]{:S(2)}, u32[]{:S(2)}) collective-permute-start(bf16[16,16,128]{2,1,0:T(8,128)(2,1)S(1)} %get-tuple-element.93), channel_id=1, source_target_pairs={{0,6},{1,7},{2,4},{3,5},{4,2},{5,3},{6,0},{7,1},{8,14},{9,15},{10,... | collective-permute-start | bytes 196616 | tf_op jit(solution)/shard_map/ppermute | solution.py:730
  11.3 0.6 %collective-permute-start.6 = (bf16[16,16,128]{2,1,0:T(8,128)(2,1)S(1)}, bf16[16,16,128]{2,1,0:T(8,128)(2,1)S(1)}, u32[]{:S(2)}, u32[]{:S(2)}) collective-permute-start(bf16[16,16,128]{2,1,0:T(8,128)(2,1)S(1)} %get-tuple-element.94), channel_id=1, source_target_pairs={{0,4},{1,5},{2,6},{3,7},{4,0},{5,1},{6,2},{7,3},{8,12},{9,13},{10,... | collective-permute-start | bytes 196616 | tf_op jit(solution)/shard_map/ppermute | solution.py:730
  11.9 1.7 %band_weights.1 = (bf16[3,768,256]{2,1,0:T(8,128)(2,1)S(1)}, bf16[288,256]{1,0:T(8,128)(2,1)S(1)}, bf16[144,256]{1,0:T(8,128)(2,1)S(1)}, bf16[64,128,128]{2,1,0:...) custom-call(bf16[27,8,16]{2,1,0:T(8,128)(2,1)} %bitcast.88, ...), custom_call_target="tpu_custom_call" | custom-call | flops 100000000 | bytes 2000000 | tf_op jit(solution)/shard_map/band_weights/pallas_call | solution.py:151
  13.7 2.0 %collective-permute-done.6 = bf16[16,16,128]{2,1,0:T(8,128)(2,1)S(1)} collective-permute-done((bf16[16,16,128]{2,1,0:T(8,128)(2,1)S(1)}, bf16[16,16,128]{2,1,0:T(8,128)(2,1)S(1)}, u32[]{:S(2)}, u32[]{:S(2)}) %collective-permute-start.6) | collective-permute-done | bytes 65568 | tf_op jit(solution)/shard_map/ppermute | solution.py:730
  15.8 0.2 collective-permute-done.7
  16.0 0.1 collective-permute-start.8
  16.1 1.3 %collective-permute-done.8 = bf16[36,16,128]{2,1,0:T(8,128)(2,1)S(1)} collective-permute-done((bf16[36,16,128]{2,1,0:T(8,128)(2,1)S(1)}, bf16[36,16,128]{2,1,0:T(8,128)(2,1)S(1)}, u32[]{:S(2)}, u32[]{:S(2)}) %collective-permute-start.8) | collective-permute-done | bytes 147488 | tf_op jit(solution)/shard_map/ppermute | solution.py:730
  17.4 13.3 %primal_dual.1 = (f32[120,128]{1,0:T(8,128)S(1)}, f32[120,128]{1,0:T(8,128)S(1)}, f32[8,256]{1,0:T(8,128)S(1)}) custom-call(s32[4,4,1,8]{3,2,1,0:T(1,128)S(1)} %get-tuple-element.53.rows_from, s32[4,4,1,8]{3,2,1,0:T(1,128)S(1)} %get-tuple-element.54.blocks_from, f32[3,16]{1,0:T(4,128)S(1)} %get-tuple-element.55.mixing_from, ...), custom_call_target="tpu_custom_call" | custom-call | flops 5000000000 | bytes 5000000 | tf_op jit(solution)/shard_map/primal_dual/pallas_call | solution.py:830
  30.8 0.2 collective-permute-start.9
  31.0 1.1 %collective-permute-done.9.near = f32[120,128]{1,0:T(8,128)S(1)} collective-permute-done((f32[120,128]{1,0:T(8,128)S(1)}, f32[120,128]{1,0:T(8,128)S(1)}, u32[]{:S(2)}, u32[]{:S(2)}) %collective-permute-start.9) | collective-permute-done | bytes 61472 | tf_op jit(solution)/shard_map/ppermute | solution.py:730
  32.1 2.3 %collective-permute-start.12 = (f32[88,128]{1,0:T(8,128)S(1)}, f32[88,128]{1,0:T(8,128)S(1)}, u32[]{:S(2)}, u32[]{:S(2)}) collective-permute-start(f32[88,128]{1,0:T(8,128)S(1)} %get-tuple-element.110), channel_id=1, source_target_pairs={{0,6},{1,7},{2,4},{3,5},{4,2},{5,3},{6,0},{7,1},{8,14},{9,15},{10,... | collective-permute-start | bytes 135176 | tf_op jit(solution)/shard_map/ppermute | solution.py:730
  34.4 0.8 %collective-permute-start.11 = (f32[88,128]{1,0:T(8,128)S(1)}, f32[88,128]{1,0:T(8,128)S(1)}, u32[]{:S(2)}, u32[]{:S(2)}) collective-permute-start(f32[88,128]{1,0:T(8,128)S(1)} %get-tuple-element.111), channel_id=1, source_target_pairs={{0,4},{1,5},{2,6},{3,7},{4,0},{5,1},{6,2},{7,3},{8,12},{9,13},{10,... | collective-permute-start | bytes 135176 | tf_op jit(solution)/shard_map/ppermute | solution.py:730
  35.2 0.5 %collective-permute-start.10 = (f32[88,128]{1,0:T(8,128)S(1)}, f32[88,128]{1,0:T(8,128)S(1)}, u32[]{:S(2)}, u32[]{:S(2)}) collective-permute-start(f32[88,128]{1,0:T(8,128)S(1)} %get-tuple-element.112), channel_id=1, source_target_pairs={{0,2},{1,3},{2,0},{3,1},{4,6},{5,7},{6,4},{7,5},{8,10},{9,11},{10,... | collective-permute-start | bytes 135176 | tf_op jit(solution)/shard_map/ppermute | solution.py:730
  35.7 1.8 %collective-permute-done.12.three = f32[88,128]{1,0:T(8,128)S(1)} collective-permute-done((f32[88,128]{1,0:T(8,128)S(1)}, f32[88,128]{1,0:T(8,128)S(1)}, u32[]{:S(2)}, u32[]{:S(2)}) %collective-permute-start.12) | collective-permute-done | bytes 45088 | tf_op jit(solution)/shard_map/ppermute | solution.py:730
  37.5 1.0 %collective-permute-done.11.two = f32[88,128]{1,0:T(8,128)S(1)} collective-permute-done((f32[88,128]{1,0:T(8,128)S(1)}, f32[88,128]{1,0:T(8,128)S(1)}, u32[]{:S(2)}, u32[]{:S(2)}) %collective-permute-start.11) | collective-permute-done | bytes 45088 | tf_op jit(solution)/shard_map/ppermute | solution.py:730
  38.5 0.8 %collective-permute-done.10.one = f32[88,128]{1,0:T(8,128)S(1)} collective-permute-done((f32[88,128]{1,0:T(8,128)S(1)}, f32[88,128]{1,0:T(8,128)S(1)}, u32[]{:S(2)}, u32[]{:S(2)}) %collective-permute-start.10) | collective-permute-done | bytes 45088 | tf_op jit(solution)/shard_map/ppermute | solution.py:730
  39.3 0.8 %finish.1 = (f32[16,8,128]{2,1,0:T(8,128)}, f32[8,256]{1,0:T(8,128)}, f32[27,8,16]{2,1,0:T(8,128)}, f32[27,2,8]{2,1,0:T(2,128)}, f32[27,1,8]{2,1,0:T(1,128)}, /*index=5*/f32[3,16]{1,0:T(4,128)}, f32[1,16]{1,0:T(1,128)}) custom-call(f32[1,16]{1,0:T(1,128)S(1)} %bitcast.84, f32[8,256]{1,0:T(8,128)S(1)} %get-tuple-element.63.dual_in, ...), custom_call_target="tpu_custom_call" | custom-call | tf_op jit(solution)/shard_map/finish/pallas_call | solution.py:873
  (31 shorter events, 0.3 us)
Async XLA Ops:
  1.5 6.6 %collective-permute-start = (bf16[1,11,16,128]{3,2,1,0:T(8,128)(2,1)S(1)}, bf16[1,11,16,128]{3,2,1,0:T(8,128)(2,1)S(1)}, u32[]{:S(2)}, u32[]{:S(2)}) collective-permute-start(bf16[1,11,16,128]{3,2,1,0:T(8,128)(2,1)S(1)} %pack.1), channel_id=1, source_target_pairs={{0,8},{1,9},{2,10},{3,11},{4,12},{5,13},{6,14},{7,15},{8,0},{9,1},... | collective-permute-start | bytes 135176 | tf_op jit(solution)/shard_map/ppermute | solution.py:730
  5.6 1.9 %collective-permute-start.1 = (bf16[27,8,16]{2,1,0:T(8,128)(2,1)}, bf16[27,8,16]{2,1,0:T(8,128)(2,1)S(1)}, u32[]{:S(2)}, u32[]{:S(2)}) collective-permute-start(bf16[27,8,16]{2,1,0:T(8,128)(2,1)} %bitcast.87), channel_id=1, source_target_pairs={{0,1},{1,0},{2,3},{3,2},{4,5},{5,4},{6,7},{7,6},{8,9},{9,8},{10,11... | collective-permute-start | bytes 20744 | tf_op jit(solution)/shard_map/ppermute | solution.py:730
  5.7 1.9 %collective-permute-start.2 = (bf16[27,2,8]{2,1,0:T(2,128)(2,1)}, bf16[27,2,8]{2,1,0:T(2,128)(2,1)S(1)}, u32[]{:S(2)}, u32[]{:S(2)}) collective-permute-start(bf16[27,2,8]{2,1,0:T(2,128)(2,1)} %bitcast.91), channel_id=1, source_target_pairs={{0,1},{1,0},{2,3},{3,2},{4,5},{5,4},{6,7},{7,6},{8,9},{9,8},{10,11... | collective-permute-start | bytes 2600 | tf_op jit(solution)/shard_map/ppermute | solution.py:730
  6.2 1.4 %collective-permute-start.3 = (bf16[3,3,3,8]{3,2,1,0:T(4,128)(2,1)}, bf16[3,3,3,8]{3,2,1,0:T(4,128)(2,1)S(1)}, u32[]{:S(2)}, u32[]{:S(2)}) collective-permute-start(bf16[3,3,3,8]{3,2,1,0:T(4,128)(2,1)} %bitcast.93), channel_id=1, source_target_pairs={{0,1},{1,0},{2,3},{3,2},{4,5},{5,4},{6,7},{7,6},{8,9},{9,8},{10,11... | collective-permute-start | bytes 1304 | tf_op jit(solution)/shard_map/ppermute | solution.py:730
  8.3 5.4 %collective-permute-start.4 = (bf16[16,16,128]{2,1,0:T(8,128)(2,1)S(1)}, bf16[16,16,128]{2,1,0:T(8,128)(2,1)S(1)}, u32[]{:S(2)}, u32[]{:S(2)}) collective-permute-start(bf16[16,16,128]{2,1,0:T(8,128)(2,1)S(1)} %get-tuple-element.95), channel_id=1, source_target_pairs={{0,2},{1,3},{2,0},{3,1},{4,6},{5,7},{6,4},{7,5},{8,10},{9,11},{10,... | collective-permute-start | bytes 196616 | tf_op jit(solution)/shard_map/ppermute | solution.py:730
  10.1 3.6 %collective-permute-start.5 = (bf16[12,16,128]{2,1,0:T(8,128)(2,1)S(1)}, bf16[12,16,128]{2,1,0:T(8,128)(2,1)S(1)}, u32[]{:S(2)}, u32[]{:S(2)}) collective-permute-start(bf16[12,16,128]{2,1,0:T(8,128)(2,1)S(1)} %pad_maximum_fusion.4), channel_id=1, source_target_pairs={{0,1},{1,0},{2,3},{3,2},{4,5},{5,4},{6,7},{7,6},{8,9},{9,8},{10,11... | collective-permute-start | bytes 147464 | tf_op jit(solution)/shard_map/ppermute | solution.py:730
  10.1 5.9 %collective-permute-start.7 = (bf16[16,16,128]{2,1,0:T(8,128)(2,1)S(1)}, bf16[16,16,128]{2,1,0:T(8,128)(2,1)S(1)}, u32[]{:S(2)}, u32[]{:S(2)}) collective-permute-start(bf16[16,16,128]{2,1,0:T(8,128)(2,1)S(1)} %get-tuple-element.93), channel_id=1, source_target_pairs={{0,6},{1,7},{2,4},{3,5},{4,2},{5,3},{6,0},{7,1},{8,14},{9,15},{10,... | collective-permute-start | bytes 196616 | tf_op jit(solution)/shard_map/ppermute | solution.py:730
  11.3 4.4 %collective-permute-start.6 = (bf16[16,16,128]{2,1,0:T(8,128)(2,1)S(1)}, bf16[16,16,128]{2,1,0:T(8,128)(2,1)S(1)}, u32[]{:S(2)}, u32[]{:S(2)}) collective-permute-start(bf16[16,16,128]{2,1,0:T(8,128)(2,1)S(1)} %get-tuple-element.94), channel_id=1, source_target_pairs={{0,4},{1,5},{2,6},{3,7},{4,0},{5,1},{6,2},{7,3},{8,12},{9,13},{10,... | collective-permute-start | bytes 196616 | tf_op jit(solution)/shard_map/ppermute | solution.py:730
  16.0 1.4 %collective-permute-start.8 = (bf16[36,16,128]{2,1,0:T(8,128)(2,1)S(1)}, bf16[36,16,128]{2,1,0:T(8,128)(2,1)S(1)}, u32[]{:S(2)}, u32[]{:S(2)}) collective-permute-start(bf16[36,16,128]{2,1,0:T(8,128)(2,1)S(1)} %pad_maximum_fusion), channel_id=1, source_target_pairs={{0,1},{1,0},{2,3},{3,2},{4,5},{5,4},{6,7},{7,6},{8,9},{9,8},{10,11... | collective-permute-start | bytes 442376 | tf_op jit(solution)/shard_map/ppermute | solution.py:730
  17.4 21.8 %copy-start = (f32[16]{0:T(128)S(1)}, f32[16]{0:T(128)}, u32[]{:S(2)}) copy-start(f32[16]{0:T(128)} %readout_from.1) | copy-start | bytes 196
  30.8 1.3 %collective-permute-start.9 = (f32[120,128]{1,0:T(8,128)S(1)}, f32[120,128]{1,0:T(8,128)S(1)}, u32[]{:S(2)}, u32[]{:S(2)}) collective-permute-start(f32[120,128]{1,0:T(8,128)S(1)} %get-tuple-element.65), channel_id=1, source_target_pairs={{0,1},{1,0},{2,3},{3,2},{4,5},{5,4},{6,7},{7,6},{8,9},{9,8},{10,11... | collective-permute-start | bytes 184328 | tf_op jit(solution)/shard_map/ppermute | solution.py:730
  32.1 5.3 %collective-permute-start.12 = (f32[88,128]{1,0:T(8,128)S(1)}, f32[88,128]{1,0:T(8,128)S(1)}, u32[]{:S(2)}, u32[]{:S(2)}) collective-permute-start(f32[88,128]{1,0:T(8,128)S(1)} %get-tuple-element.110), channel_id=1, source_target_pairs={{0,6},{1,7},{2,4},{3,5},{4,2},{5,3},{6,0},{7,1},{8,14},{9,15},{10,... | collective-permute-start | bytes 135176 | tf_op jit(solution)/shard_map/ppermute | solution.py:730
  34.4 4.0 %collective-permute-start.11 = (f32[88,128]{1,0:T(8,128)S(1)}, f32[88,128]{1,0:T(8,128)S(1)}, u32[]{:S(2)}, u32[]{:S(2)}) collective-permute-start(f32[88,128]{1,0:T(8,128)S(1)} %get-tuple-element.111), channel_id=1, source_target_pairs={{0,4},{1,5},{2,6},{3,7},{4,0},{5,1},{6,2},{7,3},{8,12},{9,13},{10,... | collective-permute-start | bytes 135176 | tf_op jit(solution)/shard_map/ppermute | solution.py:730
  35.2 4.0 %collective-permute-start.10 = (f32[88,128]{1,0:T(8,128)S(1)}, f32[88,128]{1,0:T(8,128)S(1)}, u32[]{:S(2)}, u32[]{:S(2)}) collective-permute-start(f32[88,128]{1,0:T(8,128)S(1)} %get-tuple-element.112), channel_id=1, source_target_pairs={{0,2},{1,3},{2,0},{3,1},{4,6},{5,7},{6,4},{7,5},{8,10},{9,11},{10,... | collective-permute-start | bytes 135176 | tf_op jit(solution)/shard_map/ppermute | solution.py:730
